TPU v7x, 32 devices: a whole 2x2x4 slice. The times are simulated.
32 devices in a mesh: group: 2 (over x), head: 2 (over core), blk: 8 (over z, y).
Axes of the slice: x: 2, y: 2, z: 4, core: 2. Of those that a mesh axis runs over, the one named last changes fastest.
Arguments:
- patches: bfloat16 [4096, 1024], P(('group', 'head', 'blk')), parts along dimension 0, may hold values from -60 to 60
- ln_gain: float32 [1024], replicated, may hold values from 0.1 to 1.9
- w_qkv: bfloat16 [1024, 3072], replicated, may hold values from -0.21875 to 0.21875
- qk_gains: float32 [2, 1024], replicated, may hold values from 0.5 to 6
- w_out: bfloat16 [1024, 1024], replicated, may hold values from -0.1875 to 0.1875
Outputs:
- attn_out: bfloat16 [4096, 1024], P(('group', 'head', 'blk')), parts along dimension 0
There are 2 independent parts, one for each index of `group`. A program takes and returns all parts, laid end to end along the dimension named above; an argument that names none is the same for every part. Nothing has to cross between parts.
All inputs are finite; a program needn't handle non-finite values.
Results may differ from a plain program's by a relative error of at most 0.025.
Values may be sent and summed in bfloat16 or wider, within the bound.
No kernel may reach another device: no remote copies, remote signals or barrier semaphores. Data moves between devices by JAX's collectives and lax.ppermute only.
A program may use at most 128 MiB of HBM per device.

v0:
```python
import jax
import jax.numpy as jnp
from jax import lax
from jax.sharding import PartitionSpec as P

H = 16
HD = 64


def from_behind(array, axis, by):
    peers = lax.axis_size(axis)
    return lax.ppermute(array, axis, [(i, (i + by) % peers) for i in range(peers)])


def layer_norm(patches, ln_gain):
    values_f = patches.astype(jnp.float32)
    centre = values_f - jnp.mean(values_f, axis=-1, keepdims=True)
    variance = jnp.mean(centre * centre, axis=-1, keepdims=True)
    return (centre * lax.rsqrt(variance + 1e-05) * ln_gain).astype(jnp.bfloat16)


def head_norm(columns, gain_vector, head_count):
    row_count = columns.shape[0]
    shaped = columns.reshape(row_count, head_count, HD)
    square_mean = jnp.mean(shaped * shaped, axis=-1, keepdims=True)
    scaled = shaped * lax.rsqrt(square_mean + 1e-06) * gain_vector.reshape(head_count, HD)
    return scaled.astype(jnp.bfloat16).reshape(row_count, head_count * HD)


def project(normed, weight, gain_query, gain_key, head_count):
    projected = jnp.dot(normed, weight, preferred_element_type=jnp.float32)
    span = head_count * HD
    query = head_norm(projected[:, :span], gain_query, head_count)
    key_rows = head_norm(projected[:, span : 2 * span], gain_key, head_count)
    value_rows = projected[:, 2 * span :].astype(jnp.bfloat16)
    return (query, key_rows, value_rows)


def absorb(query, carried, key_rows, value_rows):
    row_count = key_rows.shape[0]
    head_count = query.shape[1]
    key_blocks = key_rows.reshape(row_count // row_count, row_count, head_count, HD)
    value_blocks = value_rows.reshape(row_count // row_count, row_count, head_count, HD)
    score_scale = HD ** (-0.5)

    def absorb_block(state_now, block_pair):
        running_max, running_sum, weighted = state_now
        key_block, value_block = block_pair
        scores = (
            jnp.einsum("qhd,khd->hqk", query, key_block, preferred_element_type=jnp.float32)
            * score_scale
        )
        new_max = jnp.maximum(running_max, jnp.max(scores, axis=-1))
        shrink = jnp.exp(running_max - new_max)
        exponent = jnp.exp(scores - new_max[:, :, None])
        running_sum = running_sum * shrink + jnp.sum(exponent, axis=-1)
        added = jnp.einsum(
            "hqk,khd->qhd",
            exponent.astype(jnp.bfloat16),
            value_block,
            preferred_element_type=jnp.float32,
        )
        weighted = weighted * shrink.T[:, :, None] + added
        return ((new_max, running_sum, weighted), None)

    return lax.scan(absorb_block, carried, (key_blocks, value_blocks))[0]


def per_device(patches, ln_gain, w_qkv, qk_gains, w_out):
    tok_rows = patches.shape[0]
    head_devices = lax.axis_size("head")
    local_heads = H // head_devices
    local_width = local_heads * HD
    normed = layer_norm(patches, ln_gain)
    query, key_rows, value_rows = project(normed, w_qkv, qk_gains[0], qk_gains[1], H)
    stacked = jnp.stack((query, key_rows, value_rows), axis=1).reshape(
        tok_rows, 3, head_devices, local_width
    )
    regrouped = lax.all_to_all(stacked, "head", split_axis=2, concat_axis=0, tiled=True)
    regrouped = regrouped.reshape(head_devices * tok_rows, 3, local_width)
    query = regrouped[:, 0]
    key_rows = regrouped[:, 1]
    value_rows = regrouped[:, 2]
    query_rows = query.shape[0]
    query = query.reshape(query_rows, local_heads, HD)
    initial = (
        jnp.full((local_heads, query_rows), -jnp.inf, jnp.float32),
        jnp.zeros((local_heads, query_rows), jnp.float32),
        jnp.zeros((query_rows, local_heads, HD), jnp.float32),
    )

    def visit(turn, state_now):
        visitor, running_max, running_sum, weighted = state_now
        running_max, running_sum, weighted = absorb(
            visitor, (running_max, running_sum, weighted), key_rows, value_rows
        )
        visitor = from_behind(visitor, "blk", 1)
        running_max, running_sum, weighted = (
            from_behind(running_max.astype(jnp.bfloat16), "blk", 1).astype(running_max.dtype),
            from_behind(running_sum.astype(jnp.bfloat16), "blk", 1).astype(running_sum.dtype),
            from_behind(weighted.astype(jnp.bfloat16), "blk", 1).astype(weighted.dtype),
        )
        return (visitor, running_max, running_sum, weighted)

    final_state = lax.fori_loop(
        0, lax.axis_size("blk"), visit, (query, initial[0], initial[1], initial[2])
    )
    running_max, running_sum, weighted = (final_state[1], final_state[2], final_state[3])
    attended = (
        (weighted / running_sum.T[:, :, None]).astype(jnp.bfloat16).reshape(query_rows, local_width)
    )
    attended = lax.all_to_all(attended, "head", split_axis=0, concat_axis=1, tiled=True)
    return jnp.dot(attended, w_out, preferred_element_type=jnp.float32).astype(jnp.bfloat16)


def solution(mesh):
    placed = (P(("group", "head", "blk"), None), P(), P(), P(), P())
    return jax.shard_map(
        per_device,
        mesh=mesh,
        in_specs=placed,
        out_specs=P(("group", "head", "blk"), None),
        check_vma=False,
    )
```

profile of v0, /device:TPU:0, one launch (start us, length us, event | category | flops | bytes accessed | tf_op | source)
XLA Modules:
  0.0 165.0 jit_solution(5658059260935367762)
XLA Ops:
  2.4 4.0 %fusion.16 = f32[128,3072]{1,0:T(8,128)S(1)} fusion(bf16[1024,3072]{1,0:T(8,128)(2,1)} %param.9, bf16[128,1024]{1,0:T(8,128)(2,1)} %param.7, f32[1024]{0:T(1024)} %param.8, f32[128]{0:T(128)S(1)} %add_rsqrt_fusion.2, f32[128]{0:T(128)S(1)} %broadcast_multiply_fusion), kind=kOutput, calls=%fused_computation.32 | convolution fusion | flops 805961728 | bytes 8131584 | tf_op jit(solution)/shard_map/dot_general | solution.py:31
  15.4 3.5 %all-to-all-start = ((bf16[128,3,2,512]{0,3,1,2:T(8,128)(2,1)}), bf16[128,3,2,512]{0,3,1,2:T(8,128)(2,1)S(1)}, u32[]{:S(2)}, u32[]{:S(2)}) async-start(bf16[128,3,2,512]{0,3,1,2:T(8,128)(2,1)} %copy.42), calls=%async_computation | async-start | bytes 1572864 | tf_op jit(solution)/shard_map/all_to_all | solution.py:79
  25.9 133.8 %while.16 = (s32[]{:T(128)}, bf16[256,8,64]{0,2,1:T(8,128)(2,1)S(1)}, f32[8,256]{1,0:T(8,128)S(1)}, f32[8,256]{1,0:T(8,128)S(1)}, f32[256,8,64]{0,2,1:T(8,128)S(...) while((s32[]{:T(128)}, ...), condition=%wide.region_7.8_spmd.clone, body=%wide.region_4.7_spmd.clone.sunk | while | flops 139087872 | bytes 19833124 | solution.py:105
  26.0 3.0 %collective-permute-start = (bf16[256,8,64]{0,2,1:T(8,128)(2,1)S(1)}, bf16[256,8,64]{0,2,1:T(8,128)(2,1)S(1)}, u32[]{:S(2)}, u32[]{:S(2)}) collective-permute-start(bf16[256,8,64]{0,2,1:T(8,128)(2,1)S(1)} %copy.58), channel_id=1, source_target_pairs={{0,1},{1,2},{2,3},{3,4},{4,5},{5,6},{6,7},{7,0},{8,9},{9,10},{10,1... | collective-permute-start | bytes 786440 | tf_op jit(solution)/shard_map/while/body/eval_jaxpr/ppermute | solution.py:12
  30.8 3.0 %fusion.43 = bf16[256,8,64]{0,2,1:T(8,128)(2,1)} fusion(bf16[256,8,64]{0,2,1:T(8,128)(2,1)} %bitcast.53, f32[8,256,256]{1,2,0:T(8,128)} %get-tuple-element.191, f32[8,256]{1,0:T(8,128)S(1)} %get-tuple-element.193, f32[256,8,64]{0,2,1:T(8,128)S(1)} %get-tuple-element.210, f32[256,8]{0,1:T(8,128)S(1)} %get-tuple-element.196, pred[]{:T(512)S(6)} %compare.3), kind=kOutput, calls=%fused_computation.6.clone.1 | convolution fusion | flops 69206016 | bytes 3162113 | tf_op jit(solution)/shard_map/while/body/eval_jaxpr/while/body/eval_jaxpr/hqk,khd->qhd/dot_general | solution.py:57
  38.9 6.2 %collective-permute-done.1 = bf16[8,256]{1,0:T(8,128)(2,1)S(1)} collective-permute-done((bf16[8,256]{1,0:T(8,128)(2,1)S(1)}, bf16[8,256]{1,0:T(8,128)(2,1)S(1)}, u32[]{:S(2)}, u32[]{:S(2)}) %collective-permute-start.1) | collective-permute-done | bytes 4128 | tf_op jit(solution)/shard_map/while/body/eval_jaxpr/ppermute | solution.py:12
  48.0 3.0 %fusion.43 = bf16[256,8,64]{0,2,1:T(8,128)(2,1)} fusion(bf16[256,8,64]{0,2,1:T(8,128)(2,1)} %bitcast.53, f32[8,256,256]{1,2,0:T(8,128)} %get-tuple-element.191, f32[8,256]{1,0:T(8,128)S(1)} %get-tuple-element.193, f32[256,8,64]{0,2,1:T(8,128)S(1)} %get-tuple-element.210, f32[256,8]{0,1:T(8,128)S(1)} %get-tuple-element.196, pred[]{:T(512)S(6)} %compare.3), kind=kOutput, calls=%fused_computation.6.clone.1 | convolution fusion | flops 69206016 | bytes 3162113 | tf_op jit(solution)/shard_map/while/body/eval_jaxpr/while/body/eval_jaxpr/hqk,khd->qhd/dot_general | solution.py:57
  55.8 6.2 %collective-permute-done.1 = bf16[8,256]{1,0:T(8,128)(2,1)S(1)} collective-permute-done((bf16[8,256]{1,0:T(8,128)(2,1)S(1)}, bf16[8,256]{1,0:T(8,128)(2,1)S(1)}, u32[]{:S(2)}, u32[]{:S(2)}) %collective-permute-start.1) | collective-permute-done | bytes 4128 | tf_op jit(solution)/shard_map/while/body/eval_jaxpr/ppermute | solution.py:12
  64.9 3.0 %fusion.43 = bf16[256,8,64]{0,2,1:T(8,128)(2,1)} fusion(bf16[256,8,64]{0,2,1:T(8,128)(2,1)} %bitcast.53, f32[8,256,256]{1,2,0:T(8,128)} %get-tuple-element.191, f32[8,256]{1,0:T(8,128)S(1)} %get-tuple-element.193, f32[256,8,64]{0,2,1:T(8,128)S(1)} %get-tuple-element.210, f32[256,8]{0,1:T(8,128)S(1)} %get-tuple-element.196, pred[]{:T(512)S(6)} %compare.3), kind=kOutput, calls=%fused_computation.6.clone.1 | convolution fusion | flops 69206016 | bytes 3162113 | tf_op jit(solution)/shard_map/while/body/eval_jaxpr/while/body/eval_jaxpr/hqk,khd->qhd/dot_general | solution.py:57
  70.9 7.6 %collective-permute-done.1 = bf16[8,256]{1,0:T(8,128)(2,1)S(1)} collective-permute-done((bf16[8,256]{1,0:T(8,128)(2,1)S(1)}, bf16[8,256]{1,0:T(8,128)(2,1)S(1)}, u32[]{:S(2)}, u32[]{:S(2)}) %collective-permute-start.1) | collective-permute-done | bytes 4128 | tf_op jit(solution)/shard_map/while/body/eval_jaxpr/ppermute | solution.py:12
  81.5 3.0 %fusion.43 = bf16[256,8,64]{0,2,1:T(8,128)(2,1)} fusion(bf16[256,8,64]{0,2,1:T(8,128)(2,1)} %bitcast.53, f32[8,256,256]{1,2,0:T(8,128)} %get-tuple-element.191, f32[8,256]{1,0:T(8,128)S(1)} %get-tuple-element.193, f32[256,8,64]{0,2,1:T(8,128)S(1)} %get-tuple-element.210, f32[256,8]{0,1:T(8,128)S(1)} %get-tuple-element.196, pred[]{:T(512)S(6)} %compare.3), kind=kOutput, calls=%fused_computation.6.clone.1 | convolution fusion | flops 69206016 | bytes 3162113 | tf_op jit(solution)/shard_map/while/body/eval_jaxpr/while/body/eval_jaxpr/hqk,khd->qhd/dot_general | solution.py:57
  86.9 7.8 %collective-permute-done.1 = bf16[8,256]{1,0:T(8,128)(2,1)S(1)} collective-permute-done((bf16[8,256]{1,0:T(8,128)(2,1)S(1)}, bf16[8,256]{1,0:T(8,128)(2,1)S(1)}, u32[]{:S(2)}, u32[]{:S(2)}) %collective-permute-start.1) | collective-permute-done | bytes 4128 | tf_op jit(solution)/shard_map/while/body/eval_jaxpr/ppermute | solution.py:12
  97.7 3.0 %fusion.43 = bf16[256,8,64]{0,2,1:T(8,128)(2,1)} fusion(bf16[256,8,64]{0,2,1:T(8,128)(2,1)} %bitcast.53, f32[8,256,256]{1,2,0:T(8,128)} %get-tuple-element.191, f32[8,256]{1,0:T(8,128)S(1)} %get-tuple-element.193, f32[256,8,64]{0,2,1:T(8,128)S(1)} %get-tuple-element.210, f32[256,8]{0,1:T(8,128)S(1)} %get-tuple-element.196, pred[]{:T(512)S(6)} %compare.3), kind=kOutput, calls=%fused_computation.6.clone.1 | convolution fusion | flops 69206016 | bytes 3162113 | tf_op jit(solution)/shard_map/while/body/eval_jaxpr/while/body/eval_jaxpr/hqk,khd->qhd/dot_general | solution.py:57
  103.5 7.2 %collective-permute-done.1 = bf16[8,256]{1,0:T(8,128)(2,1)S(1)} collective-permute-done((bf16[8,256]{1,0:T(8,128)(2,1)S(1)}, bf16[8,256]{1,0:T(8,128)(2,1)S(1)}, u32[]{:S(2)}, u32[]{:S(2)}) %collective-permute-start.1) | collective-permute-done | bytes 4128 | tf_op jit(solution)/shard_map/while/body/eval_jaxpr/ppermute | solution.py:12
  113.7 3.0 %fusion.43 = bf16[256,8,64]{0,2,1:T(8,128)(2,1)} fusion(bf16[256,8,64]{0,2,1:T(8,128)(2,1)} %bitcast.53, f32[8,256,256]{1,2,0:T(8,128)} %get-tuple-element.191, f32[8,256]{1,0:T(8,128)S(1)} %get-tuple-element.193, f32[256,8,64]{0,2,1:T(8,128)S(1)} %get-tuple-element.210, f32[256,8]{0,1:T(8,128)S(1)} %get-tuple-element.196, pred[]{:T(512)S(6)} %compare.3), kind=kOutput, calls=%fused_computation.6.clone.1 | convolution fusion | flops 69206016 | bytes 3162113 | tf_op jit(solution)/shard_map/while/body/eval_jaxpr/while/body/eval_jaxpr/hqk,khd->qhd/dot_general | solution.py:57
  117.2 2.5 %collective-permute-start.2 = (bf16[8,256]{1,0:T(8,128)(2,1)S(1)}, bf16[8,256]{1,0:T(8,128)(2,1)S(1)}, u32[]{:S(2)}, u32[]{:S(2)}) collective-permute-start(bf16[8,256]{1,0:T(8,128)(2,1)S(1)} %get-tuple-element.195), channel_id=1, source_target_pairs={{0,1},{1,2},{2,3},{3,4},{4,5},{5,6},{6,7},{7,0},{8,9},{9,10},{10,1... | collective-permute-start | bytes 12296 | tf_op jit(solution)/shard_map/while/body/eval_jaxpr/ppermute | solution.py:12
  119.7 7.0 %collective-permute-done.1 = bf16[8,256]{1,0:T(8,128)(2,1)S(1)} collective-permute-done((bf16[8,256]{1,0:T(8,128)(2,1)S(1)}, bf16[8,256]{1,0:T(8,128)(2,1)S(1)}, u32[]{:S(2)}, u32[]{:S(2)}) %collective-permute-start.1) | collective-permute-done | bytes 4128 | tf_op jit(solution)/shard_map/while/body/eval_jaxpr/ppermute | solution.py:12
  129.7 3.0 %fusion.43 = bf16[256,8,64]{0,2,1:T(8,128)(2,1)} fusion(bf16[256,8,64]{0,2,1:T(8,128)(2,1)} %bitcast.53, f32[8,256,256]{1,2,0:T(8,128)} %get-tuple-element.191, f32[8,256]{1,0:T(8,128)S(1)} %get-tuple-element.193, f32[256,8,64]{0,2,1:T(8,128)S(1)} %get-tuple-element.210, f32[256,8]{0,1:T(8,128)S(1)} %get-tuple-element.196, pred[]{:T(512)S(6)} %compare.3), kind=kOutput, calls=%fused_computation.6.clone.1 | convolution fusion | flops 69206016 | bytes 3162113 | tf_op jit(solution)/shard_map/while/body/eval_jaxpr/while/body/eval_jaxpr/hqk,khd->qhd/dot_general | solution.py:57
  133.2 2.5 %collective-permute-start.2 = (bf16[8,256]{1,0:T(8,128)(2,1)S(1)}, bf16[8,256]{1,0:T(8,128)(2,1)S(1)}, u32[]{:S(2)}, u32[]{:S(2)}) collective-permute-start(bf16[8,256]{1,0:T(8,128)(2,1)S(1)} %get-tuple-element.195), channel_id=1, source_target_pairs={{0,1},{1,2},{2,3},{3,4},{4,5},{5,6},{6,7},{7,0},{8,9},{9,10},{10,1... | collective-permute-start | bytes 12296 | tf_op jit(solution)/shard_map/while/body/eval_jaxpr/ppermute | solution.py:12
  135.7 7.0 %collective-permute-done.1 = bf16[8,256]{1,0:T(8,128)(2,1)S(1)} collective-permute-done((bf16[8,256]{1,0:T(8,128)(2,1)S(1)}, bf16[8,256]{1,0:T(8,128)(2,1)S(1)}, u32[]{:S(2)}, u32[]{:S(2)}) %collective-permute-start.1) | collective-permute-done | bytes 4128 | tf_op jit(solution)/shard_map/while/body/eval_jaxpr/ppermute | solution.py:12
  145.7 3.0 %fusion.43 = bf16[256,8,64]{0,2,1:T(8,128)(2,1)} fusion(bf16[256,8,64]{0,2,1:T(8,128)(2,1)} %bitcast.53, f32[8,256,256]{1,2,0:T(8,128)} %get-tuple-element.191, f32[8,256]{1,0:T(8,128)S(1)} %get-tuple-element.193, f32[256,8,64]{0,2,1:T(8,128)S(1)} %get-tuple-element.210, f32[256,8]{0,1:T(8,128)S(1)} %get-tuple-element.196, pred[]{:T(512)S(6)} %compare.3), kind=kOutput, calls=%fused_computation.6.clone.1 | convolution fusion | flops 69206016 | bytes 3162113 | tf_op jit(solution)/shard_map/while/body/eval_jaxpr/while/body/eval_jaxpr/hqk,khd->qhd/dot_general | solution.py:57
  149.2 2.5 %collective-permute-start.2 = (bf16[8,256]{1,0:T(8,128)(2,1)S(1)}, bf16[8,256]{1,0:T(8,128)(2,1)S(1)}, u32[]{:S(2)}, u32[]{:S(2)}) collective-permute-start(bf16[8,256]{1,0:T(8,128)(2,1)S(1)} %get-tuple-element.195), channel_id=1, source_target_pairs={{0,1},{1,2},{2,3},{3,4},{4,5},{5,6},{6,7},{7,0},{8,9},{9,10},{10,1... | collective-permute-start | bytes 12296 | tf_op jit(solution)/shard_map/while/body/eval_jaxpr/ppermute | solution.py:12
  151.7 7.0 %collective-permute-done.1 = bf16[8,256]{1,0:T(8,128)(2,1)S(1)} collective-permute-done((bf16[8,256]{1,0:T(8,128)(2,1)S(1)}, bf16[8,256]{1,0:T(8,128)(2,1)S(1)}, u32[]{:S(2)}, u32[]{:S(2)}) %collective-permute-start.1) | collective-permute-done | bytes 4128 | tf_op jit(solution)/shard_map/while/body/eval_jaxpr/ppermute | solution.py:12
  159.9 3.9 %all_to_all.34 = bf16[2,128,512]{1,2,0:T(8,128)(2,1)S(1)} all-to-all(bf16[2,128,512]{1,2,0:T(8,128)(2,1)S(1)} %copy.47), channel_id=1, replica_groups=mesh['group'=2,'head'=2,'blk'=8] {'head'}, dimensions={0} | all-to-all | bytes 524288 | tf_op jit(solution)/shard_map/all_to_all | solution.py:112
  (172 shorter events, 61.9 us)
Async XLA Ops:
  26.0 20.1 %collective-permute-start = (bf16[256,8,64]{0,2,1:T(8,128)(2,1)S(1)}, bf16[256,8,64]{0,2,1:T(8,128)(2,1)S(1)}, u32[]{:S(2)}, u32[]{:S(2)}) collective-permute-start(bf16[256,8,64]{0,2,1:T(8,128)(2,1)S(1)} %copy.58), channel_id=1, source_target_pairs={{0,1},{1,2},{2,3},{3,4},{4,5},{5,6},{6,7},{7,0},{8,9},{9,10},{10,1... | collective-permute-start | bytes 786440 | tf_op jit(solution)/shard_map/while/body/eval_jaxpr/ppermute | solution.py:12
  33.9 11.2 %collective-permute-start.3 = (bf16[256,8,64]{0,2,1:T(8,128)(2,1)}, bf16[256,8,64]{0,2,1:T(8,128)(2,1)}, u32[]{:S(2)}, u32[]{:S(2)}) collective-permute-start(bf16[256,8,64]{0,2,1:T(8,128)(2,1)} %fusion.43), channel_id=1, source_target_pairs={{0,1},{1,2},{2,3},{3,4},{4,5},{5,6},{6,7},{7,0},{8,9},{9,10},{10,1... | collective-permute-start | bytes 786440 | tf_op jit(solution)/shard_map/while/body/eval_jaxpr/ppermute | solution.py:12
  46.1 16.9 %collective-permute-start = (bf16[256,8,64]{0,2,1:T(8,128)(2,1)S(1)}, bf16[256,8,64]{0,2,1:T(8,128)(2,1)S(1)}, u32[]{:S(2)}, u32[]{:S(2)}) collective-permute-start(bf16[256,8,64]{0,2,1:T(8,128)(2,1)S(1)} %copy.58), channel_id=1, source_target_pairs={{0,1},{1,2},{2,3},{3,4},{4,5},{5,6},{6,7},{7,0},{8,9},{9,10},{10,1... | collective-permute-start | bytes 786440 | tf_op jit(solution)/shard_map/while/body/eval_jaxpr/ppermute | solution.py:12
  51.1 10.9 %collective-permute-start.3 = (bf16[256,8,64]{0,2,1:T(8,128)(2,1)}, bf16[256,8,64]{0,2,1:T(8,128)(2,1)}, u32[]{:S(2)}, u32[]{:S(2)}) collective-permute-start(bf16[256,8,64]{0,2,1:T(8,128)(2,1)} %fusion.43), channel_id=1, source_target_pairs={{0,1},{1,2},{2,3},{3,4},{4,5},{5,6},{6,7},{7,0},{8,9},{9,10},{10,1... | collective-permute-start | bytes 786440 | tf_op jit(solution)/shard_map/while/body/eval_jaxpr/ppermute | solution.py:12
  63.0 16.5 %collective-permute-start = (bf16[256,8,64]{0,2,1:T(8,128)(2,1)S(1)}, bf16[256,8,64]{0,2,1:T(8,128)(2,1)S(1)}, u32[]{:S(2)}, u32[]{:S(2)}) collective-permute-start(bf16[256,8,64]{0,2,1:T(8,128)(2,1)S(1)} %copy.58), channel_id=1, source_target_pairs={{0,1},{1,2},{2,3},{3,4},{4,5},{5,6},{6,7},{7,0},{8,9},{9,10},{10,1... | collective-permute-start | bytes 786440 | tf_op jit(solution)/shard_map/while/body/eval_jaxpr/ppermute | solution.py:12
  68.0 10.5 %collective-permute-start.3 = (bf16[256,8,64]{0,2,1:T(8,128)(2,1)}, bf16[256,8,64]{0,2,1:T(8,128)(2,1)}, u32[]{:S(2)}, u32[]{:S(2)}) collective-permute-start(bf16[256,8,64]{0,2,1:T(8,128)(2,1)} %fusion.43), channel_id=1, source_target_pairs={{0,1},{1,2},{2,3},{3,4},{4,5},{5,6},{6,7},{7,0},{8,9},{9,10},{10,1... | collective-permute-start | bytes 786440 | tf_op jit(solution)/shard_map/while/body/eval_jaxpr/ppermute | solution.py:12
  68.4 10.1 %collective-permute-start.1 = (bf16[8,256]{1,0:T(8,128)(2,1)S(1)}, bf16[8,256]{1,0:T(8,128)(2,1)S(1)}, u32[]{:S(2)}, u32[]{:S(2)}) collective-permute-start(bf16[8,256]{1,0:T(8,128)(2,1)S(1)} %get-tuple-element.194), channel_id=1, source_target_pairs={{0,1},{1,2},{2,3},{3,4},{4,5},{5,6},{6,7},{7,0},{8,9},{9,10},{10,1... | collective-permute-start | bytes 12296 | tf_op jit(solution)/shard_map/while/body/eval_jaxpr/ppermute | solution.py:12
  79.6 16.2 %collective-permute-start = (bf16[256,8,64]{0,2,1:T(8,128)(2,1)S(1)}, bf16[256,8,64]{0,2,1:T(8,128)(2,1)S(1)}, u32[]{:S(2)}, u32[]{:S(2)}) collective-permute-start(bf16[256,8,64]{0,2,1:T(8,128)(2,1)S(1)} %copy.58), channel_id=1, source_target_pairs={{0,1},{1,2},{2,3},{3,4},{4,5},{5,6},{6,7},{7,0},{8,9},{9,10},{10,1... | collective-permute-start | bytes 786440 | tf_op jit(solution)/shard_map/while/body/eval_jaxpr/ppermute | solution.py:12
  84.5 10.2 %collective-permute-start.3 = (bf16[256,8,64]{0,2,1:T(8,128)(2,1)}, bf16[256,8,64]{0,2,1:T(8,128)(2,1)}, u32[]{:S(2)}, u32[]{:S(2)}) collective-permute-start(bf16[256,8,64]{0,2,1:T(8,128)(2,1)} %fusion.43), channel_id=1, source_target_pairs={{0,1},{1,2},{2,3},{3,4},{4,5},{5,6},{6,7},{7,0},{8,9},{9,10},{10,1... | collective-permute-start | bytes 786440 | tf_op jit(solution)/shard_map/while/body/eval_jaxpr/ppermute | solution.py:12
  84.9 9.8 %collective-permute-start.1 = (bf16[8,256]{1,0:T(8,128)(2,1)S(1)}, bf16[8,256]{1,0:T(8,128)(2,1)S(1)}, u32[]{:S(2)}, u32[]{:S(2)}) collective-permute-start(bf16[8,256]{1,0:T(8,128)(2,1)S(1)} %get-tuple-element.194), channel_id=1, source_target_pairs={{0,1},{1,2},{2,3},{3,4},{4,5},{5,6},{6,7},{7,0},{8,9},{9,10},{10,1... | collective-permute-start | bytes 12296 | tf_op jit(solution)/shard_map/while/body/eval_jaxpr/ppermute | solution.py:12
  85.0 9.7 %collective-permute-start.2 = (bf16[8,256]{1,0:T(8,128)(2,1)S(1)}, bf16[8,256]{1,0:T(8,128)(2,1)S(1)}, u32[]{:S(2)}, u32[]{:S(2)}) collective-permute-start(bf16[8,256]{1,0:T(8,128)(2,1)S(1)} %get-tuple-element.195), channel_id=1, source_target_pairs={{0,1},{1,2},{2,3},{3,4},{4,5},{5,6},{6,7},{7,0},{8,9},{9,10},{10,1... | collective-permute-start | bytes 12296 | tf_op jit(solution)/shard_map/while/body/eval_jaxpr/ppermute | solution.py:12
  95.8 15.9 %collective-permute-start = (bf16[256,8,64]{0,2,1:T(8,128)(2,1)S(1)}, bf16[256,8,64]{0,2,1:T(8,128)(2,1)S(1)}, u32[]{:S(2)}, u32[]{:S(2)}) collective-permute-start(bf16[256,8,64]{0,2,1:T(8,128)(2,1)S(1)} %copy.58), channel_id=1, source_target_pairs={{0,1},{1,2},{2,3},{3,4},{4,5},{5,6},{6,7},{7,0},{8,9},{9,10},{10,1... | collective-permute-start | bytes 786440 | tf_op jit(solution)/shard_map/while/body/eval_jaxpr/ppermute | solution.py:12
  100.7 10.0 %collective-permute-start.3 = (bf16[256,8,64]{0,2,1:T(8,128)(2,1)}, bf16[256,8,64]{0,2,1:T(8,128)(2,1)}, u32[]{:S(2)}, u32[]{:S(2)}) collective-permute-start(bf16[256,8,64]{0,2,1:T(8,128)(2,1)} %fusion.43), channel_id=1, source_target_pairs={{0,1},{1,2},{2,3},{3,4},{4,5},{5,6},{6,7},{7,0},{8,9},{9,10},{10,1... | collective-permute-start | bytes 786440 | tf_op jit(solution)/shard_map/while/body/eval_jaxpr/ppermute | solution.py:12
  101.1 9.6 %collective-permute-start.1 = (bf16[8,256]{1,0:T(8,128)(2,1)S(1)}, bf16[8,256]{1,0:T(8,128)(2,1)S(1)}, u32[]{:S(2)}, u32[]{:S(2)}) collective-permute-start(bf16[8,256]{1,0:T(8,128)(2,1)S(1)} %get-tuple-element.194), channel_id=1, source_target_pairs={{0,1},{1,2},{2,3},{3,4},{4,5},{5,6},{6,7},{7,0},{8,9},{9,10},{10,1... | collective-permute-start | bytes 12296 | tf_op jit(solution)/shard_map/while/body/eval_jaxpr/ppermute | solution.py:12
  101.2 9.5 %collective-permute-start.2 = (bf16[8,256]{1,0:T(8,128)(2,1)S(1)}, bf16[8,256]{1,0:T(8,128)(2,1)S(1)}, u32[]{:S(2)}, u32[]{:S(2)}) collective-permute-start(bf16[8,256]{1,0:T(8,128)(2,1)S(1)} %get-tuple-element.195), channel_id=1, source_target_pairs={{0,1},{1,2},{2,3},{3,4},{4,5},{5,6},{6,7},{7,0},{8,9},{9,10},{10,1... | collective-permute-start | bytes 12296 | tf_op jit(solution)/shard_map/while/body/eval_jaxpr/ppermute | solution.py:12
  111.8 15.9 %collective-permute-start = (bf16[256,8,64]{0,2,1:T(8,128)(2,1)S(1)}, bf16[256,8,64]{0,2,1:T(8,128)(2,1)S(1)}, u32[]{:S(2)}, u32[]{:S(2)}) collective-permute-start(bf16[256,8,64]{0,2,1:T(8,128)(2,1)S(1)} %copy.58), channel_id=1, source_target_pairs={{0,1},{1,2},{2,3},{3,4},{4,5},{5,6},{6,7},{7,0},{8,9},{9,10},{10,1... | collective-permute-start | bytes 786440 | tf_op jit(solution)/shard_map/while/body/eval_jaxpr/ppermute | solution.py:12
  116.7 10.0 %collective-permute-start.3 = (bf16[256,8,64]{0,2,1:T(8,128)(2,1)}, bf16[256,8,64]{0,2,1:T(8,128)(2,1)}, u32[]{:S(2)}, u32[]{:S(2)}) collective-permute-start(bf16[256,8,64]{0,2,1:T(8,128)(2,1)} %fusion.43), channel_id=1, source_target_pairs={{0,1},{1,2},{2,3},{3,4},{4,5},{5,6},{6,7},{7,0},{8,9},{9,10},{10,1... | collective-permute-start | bytes 786440 | tf_op jit(solution)/shard_map/while/body/eval_jaxpr/ppermute | solution.py:12
  117.1 9.6 %collective-permute-start.1 = (bf16[8,256]{1,0:T(8,128)(2,1)S(1)}, bf16[8,256]{1,0:T(8,128)(2,1)S(1)}, u32[]{:S(2)}, u32[]{:S(2)}) collective-permute-start(bf16[8,256]{1,0:T(8,128)(2,1)S(1)} %get-tuple-element.194), channel_id=1, source_target_pairs={{0,1},{1,2},{2,3},{3,4},{4,5},{5,6},{6,7},{7,0},{8,9},{9,10},{10,1... | collective-permute-start | bytes 12296 | tf_op jit(solution)/shard_map/while/body/eval_jaxpr/ppermute | solution.py:12
  127.8 15.9 %collective-permute-start = (bf16[256,8,64]{0,2,1:T(8,128)(2,1)S(1)}, bf16[256,8,64]{0,2,1:T(8,128)(2,1)S(1)}, u32[]{:S(2)}, u32[]{:S(2)}) collective-permute-start(bf16[256,8,64]{0,2,1:T(8,128)(2,1)S(1)} %copy.58), channel_id=1, source_target_pairs={{0,1},{1,2},{2,3},{3,4},{4,5},{5,6},{6,7},{7,0},{8,9},{9,10},{10,1... | collective-permute-start | bytes 786440 | tf_op jit(solution)/shard_map/while/body/eval_jaxpr/ppermute | solution.py:12
  132.7 10.0 %collective-permute-start.3 = (bf16[256,8,64]{0,2,1:T(8,128)(2,1)}, bf16[256,8,64]{0,2,1:T(8,128)(2,1)}, u32[]{:S(2)}, u32[]{:S(2)}) collective-permute-start(bf16[256,8,64]{0,2,1:T(8,128)(2,1)} %fusion.43), channel_id=1, source_target_pairs={{0,1},{1,2},{2,3},{3,4},{4,5},{5,6},{6,7},{7,0},{8,9},{9,10},{10,1... | collective-permute-start | bytes 786440 | tf_op jit(solution)/shard_map/while/body/eval_jaxpr/ppermute | solution.py:12
  133.1 9.6 %collective-permute-start.1 = (bf16[8,256]{1,0:T(8,128)(2,1)S(1)}, bf16[8,256]{1,0:T(8,128)(2,1)S(1)}, u32[]{:S(2)}, u32[]{:S(2)}) collective-permute-start(bf16[8,256]{1,0:T(8,128)(2,1)S(1)} %get-tuple-element.194), channel_id=1, source_target_pairs={{0,1},{1,2},{2,3},{3,4},{4,5},{5,6},{6,7},{7,0},{8,9},{9,10},{10,1... | collective-permute-start | bytes 12296 | tf_op jit(solution)/shard_map/while/body/eval_jaxpr/ppermute | solution.py:12
  143.8 15.9 %collective-permute-start = (bf16[256,8,64]{0,2,1:T(8,128)(2,1)S(1)}, bf16[256,8,64]{0,2,1:T(8,128)(2,1)S(1)}, u32[]{:S(2)}, u32[]{:S(2)}) collective-permute-start(bf16[256,8,64]{0,2,1:T(8,128)(2,1)S(1)} %copy.58), channel_id=1, source_target_pairs={{0,1},{1,2},{2,3},{3,4},{4,5},{5,6},{6,7},{7,0},{8,9},{9,10},{10,1... | collective-permute-start | bytes 786440 | tf_op jit(solution)/shard_map/while/body/eval_jaxpr/ppermute | solution.py:12
  148.7 10.0 %collective-permute-start.3 = (bf16[256,8,64]{0,2,1:T(8,128)(2,1)}, bf16[256,8,64]{0,2,1:T(8,128)(2,1)}, u32[]{:S(2)}, u32[]{:S(2)}) collective-permute-start(bf16[256,8,64]{0,2,1:T(8,128)(2,1)} %fusion.43), channel_id=1, source_target_pairs={{0,1},{1,2},{2,3},{3,4},{4,5},{5,6},{6,7},{7,0},{8,9},{9,10},{10,1... | collective-permute-start | bytes 786440 | tf_op jit(solution)/shard_map/while/body/eval_jaxpr/ppermute | solution.py:12
  149.1 9.6 %collective-permute-start.1 = (bf16[8,256]{1,0:T(8,128)(2,1)S(1)}, bf16[8,256]{1,0:T(8,128)(2,1)S(1)}, u32[]{:S(2)}, u32[]{:S(2)}) collective-permute-start(bf16[8,256]{1,0:T(8,128)(2,1)S(1)} %get-tuple-element.194), channel_id=1, source_target_pairs={{0,1},{1,2},{2,3},{3,4},{4,5},{5,6},{6,7},{7,0},{8,9},{9,10},{10,1... | collective-permute-start | bytes 12296 | tf_op jit(solution)/shard_map/while/body/eval_jaxpr/ppermute | solution.py:12
  (19 other events, 271.0 us)
where the time goes:
time: 166 us; the launch traced here: 165 us
  waiting for transfers between devices  57.9 us (35%)
  matrix products  44.1 us (27%)
  starting transfers between devices  30.6 us (18%)
  other arithmetic  16.3 us (10%)
  local copies, waits for them, and re-layouts  11.3 us (7%)
  blocking collectives  3.94 us (2%)
    ppermute x32, waiting for transfers between devices, from_behind(): lax.ppermute(array, axis, [(i, (i + by) % peers) for i in range(peers)])  56 us
    ppermute x32, starting transfers between devices, from_behind(): lax.ppermute(array, axis, [(i, (i + by) % peers) for i in range(peers)])  27.1 us
    dot_general x8, matrix products, absorb_block(): jnp.einsum('hqk,khd->qhd', exponent.astype(jnp.bfloat16), value_block, pr...  24.3 us
    dot_general x8, matrix products, absorb_block(): jnp.einsum('qhd,khd->hqk', query, key_block, preferred_element_type=jnp.f...  14.7 us
    convert_element_type x8, other arithmetic, visit(): from_behind(weighted.astype(jnp.bfloat16), 'blk', 1).astype(weighted.dtype)  7.89 us
    dot_general x1, matrix products, project(): projected = jnp.dot(normed, weight, preferred_element_type=jnp.float32)  3.97 us
    all_to_all x1, blocking collectives, per_device(): lax.all_to_all(attended, 'head', split_axis=0, concat_axis=1, tiled=True)  3.94 us
    all_to_all x1, starting transfers between devices, per_device(): lax.all_to_all(stacked, 'head', split_axis=2, concat_axis=0, tiled=True)  3.53 us
  transfers between devices with their start and end apart: 33, of which 9 were waited for; matrix products, arithmetic and copies ran while one was open for 30% of the time, Pallas kernels for 0%

commit v1 on v0

v1 whole, which is shorter than its diff:
```python
import functools

import jax
import jax.numpy as jnp
from jax import lax
from jax.experimental import pallas as pl
from jax.experimental.pallas import tpu as pltpu
from jax.sharding import PartitionSpec as P

H = 16
HD = 64
PAIR = 2 * HD
F32 = jnp.float32
BF16 = jnp.bfloat16
LOW = -1e30
VMEM = pl.BlockSpec(memory_space=pltpu.VMEM)


def ring_order(mesh):
    axis = mesh.axis_names.index("blk")
    along = mesh.devices
    for other in reversed(range(along.ndim)):
        if other != axis:
            along = along.take(0, axis=other)
    count = along.shape[0]
    coords = [getattr(device, "coords", None) for device in along]
    if any(c is None for c in coords):
        return list(range(count))
    place = {tuple(c): i for i, c in enumerate(coords)}
    varying = [a for a in range(3) if len({c[a] for c in place}) > 1]
    if len(place) != count or len(varying) != 2:
        return list(range(count))
    short, long = sorted(varying, key=lambda a: len({c[a] for c in place}))
    columns = sorted({c[short] for c in place})
    if len(columns) != 2:
        return list(range(count))
    up = sorted((c for c in place if c[short] == columns[0]), key=lambda c: c[long])
    down = sorted((c for c in place if c[short] == columns[1]), key=lambda c: -c[long])
    return [place[c] for c in up + down]


def normalise(x_ref, gain_ref):
    values = x_ref[...].astype(F32)
    centre = values - jnp.mean(values, axis=-1, keepdims=True)
    variance = jnp.mean(centre * centre, axis=-1, keepdims=True)
    return (centre * lax.rsqrt(variance + 1e-05) * gain_ref[...]).astype(BF16)


def head_scale(columns):
    squares = columns * columns
    high = squares.astype(BF16)
    low = (squares - high.astype(F32)).astype(BF16)
    width = 256
    row = lax.broadcasted_iota(jnp.int32, (width, width), 0) // HD
    column = lax.broadcasted_iota(jnp.int32, (width, width), 1) // HD
    same_head = jnp.where(row == column, 1.0, 0.0).astype(BF16)
    sums = [
        jnp.dot(part[:, at : at + width], same_head, preferred_element_type=F32)
        for at in range(0, columns.shape[1], width)
        for part in (high, low)
    ]
    total = jnp.concatenate([a + b for a, b in zip(sums[0::2], sums[1::2])], axis=1)
    return lax.rsqrt(total * (1.0 / HD) + 1e-06)


def query_kernel(own_ref, sibling_ref, gain_ref, wq_ref, gq_ref, out_ref):
    rows = own_ref.shape[0]
    for i, x_ref in enumerate((own_ref, sibling_ref)):
        projected = jnp.dot(normalise(x_ref, gain_ref), wq_ref[...], preferred_element_type=F32)
        query = (projected * head_scale(projected) * gq_ref[...]).astype(BF16).astype(F32)
        out_ref[:, i * rows : (i + 1) * rows] = (query * (HD**-0.5)).T.astype(BF16)


def absorb(first, last, x_ref, gain_ref, wkv_ref, gk_ref, q_ref, *refs):
    if first:
        outs = refs
    else:
        (max_ref, sum_ref, acc_ref), outs = refs[:3], refs[3:]
    width = H * HD
    projected = jnp.dot(normalise(x_ref, gain_ref), wkv_ref[...], preferred_element_type=F32)
    keys = projected[:, :width]
    keys = (keys * head_scale(keys) * gk_ref[...]).astype(BF16)
    values = projected[:, width:].T.astype(BF16)
    queries = q_ref.shape[1]
    zeros = jnp.zeros((HD, queries), BF16)
    for h in range(H):
        at = h * HD
        pair = (h // 2) * PAIR
        query = q_ref[at : at + HD, :]
        query = jnp.concatenate([query, zeros] if h % 2 == 0 else [zeros, query], axis=0)
        scores = jnp.dot(keys[:, pair : pair + PAIR], query, preferred_element_type=F32)
        new_max = jnp.max(scores, axis=0, keepdims=True)
        if not first:
            old_max = max_ref[h : h + 1, :]
            new_max = jnp.maximum(new_max, old_max)
        exponent = jnp.exp(scores - new_max)
        total = jnp.sum(exponent, axis=0, keepdims=True)
        added = jnp.dot(values[at : at + HD, :], exponent.astype(BF16), preferred_element_type=F32)
        if not first:
            shrink = jnp.exp(old_max - new_max)
            total = total + sum_ref[h : h + 1, :] * shrink
            added = added + acc_ref[at : at + HD, :] * shrink
        if last:
            keep_ref, send_ref = outs
            half = queries // 2
            for ref, part in ((keep_ref, slice(0, half)), (send_ref, slice(half, queries))):
                ref[at : at + HD, :] = added[:, part]
                ref[width + h : width + h + 1, :] = new_max[:, part]
                ref[width + H + h : width + H + h + 1, :] = total[:, part]
        else:
            new_max_ref, new_sum_ref, new_acc_ref = outs
            new_max_ref[h : h + 1, :] = new_max
            new_sum_ref[h : h + 1, :] = total
            new_acc_ref[at : at + HD, :] = added


def finish_kernel(kept_ref, came_ref, w_ref, out_ref):
    width = H * HD
    heads = []
    for h in range(H):
        at = slice(h * HD, (h + 1) * HD)
        m, s = slice(width + h, width + h + 1), slice(width + H + h, width + H + h + 1)
        top = jnp.maximum(kept_ref[m, :], came_ref[m, :])
        mine, theirs = jnp.exp(kept_ref[m, :] - top), jnp.exp(came_ref[m, :] - top)
        total = kept_ref[s, :] * mine + came_ref[s, :] * theirs
        summed = kept_ref[at, :] * mine + came_ref[at, :] * theirs
        heads.append((summed / total).astype(BF16))
    attended = jnp.concatenate(heads, axis=0)
    out_ref[...] = lax.dot_general(
        attended, w_ref[...], (((0,), (0,)), ((), ())), preferred_element_type=F32
    ).astype(BF16)


def call(body, outs, operands, flops, exps):
    moved = sum(a.size * a.dtype.itemsize for a in (*operands, *outs))
    return pl.pallas_call(
        body,
        out_shape=outs if len(outs) > 1 else outs[0],
        in_specs=[VMEM] * len(operands),
        out_specs=[VMEM] * len(outs) if len(outs) > 1 else VMEM,
        compiler_params=pltpu.CompilerParams(vmem_limit_bytes=24 * 1024 * 1024),
        cost_estimate=pl.CostEstimate(flops=flops, bytes_accessed=moved, transcendentals=exps),
    )(*operands)


def per_device(order, patches, ln_gain, w_qkv, qk_gains, w_out):
    rows, width = patches.shape
    count = lax.axis_size("blk")
    place = {index: i for i, index in enumerate(order)}

    def ahead(index, head):
        return order[(place[index] + (1 if head == 0 else -1)) % count]

    straight = [(h * count + b, h * count + ahead(b, h)) for h in range(2) for b in range(count)]
    cross = [((1 - h) * count + b, h * count + ahead(b, h)) for h in range(2) for b in range(count)]
    axes = ("head", "blk")

    gain = ln_gain.reshape(1, width)
    w_query, w_kv = w_qkv[:, :width], w_qkv[:, width:]
    gain_query, gain_key = qk_gains[0:1], qk_gains[1:2]
    sibling = lax.ppermute(patches, "head", [(0, 1), (1, 0)])
    one = lax.ppermute(patches, axes, straight)
    two = lax.ppermute(patches, axes, cross)
    query = call(
        query_kernel,
        [jax.ShapeDtypeStruct((width, 2 * rows), BF16)],
        (patches, sibling, gain, w_query, gain_query),
        2 * 2 * rows * width * width,
        0,
    )
    state_shapes = [
        jax.ShapeDtypeStruct((H, 2 * rows), F32),
        jax.ShapeDtypeStruct((H, 2 * rows), F32),
        jax.ShapeDtypeStruct((width, 2 * rows), F32),
    ]
    last_shapes = [jax.ShapeDtypeStruct((width + 2 * H, rows), F32)] * 2
    flops = 2 * rows * width * 2 * width + 2 * 2 * rows * 2 * rows * width
    exps = H * rows * 2 * rows

    def take(block, state, last=False):
        return call(
            functools.partial(absorb, not state, last),
            last_shapes if last else state_shapes,
            (block, gain, w_kv, gain_key, query, *state),
            flops,
            exps,
        )

    state = take(patches, ())
    for turn in range(1, count // 2 + 1):
        here = one
        if turn < count // 2:
            one = lax.ppermute(one, axes, straight)
            state = take(here, state)
            here = two
            if turn < count // 2 - 1:
                two = lax.ppermute(two, axes, straight)
            state = take(here, state)
        else:
            kept, sent = take(here, state, last=True)
    came = lax.ppermute(sent, "head", [(0, 1), (1, 0)])
    return call(
        finish_kernel,
        [jax.ShapeDtypeStruct((rows, width), BF16)],
        (kept, came, w_out),
        2 * rows * width * width,
        0,
    )


def solution(mesh):
    placed = (P(("group", "head", "blk"), None), P(), P(), P(), P())
    return jax.shard_map(
        functools.partial(per_device, ring_order(mesh)),
        mesh=mesh,
        in_specs=placed,
        out_specs=P(("group", "head", "blk"), None),
        check_vma=False,
    )
```

time: 166 us -> 68.1 us (0.41)
  waiting for transfers between devices: 57.9 us -> 11 us
  matrix products: 44.1 us -> 0 us
  Pallas kernels: 0 us -> 39.3 us
  starting transfers between devices: 30.6 us -> 12.3 us
  other arithmetic: 16.3 us -> 0 us
  local copies, waits for them, and re-layouts: 11.3 us -> 5.1 us
  blocking collectives: 3.94 us -> 0 us
    ppermute x32 -> x9, waiting for transfers between devices: 56 us -> 11 us  [the longest x1 5.33 us: per_device(): one = lax.ppermute(patches, axes, straight)]
    dot_general x18 -> x0, matrix products: 44.1 us -> none  [the longest x8 24.3 us: absorb_block(): jnp.einsum('hqk,khd->qhd', exponent.astype(jnp.bfloat16), value_block, pr...]
    pallas_call x0 -> x10, Pallas kernels: none -> 39.3 us  [call(): pl.pallas_call(body, out_shape=outs if len(outs) > 1 else outs[0], in_spe...]
    ppermute x32 -> x9, starting transfers between devices: 27.1 us -> 12.3 us  [the longest x3 5.36 us: per_device(): one = lax.ppermute(one, axes, straight)]
    convert_element_type x34 -> x0, other arithmetic: 8.45 us -> none  [the longest x8 7.89 us: visit(): from_behind(weighted.astype(jnp.bfloat16), 'blk', 1).astype(weighted.dtype)]
    reduce_sum x12 -> x0, other arithmetic: 6.36 us -> none  [the longest x8 2.85 us: absorb_block(): running_sum = running_sum * shrink + jnp.sum(exponent, axis=-1)]
    all_to_all x1 -> x0, blocking collectives: 3.94 us -> none  [per_device(): lax.all_to_all(attended, 'head', split_axis=0, concat_axis=1, tiled=True)]
    all_to_all x1 -> x0, starting transfers between devices: 3.53 us -> none  [per_device(): lax.all_to_all(stacked, 'head', split_axis=2, concat_axis=0, tiled=True)]
  transfers between devices with their start and end apart: 33 -> 9, of which waited for: 9 -> 3; matrix products, arithmetic and copies ran while one was open for 30% -> 7% of each run, Pallas kernels for 0% -> 49%
where the time goes in v1:
time: 68.1 us; the launch traced here: 67.9 us
  Pallas kernels  39.3 us (58%)
  starting transfers between devices  12.3 us (18%)
  waiting for transfers between devices  11 us (16%)
  local copies, waits for them, and re-layouts  5.1 us (7%)
    pallas_call x10, Pallas kernels, call(): pl.pallas_call(body, out_shape=outs if len(outs) > 1 else outs[0], in_spe...  39.3 us
    ppermute x3, starting transfers between devices, per_device(): one = lax.ppermute(one, axes, straight)  5.36 us
    ppermute x1, waiting for transfers between devices, per_device(): one = lax.ppermute(patches, axes, straight)  5.33 us
    slice x2, local copies, waits for them, and re-layouts, per_device(): w_query, w_kv = (w_qkv[:, :width], w_qkv[:, width:])  4.3 us
    ppermute x3, waiting for transfers between devices, per_device(): one = lax.ppermute(one, axes, straight)  3.69 us
    ppermute x2, starting transfers between devices, per_device(): two = lax.ppermute(two, axes, straight)  3.22 us
    ppermute x1, starting transfers between devices, per_device(): one = lax.ppermute(patches, axes, straight)  3.02 us
    ppermute x1, waiting for transfers between devices, per_device(): came = lax.ppermute(sent, 'head', [(0, 1), (1, 0)])  1.92 us
  transfers between devices with their start and end apart: 9, of which 3 were waited for; matrix products, arithmetic and copies ran while one was open for 7% of the time, Pallas kernels for 49%

profile of v1, /device:TPU:0, one launch (start us, length us, event | category | flops | bytes accessed | tf_op | source)
XLA Modules:
  0.0 67.9 jit_solution(335698108173287890)
XLA Ops:
  0.0 3.0 %collective-permute-start = (bf16[128,1024]{1,0:T(8,128)(2,1)}, bf16[128,1024]{1,0:T(8,128)(2,1)S(1)}, u32[]{:S(2)}, u32[]{:S(2)}) collective-permute-start(bf16[128,1024]{1,0:T(8,128)(2,1)} %x_ref.1), channel_id=1, source_target_pairs={{0,2},{1,0},{2,4},{3,1},{4,6},{5,3},{6,7},{7,5},{8,9},{9,11},{10,8... | collective-permute-start | bytes 786440 | tf_op jit(solution)/shard_map/ppermute | solution.py:162
  3.0 0.7 collective-permute-start.5
  3.7 5.3 %collective-permute-done.x_ref = bf16[128,1024]{1,0:T(8,128)(2,1)S(1)} collective-permute-done((bf16[128,1024]{1,0:T(8,128)(2,1)}, bf16[128,1024]{1,0:T(8,128)(2,1)S(1)}, u32[]{:S(2)}, u32[]{:S(2)}) %collective-permute-start) | collective-permute-done | bytes 262176 | tf_op jit(solution)/shard_map/ppermute | solution.py:162
  9.0 2.4 %collective-permute-start.1 = (bf16[128,1024]{1,0:T(8,128)(2,1)S(1)}, bf16[128,1024]{1,0:T(8,128)(2,1)S(1)}, u32[]{:S(2)}, u32[]{:S(2)}) collective-permute-start(bf16[128,1024]{1,0:T(8,128)(2,1)S(1)} %collective-permute-done.x_ref), channel_id=1, source_target_pairs={{0,2},{1,0},{2,4},{3,1},{4,6},{5,3},{6,7},{7,5},{8,9},{9,11},{10,8... | collective-permute-start | bytes 786440 | tf_op jit(solution)/shard_map/ppermute | solution.py:193
  11.4 1.6 %collective-permute-start.6 = (bf16[128,1024]{1,0:T(8,128)(2,1)S(1)}, bf16[128,1024]{1,0:T(8,128)(2,1)S(1)}, u32[]{:S(2)}, u32[]{:S(2)}) collective-permute-start(bf16[128,1024]{1,0:T(8,128)(2,1)S(1)} %collective-permute-done.5.x_ref), channel_id=1, source_target_pairs={{0,2},{1,0},{2,4},{3,1},{4,6},{5,3},{6,7},{7,5},{8,9},{9,11},{10,8... | collective-permute-start | bytes 786440 | tf_op jit(solution)/shard_map/ppermute | solution.py:197
  13.0 3.7 %collective-permute-done.1.x_ref = bf16[128,1024]{1,0:T(8,128)(2,1)S(1)} collective-permute-done((bf16[128,1024]{1,0:T(8,128)(2,1)S(1)}, bf16[128,1024]{1,0:T(8,128)(2,1)S(1)}, u32[]{:S(2)}, u32[]{:S(2)}) %collective-permute-start.1) | collective-permute-done | bytes 262176 | tf_op jit(solution)/shard_map/ppermute | solution.py:193
  16.7 1.1 %collective-permute-start.2 = (bf16[128,1024]{1,0:T(8,128)(2,1)S(1)}, bf16[128,1024]{1,0:T(8,128)(2,1)S(1)}, u32[]{:S(2)}, u32[]{:S(2)}) collective-permute-start(bf16[128,1024]{1,0:T(8,128)(2,1)S(1)} %collective-permute-done.1.x_ref), channel_id=1, source_target_pairs={{0,2},{1,0},{2,4},{3,1},{4,6},{5,3},{6,7},{7,5},{8,9},{9,11},{10,8... | collective-permute-start | bytes 786440 | tf_op jit(solution)/shard_map/ppermute | solution.py:193
  17.8 0.8 %fusion = (f32[1,1024]{1,0:T(1,128)S(1)}, f32[1,1024]{1,0:T(1,128)S(1)}) fusion(f32[2,1024]{1,0:T(2,128)} %param.8), kind=kLoop, calls=%fused_computation | loop fusion | bytes 16384 | tf_op jit(solution)/shard_map/slice | solution.py:160
  18.6 1.8 %slice.14.wq_ref = bf16[1024,1024]{1,0:T(8,128)(2,1)S(1)} slice(bf16[1024,3072]{1,0:T(8,128)(2,1)} %param.7), slice={[0:1024], [0:1024]} | slice | bytes 4194304 | tf_op jit(solution)/shard_map/slice | solution.py:159
  20.4 2.5 %slice.12.wkv_ref = bf16[1024,2048]{1,0:T(8,128)(2,1)S(1)} slice(bf16[1024,3072]{1,0:T(8,128)(2,1)} %param.7), slice={[0:1024], [1024:3072]} | slice | bytes 8388608 | tf_op jit(solution)/shard_map/slice | solution.py:159
  22.9 1.7 %shard_map.55.q_ref = bf16[1024,256]{1,0:T(8,128)(2,1)S(1)} custom-call(bf16[128,1024]{1,0:T(8,128)(2,1)S(1)} %copy-done.1, bf16[128,1024]{1,0:T(8,128)(2,1)S(1)} %collective-permute-done.4.sibling_ref, f32[1,1024]{1,0:T(1,128)S(1)} %bitcast.1, bf16[1024,1024]{1,0:T(8,128)(2,1)S(1)} %slice.14.wq_ref, f32[1,1024]{1,0:T(1,128)S(1)} %get-tuple-element.51.gq_ref), custom_call_target="tpu_custom_call" | custom-call | flops 536870912 | bytes 3153920 | tf_op jit(solution)/shard_map/pallas_call | solution.py:136
  24.7 4.5 %shard_map.56 = (f32[16,256]{1,0:T(8,128)S(1)}, f32[16,256]{1,0:T(8,128)S(1)}, f32[1024,256]{1,0:T(8,128)S(1)}) custom-call(bf16[128,1024]{1,0:T(8,128)(2,1)S(1)} %copy-done.1, f32[1,1024]{1,0:T(1,128)S(1)} %bitcast.2, bf16[1024,2048]{1,0:T(8,128)(2,1)S(1)} %slice.12.wkv_ref, f32[1,1024]{1,0:T(1,128)S(1)} %get-tuple-element.52.gk_ref, ...), custom_call_target="tpu_custom_call" | custom-call | flops 671088640 | bytes 6070272 | tf_op jit(solution)/shard_map/pallas_call | solution.py:136
  29.2 1.6 %collective-permute-start.7 = (bf16[128,1024]{1,0:T(8,128)(2,1)S(1)}, bf16[128,1024]{1,0:T(8,128)(2,1)S(1)}, u32[]{:S(2)}, u32[]{:S(2)}) collective-permute-start(bf16[128,1024]{1,0:T(8,128)(2,1)S(1)} %collective-permute-done.6.x_ref), channel_id=1, source_target_pairs={{0,2},{1,0},{2,4},{3,1},{4,6},{5,3},{6,7},{7,5},{8,9},{9,11},{10,8... | collective-permute-start | bytes 786440 | tf_op jit(solution)/shard_map/ppermute | solution.py:197
  30.8 4.5 %shard_map.57 = (f32[16,256]{1,0:T(8,128)S(1)}, f32[16,256]{1,0:T(8,128)S(1)}, f32[1024,256]{1,0:T(8,128)S(1)}) custom-call(bf16[128,1024]{1,0:T(8,128)(2,1)S(1)} %collective-permute-done.x_ref, f32[1,1024]{1,0:T(1,128)S(1)} %bitcast.3, bf16[1024,2048]{1,0:T(8,128)(2,1)S(1)} %slice.12.wkv_ref, f32[1,1024]{1,0:T(1,128)S(1)} %get-tuple-element.52.gk_ref, ...), custom_call_target="tpu_custom_call" | custom-call | flops 671088640 | bytes 7151616 | tf_op jit(solution)/shard_map/pallas_call | solution.py:136
  35.4 1.9 %collective-permute-start.3 = (bf16[128,1024]{1,0:T(8,128)(2,1)S(1)}, bf16[128,1024]{1,0:T(8,128)(2,1)S(1)}, u32[]{:S(2)}, u32[]{:S(2)}) collective-permute-start(bf16[128,1024]{1,0:T(8,128)(2,1)S(1)} %collective-permute-done.2.x_ref), channel_id=1, source_target_pairs={{0,2},{1,0},{2,4},{3,1},{4,6},{5,3},{6,7},{7,5},{8,9},{9,11},{10,8... | collective-permute-start | bytes 786440 | tf_op jit(solution)/shard_map/ppermute | solution.py:193
  37.2 4.5 %shard_map.58 = (f32[16,256]{1,0:T(8,128)S(1)}, f32[16,256]{1,0:T(8,128)S(1)}, f32[1024,256]{1,0:T(8,128)S(1)}) custom-call(bf16[128,1024]{1,0:T(8,128)(2,1)S(1)} %collective-permute-done.5.x_ref, f32[1,1024]{1,0:T(1,128)S(1)} %bitcast.4, bf16[1024,2048]{1,0:T(8,128)(2,1)S(1)} %slice.12.wkv_ref, f32[1,1024]{1,0:T(1,128)S(1)} %get-tuple-element.52.gk_ref, ...), custom_call_target="tpu_custom_call" | custom-call | flops 671088640 | bytes 7151616 | tf_op jit(solution)/shard_map/pallas_call | solution.py:136
  41.8 4.5 %shard_map.59 = (f32[16,256]{1,0:T(8,128)S(1)}, f32[16,256]{1,0:T(8,128)S(1)}, f32[1024,256]{1,0:T(8,128)S(1)}) custom-call(bf16[128,1024]{1,0:T(8,128)(2,1)S(1)} %collective-permute-done.1.x_ref, f32[1,1024]{1,0:T(1,128)S(1)} %bitcast.5, bf16[1024,2048]{1,0:T(8,128)(2,1)S(1)} %slice.12.wkv_ref, f32[1,1024]{1,0:T(1,128)S(1)} %get-tuple-element.52.gk_ref, ...), custom_call_target="tpu_custom_call" | custom-call | flops 671088640 | bytes 7151616 | tf_op jit(solution)/shard_map/pallas_call | solution.py:136
  46.3 4.5 %shard_map.60 = (f32[16,256]{1,0:T(8,128)S(1)}, f32[16,256]{1,0:T(8,128)S(1)}, f32[1024,256]{1,0:T(8,128)S(1)}) custom-call(bf16[128,1024]{1,0:T(8,128)(2,1)S(1)} %collective-permute-done.6.x_ref, f32[1,1024]{1,0:T(1,128)S(1)} %bitcast.6, bf16[1024,2048]{1,0:T(8,128)(2,1)S(1)} %slice.12.wkv_ref, f32[1,1024]{1,0:T(1,128)S(1)} %get-tuple-element.52.gk_ref, ...), custom_call_target="tpu_custom_call" | custom-call | flops 671088640 | bytes 7151616 | tf_op jit(solution)/shard_map/pallas_call | solution.py:136
  50.8 4.5 %shard_map.61 = (f32[16,256]{1,0:T(8,128)S(1)}, f32[16,256]{1,0:T(8,128)S(1)}, f32[1024,256]{1,0:T(8,128)S(1)}) custom-call(bf16[128,1024]{1,0:T(8,128)(2,1)S(1)} %collective-permute-done.2.x_ref, f32[1,1024]{1,0:T(1,128)S(1)} %bitcast.7, bf16[1024,2048]{1,0:T(8,128)(2,1)S(1)} %slice.12.wkv_ref, f32[1,1024]{1,0:T(1,128)S(1)} %get-tuple-element.52.gk_ref, ...), custom_call_target="tpu_custom_call" | custom-call | flops 671088640 | bytes 7151616 | tf_op jit(solution)/shard_map/pallas_call | solution.py:136
  55.4 4.7 %shard_map.62 = (f32[16,256]{1,0:T(8,128)S(1)}, f32[16,256]{1,0:T(8,128)S(1)}, f32[1024,256]{1,0:T(8,128)S(1)}) custom-call(bf16[128,1024]{1,0:T(8,128)(2,1)S(1)} %collective-permute-done.7.x_ref, f32[1,1024]{1,0:T(1,128)S(1)} %bitcast.8, bf16[1024,2048]{1,0:T(8,128)(2,1)S(1)} %slice.12.wkv_ref, f32[1,1024]{1,0:T(1,128)S(1)} %get-tuple-element.52.gk_ref, ...), custom_call_target="tpu_custom_call" | custom-call | flops 671088640 | bytes 7151616 | tf_op jit(solution)/shard_map/pallas_call | solution.py:136
  60.1 4.5 %shard_map.63 = (f32[1056,128]{1,0:T(8,128)S(1)}, f32[1056,128]{1,0:T(8,128)S(1)}) custom-call(bf16[128,1024]{1,0:T(8,128)(2,1)S(1)} %collective-permute-done.3.x_ref, f32[1,1024]{1,0:T(1,128)S(1)} %bitcast.9, bf16[1024,2048]{1,0:T(8,128)(2,1)S(1)} %slice.12.wkv_ref, f32[1,1024]{1,0:T(1,128)S(1)} %get-tuple-element.52.gk_ref, ...), custom_call_target="tpu_custom_call" | custom-call | flops 671088640 | bytes 7151616 | tf_op jit(solution)/shard_map/pallas_call | solution.py:136
  64.7 0.1 collective-permute-start.8
  64.7 1.9 %collective-permute-done.8.came_ref = f32[1056,128]{1,0:T(8,128)S(1)} collective-permute-done((f32[1056,128]{1,0:T(8,128)S(1)}, f32[1056,128]{1,0:T(8,128)S(1)}, u32[]{:S(2)}, u32[]{:S(2)}) %collective-permute-start.8) | collective-permute-done | bytes 540704 | tf_op jit(solution)/shard_map/ppermute | solution.py:201
  66.7 1.2 %shard_map.64 = bf16[128,1024]{1,0:T(8,128)(2,1)} custom-call(f32[1056,128]{1,0:T(8,128)S(1)} %get-tuple-element.49.kept_ref, f32[1056,128]{1,0:T(8,128)S(1)} %collective-permute-done.8.came_ref, bf16[1024,1024]{1,0:T(8,128)(2,1)S(1)} %copy-done), custom_call_target="tpu_custom_call" | custom-call | flops 268435456 | bytes 3440640 | tf_op jit(solution)/shard_map/pallas_call | solution.py:136
  (13 shorter events, 0.0 us)
Async XLA Ops:
  0.0 9.0 %collective-permute-start = (bf16[128,1024]{1,0:T(8,128)(2,1)}, bf16[128,1024]{1,0:T(8,128)(2,1)S(1)}, u32[]{:S(2)}, u32[]{:S(2)}) collective-permute-start(bf16[128,1024]{1,0:T(8,128)(2,1)} %x_ref.1), channel_id=1, source_target_pairs={{0,2},{1,0},{2,4},{3,1},{4,6},{5,3},{6,7},{7,5},{8,9},{9,11},{10,8... | collective-permute-start | bytes 786440 | tf_op jit(solution)/shard_map/ppermute | solution.py:162
  3.0 8.4 %collective-permute-start.5 = (bf16[128,1024]{1,0:T(8,128)(2,1)}, bf16[128,1024]{1,0:T(8,128)(2,1)S(1)}, u32[]{:S(2)}, u32[]{:S(2)}) collective-permute-start(bf16[128,1024]{1,0:T(8,128)(2,1)} %x_ref.1), channel_id=1, source_target_pairs={{8,2},{9,0},{10,4},{11,1},{12,6},{13,3},{14,7},{15,5},{0,9},{1,11}... | collective-permute-start | bytes 786440 | tf_op jit(solution)/shard_map/ppermute | solution.py:163
  9.0 7.6 %collective-permute-start.1 = (bf16[128,1024]{1,0:T(8,128)(2,1)S(1)}, bf16[128,1024]{1,0:T(8,128)(2,1)S(1)}, u32[]{:S(2)}, u32[]{:S(2)}) collective-permute-start(bf16[128,1024]{1,0:T(8,128)(2,1)S(1)} %collective-permute-done.x_ref), channel_id=1, source_target_pairs={{0,2},{1,0},{2,4},{3,1},{4,6},{5,3},{6,7},{7,5},{8,9},{9,11},{10,8... | collective-permute-start | bytes 786440 | tf_op jit(solution)/shard_map/ppermute | solution.py:193
  11.4 11.5 %collective-permute-start.4 = (bf16[128,1024]{1,0:T(8,128)(2,1)}, bf16[128,1024]{1,0:T(8,128)(2,1)S(1)}, u32[]{:S(2)}, u32[]{:S(2)}) collective-permute-start(bf16[128,1024]{1,0:T(8,128)(2,1)} %x_ref.1), channel_id=1, source_target_pairs={{0,8},{8,0},{1,9},{9,1},{2,10},{10,2},{3,11},{11,3},{4,12},{12,4},... | collective-permute-start | bytes 786440 | tf_op jit(solution)/shard_map/ppermute | solution.py:161
  11.4 17.7 %collective-permute-start.6 = (bf16[128,1024]{1,0:T(8,128)(2,1)S(1)}, bf16[128,1024]{1,0:T(8,128)(2,1)S(1)}, u32[]{:S(2)}, u32[]{:S(2)}) collective-permute-start(bf16[128,1024]{1,0:T(8,128)(2,1)S(1)} %collective-permute-done.5.x_ref), channel_id=1, source_target_pairs={{0,2},{1,0},{2,4},{3,1},{4,6},{5,3},{6,7},{7,5},{8,9},{9,11},{10,8... | collective-permute-start | bytes 786440 | tf_op jit(solution)/shard_map/ppermute | solution.py:197
  16.7 18.7 %collective-permute-start.2 = (bf16[128,1024]{1,0:T(8,128)(2,1)S(1)}, bf16[128,1024]{1,0:T(8,128)(2,1)S(1)}, u32[]{:S(2)}, u32[]{:S(2)}) collective-permute-start(bf16[128,1024]{1,0:T(8,128)(2,1)S(1)} %collective-permute-done.1.x_ref), channel_id=1, source_target_pairs={{0,2},{1,0},{2,4},{3,1},{4,6},{5,3},{6,7},{7,5},{8,9},{9,11},{10,8... | collective-permute-start | bytes 786440 | tf_op jit(solution)/shard_map/ppermute | solution.py:193
  20.3 2.6 %copy-start.1 = (bf16[128,1024]{1,0:T(8,128)(2,1)S(1)}, bf16[128,1024]{1,0:T(8,128)(2,1)}, u32[]{:S(2)}) copy-start(bf16[128,1024]{1,0:T(8,128)(2,1)} %x_ref.1) | copy-start | bytes 786436
  20.4 2.6 %copy-start.2 = (f32[1024]{0:T(1024)S(1)}, f32[1024]{0:T(1024)}, u32[]{:S(2)}) copy-start(f32[1024]{0:T(1024)} %param.6) | copy-start | bytes 12292
  29.2 26.2 %collective-permute-start.7 = (bf16[128,1024]{1,0:T(8,128)(2,1)S(1)}, bf16[128,1024]{1,0:T(8,128)(2,1)S(1)}, u32[]{:S(2)}, u32[]{:S(2)}) collective-permute-start(bf16[128,1024]{1,0:T(8,128)(2,1)S(1)} %collective-permute-done.6.x_ref), channel_id=1, source_target_pairs={{0,2},{1,0},{2,4},{3,1},{4,6},{5,3},{6,7},{7,5},{8,9},{9,11},{10,8... | collective-permute-start | bytes 786440 | tf_op jit(solution)/shard_map/ppermute | solution.py:197
  35.4 24.8 %collective-permute-start.3 = (bf16[128,1024]{1,0:T(8,128)(2,1)S(1)}, bf16[128,1024]{1,0:T(8,128)(2,1)S(1)}, u32[]{:S(2)}, u32[]{:S(2)}) collective-permute-start(bf16[128,1024]{1,0:T(8,128)(2,1)S(1)} %collective-permute-done.2.x_ref), channel_id=1, source_target_pairs={{0,2},{1,0},{2,4},{3,1},{4,6},{5,3},{6,7},{7,5},{8,9},{9,11},{10,8... | collective-permute-start | bytes 786440 | tf_op jit(solution)/shard_map/ppermute | solution.py:193
  60.1 6.6 %copy-start = (bf16[1024,1024]{1,0:T(8,128)(2,1)S(1)}, bf16[1024,1024]{1,0:T(8,128)(2,1)}, u32[]{:S(2)}) copy-start(bf16[1024,1024]{1,0:T(8,128)(2,1)} %w_ref.1) | copy-start | bytes 6291460
  64.7 2.0 %collective-permute-start.8 = (f32[1056,128]{1,0:T(8,128)S(1)}, f32[1056,128]{1,0:T(8,128)S(1)}, u32[]{:S(2)}, u32[]{:S(2)}) collective-permute-start(f32[1056,128]{1,0:T(8,128)S(1)} %get-tuple-element.50), channel_id=1, source_target_pairs={{0,8},{8,0},{1,9},{9,1},{2,10},{10,2},{3,11},{11,3},{4,12},{12,4},... | collective-permute-start | bytes 1622024 | tf_op jit(solution)/shard_map/ppermute | solution.py:201

commit v2 on v1

v2 whole, which is shorter than its diff:
```python
import functools

import jax
import jax.numpy as jnp
from jax import lax
from jax.experimental import pallas as pl
from jax.experimental.pallas import tpu as pltpu
from jax.sharding import PartitionSpec as P

H = 16
HD = 64
PAIR = 2 * HD
SPAN = 4 * HD
F32 = jnp.float32
BF16 = jnp.bfloat16
VMEM = pl.BlockSpec(memory_space=pltpu.VMEM)


def ring_order(mesh):
    axis = mesh.axis_names.index("blk")
    along = mesh.devices
    for other in reversed(range(along.ndim)):
        if other != axis:
            along = along.take(0, axis=other)
    count = along.shape[0]
    coords = [getattr(device, "coords", None) for device in along]
    if any(c is None for c in coords):
        return list(range(count))
    place = {tuple(c): i for i, c in enumerate(coords)}
    varying = [a for a in range(3) if len({c[a] for c in place}) > 1]
    if len(place) != count or len(varying) != 2:
        return list(range(count))
    short, long = sorted(varying, key=lambda a: len({c[a] for c in place}))
    columns = sorted({c[short] for c in place})
    if len(columns) != 2:
        return list(range(count))
    up = sorted((c for c in place if c[short] == columns[0]), key=lambda c: c[long])
    down = sorted((c for c in place if c[short] == columns[1]), key=lambda c: -c[long])
    return [place[c] for c in up + down]


def normalise(x_ref, gain_ref, out_ref):
    values = x_ref[...].astype(F32)
    centre = values - jnp.mean(values, axis=-1, keepdims=True)
    variance = jnp.mean(centre * centre, axis=-1, keepdims=True)
    out_ref[...] = (centre * lax.rsqrt(variance + 1e-05) * gain_ref[...]).astype(BF16)


def same_head():
    row = lax.broadcasted_iota(jnp.int32, (SPAN, SPAN), 0) // HD
    column = lax.broadcasted_iota(jnp.int32, (SPAN, SPAN), 1) // HD
    return jnp.where(row == column, 1.0, 0.0).astype(BF16)


def head_norm(columns, gain, ones):
    squares = jnp.dot((columns * columns).astype(BF16), ones, preferred_element_type=F32)
    return (columns * lax.rsqrt(squares * (1.0 / HD) + 1e-06) * gain).astype(BF16)


def query_kernel(own_ref, sibling_ref, w_ref, gains_ref, out_ref):
    rows, width = own_ref.shape
    ones = same_head()
    own, sibling = own_ref[...], sibling_ref[...]
    spans = [slice(at, at + SPAN) for at in range(0, width, SPAN)]
    projected = [
        (i, span, jnp.dot(block, w_ref[:, span], preferred_element_type=F32))
        for i, block in enumerate((own, sibling))
        for span in spans
    ]
    for i, span, columns in projected:
        query = head_norm(columns, gains_ref[0:1, span], ones).astype(F32) * (HD**-0.5)
        out_ref[span, i * rows : (i + 1) * rows] = query.T.astype(BF16)


def absorb(first, last, block_ref, w_ref, gains_ref, q_ref, *refs):
    if first:
        outs = refs
    else:
        (max_ref, sum_ref, acc_ref), outs = refs[:3], refs[3:]
        old_max, old_sum = max_ref[...], sum_ref[...]
    width, queries = q_ref.shape
    heads = SPAN // HD
    block = block_ref[...]
    ones = same_head()
    zeros = jnp.zeros((HD, queries), BF16)
    held = {}
    maxima, sums = [], []

    def project(i):
        for name, at in (("key", width), ("value", 2 * width)):
            span = slice(at + i * SPAN, at + (i + 1) * SPAN)
            held[name, i] = jnp.dot(block, w_ref[:, span], preferred_element_type=F32)

    def norm(i):
        span = slice(i * SPAN, (i + 1) * SPAN)
        held["key", i] = head_norm(held["key", i], gains_ref[1:2, span], ones)
        held["value", i] = held["value", i].T.astype(BF16)

    def score(i):
        keys = held.pop(("key", i))
        for j in range(heads):
            at = i * SPAN + j * HD
            pair = j // 2 * PAIR
            query = q_ref[at : at + HD, :]
            query = jnp.concatenate([query, zeros] if j % 2 == 0 else [zeros, query], axis=0)
            held["score", i, j] = jnp.dot(
                keys[:, pair : pair + PAIR], query, preferred_element_type=F32
            )

    def soften(i):
        scores = [held.pop(("score", i, j)) for j in range(heads)]
        top = jnp.concatenate([jnp.max(s, axis=0, keepdims=True) for s in scores], axis=0)
        if not first:
            before = old_max[i * heads : (i + 1) * heads]
            top = jnp.maximum(top, before)
            held["shrink", i] = jnp.exp(before - top)
        exponents = [jnp.exp(s - top[j : j + 1]) for j, s in enumerate(scores)]
        total = jnp.concatenate([jnp.sum(e, axis=0, keepdims=True) for e in exponents], axis=0)
        if not first:
            total = total + old_sum[i * heads : (i + 1) * heads] * held["shrink", i]
        maxima.append(top)
        sums.append(total)
        for j, exponent in enumerate(exponents):
            held["weight", i, j] = exponent.astype(BF16)

    def weigh(i):
        values = held.pop(("value", i))
        for j in range(heads):
            at = i * SPAN + j * HD
            added = jnp.dot(
                values[j * HD : (j + 1) * HD],
                held.pop(("weight", i, j)),
                preferred_element_type=F32,
            )
            if not first:
                added = added + acc_ref[at : at + HD, :] * held["shrink", i][j : j + 1]
            if last:
                for ref, part in zip(outs, halves):
                    ref[at : at + HD, :] = added[:, part]
            else:
                outs[2][at : at + HD, :] = added

    halves = (slice(0, queries // 2), slice(queries // 2, queries))
    stages = (project, norm, score, soften, weigh)
    for turn in range(width // SPAN + len(stages) - 1):
        for behind, stage in enumerate(stages):
            if 0 <= turn - behind < width // SPAN:
                stage(turn - behind)
    top, total = jnp.concatenate(maxima, axis=0), jnp.concatenate(sums, axis=0)
    if last:
        for ref, part in zip(outs, halves):
            ref[width : width + H, :] = top[:, part]
            ref[width + H : width + 2 * H, :] = total[:, part]
    else:
        outs[0][...] = top
        outs[1][...] = total


def finish_kernel(kept_ref, came_ref, w_ref, out_ref):
    width = H * HD
    heads = []
    for h in range(H):
        at = slice(h * HD, (h + 1) * HD)
        m, s = slice(width + h, width + h + 1), slice(width + H + h, width + H + h + 1)
        top = jnp.maximum(kept_ref[m, :], came_ref[m, :])
        mine, theirs = jnp.exp(kept_ref[m, :] - top), jnp.exp(came_ref[m, :] - top)
        total = kept_ref[s, :] * mine + came_ref[s, :] * theirs
        summed = kept_ref[at, :] * mine + came_ref[at, :] * theirs
        heads.append((summed / total).astype(BF16))
    attended = jnp.concatenate(heads, axis=0)
    out_ref[...] = lax.dot_general(
        attended, w_ref[...], (((0,), (0,)), ((), ())), preferred_element_type=F32
    ).astype(BF16)


def call(body, outs, operands, flops, exps):
    moved = sum(a.size * a.dtype.itemsize for a in (*operands, *outs))
    return pl.pallas_call(
        body,
        out_shape=outs,
        in_specs=[VMEM] * len(operands),
        out_specs=[VMEM] * len(outs),
        compiler_params=pltpu.CompilerParams(vmem_limit_bytes=24 * 1024 * 1024),
        cost_estimate=pl.CostEstimate(flops=flops, bytes_accessed=moved, transcendentals=exps),
    )(*operands)


def per_device(order, patches, ln_gain, w_qkv, qk_gains, w_out):
    rows, width = patches.shape
    count = lax.axis_size("blk")
    place = {index: i for i, index in enumerate(order)}

    def ahead(index, head):
        return order[(place[index] + (1 if head == 0 else -1)) % count]

    straight = [(h * count + b, h * count + ahead(b, h)) for h in range(2) for b in range(count)]
    cross = [((1 - h) * count + b, h * count + ahead(b, h)) for h in range(2) for b in range(count)]
    axes = ("head", "blk")

    (normed,) = call(
        normalise, [jax.ShapeDtypeStruct((rows, width), BF16)], (patches, ln_gain.reshape(1, width)), 0, 0
    )
    one = lax.ppermute(normed, axes, straight)
    two = lax.ppermute(normed, axes, cross)
    sibling = lax.ppermute(normed, "head", [(0, 1), (1, 0)])
    (query,) = call(
        query_kernel,
        [jax.ShapeDtypeStruct((width, 2 * rows), BF16)],
        (normed, sibling, w_qkv, qk_gains),
        2 * 2 * rows * width * width,
        0,
    )
    state_shapes = [
        jax.ShapeDtypeStruct((H, 2 * rows), F32),
        jax.ShapeDtypeStruct((H, 2 * rows), F32),
        jax.ShapeDtypeStruct((width, 2 * rows), F32),
    ]
    last_shapes = [jax.ShapeDtypeStruct((width + 2 * H, rows), F32)] * 2
    flops = 2 * rows * width * 2 * width + 2 * 2 * rows * 2 * rows * width
    exps = H * rows * 2 * rows

    def take(block, state, last=False):
        return call(
            functools.partial(absorb, not state, last),
            last_shapes if last else state_shapes,
            (block, w_qkv, qk_gains, query, *state),
            4 * flops,
            exps,
        )

    state = take(normed, ())
    for turn in range(1, count // 2):
        here, one = one, lax.ppermute(one, axes, straight)
        state, two = lax.optimization_barrier((take(here, state), two))
        here = two
        if turn < count // 2 - 1:
            two = lax.ppermute(two, axes, straight)
        state, one = lax.optimization_barrier((take(here, state), one))
    kept, sent = take(one, state, last=True)
    came = lax.ppermute(sent, "head", [(0, 1), (1, 0)])
    return call(
        finish_kernel,
        [jax.ShapeDtypeStruct((rows, width), BF16)],
        (kept, came, w_out),
        2 * rows * width * width,
        0,
    )[0]


def solution(mesh):
    placed = (P(("group", "head", "blk"), None), P(), P(), P(), P())
    return jax.shard_map(
        functools.partial(per_device, ring_order(mesh)),
        mesh=mesh,
        in_specs=placed,
        out_specs=P(("group", "head", "blk"), None),
        check_vma=False,
    )
```

time: 68.1 us -> 38.4 us (0.56)
  Pallas kernels: 39.3 us -> 15.3 us
  starting transfers between devices: 12.3 us -> 8.22 us
  waiting for transfers between devices: 11 us -> 7.74 us
  local copies, waits for them, and re-layouts: 5.1 us -> 6.77 us
    pallas_call x10 -> x11, Pallas kernels: 39.3 us -> 15.3 us  [call(): pl.pallas_call(body, out_shape=outs, in_specs=[VMEM] * len(operands), out...]
    unnamed x6 -> x14, local copies, waits for them, and re-layouts: 0.02 us -> 6.77 us
    slice x3 -> x0, local copies, waits for them, and re-layouts: 5.08 us -> none  [the longest x2 4.3 us: per_device(): w_query, w_kv = (w_qkv[:, :width], w_qkv[:, width:])]
    ppermute x6, waiting for transfers between devices: 9.03 us -> 4.41 us  [the longest x3 4.41 us: per_device(): here, one = (one, lax.ppermute(one, axes, straight))]
    ppermute x6, starting transfers between devices: 9.06 us -> 5.94 us  [the longest x1 2.64 us: per_device(): one = lax.ppermute(normed, axes, straight)]
    ppermute x2, waiting for transfers between devices: 0.01 us -> 1.41 us  [per_device(): two = lax.ppermute(two, axes, straight)]
    ppermute x2, starting transfers between devices: 3.22 us -> 2.21 us  [per_device(): two = lax.ppermute(two, axes, straight)]
  transfers between devices with their start and end apart: 9 -> 9, of which waited for: 3 -> 6; matrix products, arithmetic and copies ran while one was open for 7% -> 0% of each run, Pallas kernels for 49% -> 32%
where the time goes in v2:
time: 38.4 us; the launch traced here: 38.1 us
  Pallas kernels  15.3 us (40%)
  starting transfers between devices  8.22 us (21%)
  waiting for transfers between devices  7.74 us (20%)
  local copies, waits for them, and re-layouts  6.77 us (18%)
    pallas_call x11, Pallas kernels, call(): pl.pallas_call(body, out_shape=outs, in_specs=[VMEM] * len(operands), out...  15.3 us
    unnamed x14, local copies, waits for them, and re-layouts  6.77 us
    ppermute x3, waiting for transfers between devices, per_device(): here, one = (one, lax.ppermute(one, axes, straight))  4.41 us
    ppermute x1, starting transfers between devices, per_device(): one = lax.ppermute(normed, axes, straight)  2.64 us
    ppermute x2, starting transfers between devices, per_device(): two = lax.ppermute(two, axes, straight)  2.21 us
    ppermute x1, waiting for transfers between devices, per_device(): came = lax.ppermute(sent, 'head', [(0, 1), (1, 0)])  1.92 us
    ppermute x3, starting transfers between devices, per_device(): here, one = (one, lax.ppermute(one, axes, straight))  1.5 us
    ppermute x2, waiting for transfers between devices, per_device(): two = lax.ppermute(two, axes, straight)  1.41 us
  transfers between devices with their start and end apart: 9, of which 6 were waited for; matrix products, arithmetic and copies ran while one was open for 0% of the time, Pallas kernels for 32%

profile of v2, /device:TPU:0, one launch (start us, length us, event | category | flops | bytes accessed | tf_op | source)
XLA Modules:
  0.0 38.1 jit_solution(3990109739050319256)
XLA Ops:
  0.0 0.9 %copy-done.3 = bf16[128,1024]{1,0:T(8,128)(2,1)S(1)} copy-done((bf16[128,1024]{1,0:T(8,128)(2,1)S(1)}, bf16[128,1024]{1,0:T(8,128)(2,1)}, u32[]{:S(2)}) %copy-start.3) | copy-done | bytes 262168
  1.0 0.7 %copy-done.6 = f32[1024]{0:T(1024)S(1)} copy-done((f32[1024]{0:T(1024)S(1)}, f32[1024]{0:T(1024)}, u32[]{:S(2)}) %copy-start.6) | copy-done | bytes 4120
  2.4 2.6 %collective-permute-start = (bf16[128,1024]{1,0:T(8,128)(2,1)S(1)}, bf16[128,1024]{1,0:T(8,128)(2,1)S(1)}, u32[]{:S(2)}, u32[]{:S(2)}) collective-permute-start(bf16[128,1024]{1,0:T(8,128)(2,1)S(1)} %shard_map.55.own_ref.block_ref), channel_id=1, source_target_pairs={{0,2},{1,0},{2,4},{3,1},{4,6},{5,3},{6,7},{7,5},{8,9},{9,11},{10,8... | collective-permute-start | bytes 786440 | tf_op jit(solution)/shard_map/ppermute | solution.py:203
  5.1 1.3 %collective-permute-start.2 = (bf16[128,1024]{1,0:T(8,128)(2,1)S(1)}, bf16[128,1024]{1,0:T(8,128)(2,1)S(1)}, u32[]{:S(2)}, u32[]{:S(2)}) collective-permute-start(bf16[128,1024]{1,0:T(8,128)(2,1)S(1)} %shard_map.55.own_ref.block_ref), channel_id=1, source_target_pairs={{8,2},{9,0},{10,4},{11,1},{12,6},{13,3},{14,7},{15,5},{0,9},{1,11}... | collective-permute-start | bytes 786440 | tf_op jit(solution)/shard_map/ppermute | solution.py:204
  6.3 2.8 %copy-done = bf16[1024,3072]{1,0:T(8,128)(2,1)S(1)} copy-done((bf16[1024,3072]{1,0:T(8,128)(2,1)S(1)}, bf16[1024,3072]{1,0:T(8,128)(2,1)}, u32[]{:S(2)}) %copy-start) | copy-done | bytes 6291480
  9.1 0.7 %copy-done.4 = f32[2,1024]{1,0:T(2,128)S(1)} copy-done((f32[2,1024]{1,0:T(2,128)S(1)}, f32[2,1024]{1,0:T(2,128)}, u32[]{:S(2)}) %copy-start.4) | copy-done | bytes 8216
  9.8 1.1 %shard_map.56.q_ref = bf16[1024,256]{1,0:T(8,128)(2,1)S(1)} custom-call(bf16[128,1024]{1,0:T(8,128)(2,1)S(1)} %shard_map.55.own_ref.block_ref, bf16[128,1024]{1,0:T(8,128)(2,1)S(1)} %collective-permute-done.1.sibling_ref, bf16[1024,3072]{1,0:T(8,128)(2,1)S(1)} %copy-done, f32[2,1024]{1,0:T(2,128)S(1)} %copy-done.4), custom_call_target="tpu_custom_call" | custom-call | flops 536870912 | bytes 7348224 | tf_op jit(solution)/shard_map/pallas_call | solution.py:178
  11.0 1.6 %copy-done.1 = bf16[1024,3072]{1,0:T(8,128)(2,1)S(1)} copy-done((bf16[1024,3072]{1,0:T(8,128)(2,1)S(1)}, bf16[1024,3072]{1,0:T(8,128)(2,1)}, u32[]{:S(2)}) %copy-start.1) | copy-done | bytes 6291480
  12.6 1.5 %shard_map.57 = (f32[16,256]{1,0:T(8,128)S(1)}, f32[16,256]{1,0:T(8,128)S(1)}, f32[1024,256]{1,0:T(8,128)S(1)}) custom-call(bf16[128,1024]{1,0:T(8,128)(2,1)S(1)} %shard_map.55.own_ref.block_ref, bf16[1024,3072]{1,0:T(8,128)(2,1)S(1)} %copy-done.1, f32[2,1024]{1,0:T(2,128)S(1)} %copy-done.4, bf16[1024,256]{1,0:T(8,128)(2,1)S(1)} %shard_map.56.q_ref), custom_call_target="tpu_custom_call" | custom-call | flops 2684354560 | bytes 8167424 | tf_op jit(solution)/shard_map/pallas_call | solution.py:178
  14.6 1.6 %shard_map.58 = (f32[16,256]{1,0:T(8,128)S(1)}, f32[16,256]{1,0:T(8,128)S(1)}, f32[1024,256]{1,0:T(8,128)S(1)}) custom-call(bf16[128,1024]{1,0:T(8,128)(2,1)S(1)} %collective-permute-done.block_ref, bf16[1024,3072]{1,0:T(8,128)(2,1)S(1)} %copy-done.1, f32[2,1024]{1,0:T(2,128)S(1)} %copy-done.4, bf16[1024,256]{1,0:T(8,128)(2,1)S(1)} %shard_map.56.q_ref, ...), custom_call_target="tpu_custom_call" | custom-call | flops 2684354560 | bytes 9248768 | tf_op jit(solution)/shard_map/pallas_call | solution.py:178
  16.3 1.5 %collective-permute-start.4 = (bf16[128,1024]{1,0:T(8,128)(2,1)S(1)}, bf16[128,1024]{1,0:T(8,128)(2,1)S(1)}, u32[]{:S(2)}, u32[]{:S(2)}) collective-permute-start(bf16[128,1024]{1,0:T(8,128)(2,1)S(1)} %collective-permute-done.2.block_ref), channel_id=1, source_target_pairs={{0,2},{1,0},{2,4},{3,1},{4,6},{5,3},{6,7},{7,5},{8,9},{9,11},{10,8... | collective-permute-start | bytes 786440 | tf_op jit(solution)/shard_map/ppermute | solution.py:237
  17.7 1.6 %shard_map.59 = (f32[16,256]{1,0:T(8,128)S(1)}, f32[16,256]{1,0:T(8,128)S(1)}, f32[1024,256]{1,0:T(8,128)S(1)}) custom-call(bf16[128,1024]{1,0:T(8,128)(2,1)S(1)} %collective-permute-done.2.block_ref, bf16[1024,3072]{1,0:T(8,128)(2,1)S(1)} %copy-done.1, f32[2,1024]{1,0:T(2,128)S(1)} %copy-done.4, bf16[1024,256]{1,0:T(8,128)(2,1)S(1)} %shard_map.56.q_ref, ...), custom_call_target="tpu_custom_call" | custom-call | flops 2684354560 | bytes 9248768 | tf_op jit(solution)/shard_map/pallas_call | solution.py:178
  19.3 1.2 %collective-permute-done.3.block_ref = bf16[128,1024]{1,0:T(8,128)(2,1)S(1)} collective-permute-done((bf16[128,1024]{1,0:T(8,128)(2,1)S(1)}, bf16[128,1024]{1,0:T(8,128)(2,1)S(1)}, u32[]{:S(2)}, u32[]{:S(2)}) %collective-permute-start.3) | collective-permute-done | bytes 262176 | tf_op jit(solution)/shard_map/ppermute | solution.py:233
  21.0 1.6 %shard_map.60 = (f32[16,256]{1,0:T(8,128)S(1)}, f32[16,256]{1,0:T(8,128)S(1)}, f32[1024,256]{1,0:T(8,128)S(1)}) custom-call(bf16[128,1024]{1,0:T(8,128)(2,1)S(1)} %collective-permute-done.3.block_ref, bf16[1024,3072]{1,0:T(8,128)(2,1)S(1)} %copy-done.1, f32[2,1024]{1,0:T(2,128)S(1)} %copy-done.4, bf16[1024,256]{1,0:T(8,128)(2,1)S(1)} %shard_map.56.q_ref, ...), custom_call_target="tpu_custom_call" | custom-call | flops 2684354560 | bytes 9248768 | tf_op jit(solution)/shard_map/pallas_call | solution.py:178
  22.6 0.7 %collective-permute-done.4.block_ref = bf16[128,1024]{1,0:T(8,128)(2,1)S(1)} collective-permute-done((bf16[128,1024]{1,0:T(8,128)(2,1)S(1)}, bf16[128,1024]{1,0:T(8,128)(2,1)S(1)}, u32[]{:S(2)}, u32[]{:S(2)}) %collective-permute-start.4) | collective-permute-done | bytes 262176 | tf_op jit(solution)/shard_map/ppermute | solution.py:237
  23.4 0.7 %collective-permute-start.6 = (bf16[128,1024]{1,0:T(8,128)(2,1)S(1)}, bf16[128,1024]{1,0:T(8,128)(2,1)S(1)}, u32[]{:S(2)}, u32[]{:S(2)}) collective-permute-start(bf16[128,1024]{1,0:T(8,128)(2,1)S(1)} %collective-permute-done.4.block_ref), channel_id=1, source_target_pairs={{0,2},{1,0},{2,4},{3,1},{4,6},{5,3},{6,7},{7,5},{8,9},{9,11},{10,8... | collective-permute-start | bytes 786440 | tf_op jit(solution)/shard_map/ppermute | solution.py:237
  24.1 1.6 %shard_map.61 = (f32[16,256]{1,0:T(8,128)S(1)}, f32[16,256]{1,0:T(8,128)S(1)}, f32[1024,256]{1,0:T(8,128)S(1)}) custom-call(bf16[128,1024]{1,0:T(8,128)(2,1)S(1)} %collective-permute-done.4.block_ref, bf16[1024,3072]{1,0:T(8,128)(2,1)S(1)} %copy-done.1, f32[2,1024]{1,0:T(2,128)S(1)} %copy-done.4, bf16[1024,256]{1,0:T(8,128)(2,1)S(1)} %shard_map.56.q_ref, ...), custom_call_target="tpu_custom_call" | custom-call | flops 2684354560 | bytes 9248768 | tf_op jit(solution)/shard_map/pallas_call | solution.py:178
  25.7 1.2 %collective-permute-done.5.block_ref = bf16[128,1024]{1,0:T(8,128)(2,1)S(1)} collective-permute-done((bf16[128,1024]{1,0:T(8,128)(2,1)S(1)}, bf16[128,1024]{1,0:T(8,128)(2,1)S(1)}, u32[]{:S(2)}, u32[]{:S(2)}) %collective-permute-start.5) | collective-permute-done | bytes 262176 | tf_op jit(solution)/shard_map/ppermute | solution.py:233
  27.5 1.6 %shard_map.62 = (f32[16,256]{1,0:T(8,128)S(1)}, f32[16,256]{1,0:T(8,128)S(1)}, f32[1024,256]{1,0:T(8,128)S(1)}) custom-call(bf16[128,1024]{1,0:T(8,128)(2,1)S(1)} %collective-permute-done.5.block_ref, bf16[1024,3072]{1,0:T(8,128)(2,1)S(1)} %copy-done.1, f32[2,1024]{1,0:T(2,128)S(1)} %copy-done.4, bf16[1024,256]{1,0:T(8,128)(2,1)S(1)} %shard_map.56.q_ref, ...), custom_call_target="tpu_custom_call" | custom-call | flops 2684354560 | bytes 9248768 | tf_op jit(solution)/shard_map/pallas_call | solution.py:178
  29.7 1.6 %shard_map.63 = (f32[16,256]{1,0:T(8,128)S(1)}, f32[16,256]{1,0:T(8,128)S(1)}, f32[1024,256]{1,0:T(8,128)S(1)}) custom-call(bf16[128,1024]{1,0:T(8,128)(2,1)S(1)} %collective-permute-done.6.block_ref, bf16[1024,3072]{1,0:T(8,128)(2,1)S(1)} %copy-done.1, f32[2,1024]{1,0:T(2,128)S(1)} %copy-done.4, bf16[1024,256]{1,0:T(8,128)(2,1)S(1)} %shard_map.56.q_ref, ...), custom_call_target="tpu_custom_call" | custom-call | flops 2684354560 | bytes 9248768 | tf_op jit(solution)/shard_map/pallas_call | solution.py:178
  31.3 1.9 %collective-permute-done.7.block_ref = bf16[128,1024]{1,0:T(8,128)(2,1)S(1)} collective-permute-done((bf16[128,1024]{1,0:T(8,128)(2,1)S(1)}, bf16[128,1024]{1,0:T(8,128)(2,1)S(1)}, u32[]{:S(2)}, u32[]{:S(2)}) %collective-permute-start.7) | collective-permute-done | bytes 262176 | tf_op jit(solution)/shard_map/ppermute | solution.py:233
  33.3 1.6 %shard_map.64 = (f32[1056,128]{1,0:T(8,128)S(1)}, f32[1056,128]{1,0:T(8,128)S(1)}) custom-call(bf16[128,1024]{1,0:T(8,128)(2,1)S(1)} %collective-permute-done.7.block_ref, bf16[1024,3072]{1,0:T(8,128)(2,1)S(1)} %copy-done.1, f32[2,1024]{1,0:T(2,128)S(1)} %copy-done.5, bf16[1024,256]{1,0:T(8,128)(2,1)S(1)} %shard_map.56.q_ref, ...), custom_call_target="tpu_custom_call" | custom-call | flops 2684354560 | bytes 9248768 | tf_op jit(solution)/shard_map/pallas_call | solution.py:178
  35.0 1.9 %collective-permute-done.8.came_ref = f32[1056,128]{1,0:T(8,128)S(1)} collective-permute-done((f32[1056,128]{1,0:T(8,128)S(1)}, f32[1056,128]{1,0:T(8,128)S(1)}, u32[]{:S(2)}, u32[]{:S(2)}) %collective-permute-start.8) | collective-permute-done | bytes 540704 | tf_op jit(solution)/shard_map/ppermute | solution.py:240
  36.9 1.2 %shard_map.65 = bf16[128,1024]{1,0:T(8,128)(2,1)} custom-call(f32[1056,128]{1,0:T(8,128)S(1)} %get-tuple-element.97.kept_ref, f32[1056,128]{1,0:T(8,128)S(1)} %collective-permute-done.8.came_ref, bf16[1024,1024]{1,0:T(8,128)(2,1)S(1)} %copy-done.2), custom_call_target="tpu_custom_call" | custom-call | flops 268435456 | bytes 3440640 | tf_op jit(solution)/shard_map/pallas_call | solution.py:178
  (19 shorter events, 3.0 us)
Async XLA Ops:
  0.0 0.9 %copy-start.3 = (bf16[128,1024]{1,0:T(8,128)(2,1)S(1)}, bf16[128,1024]{1,0:T(8,128)(2,1)}, u32[]{:S(2)}) copy-start(bf16[128,1024]{1,0:T(8,128)(2,1)} %x_ref.1) | copy-start | bytes 786436
  1.0 0.7 %copy-start.6 = (f32[1024]{0:T(1024)S(1)}, f32[1024]{0:T(1024)}, u32[]{:S(2)}) copy-start(f32[1024]{0:T(1024)} %param.6) | copy-start | bytes 12292
  1.9 4.4 %collective-permute-start.1 = (bf16[128,1024]{1,0:T(8,128)(2,1)S(1)}, bf16[128,1024]{1,0:T(8,128)(2,1)S(1)}, u32[]{:S(2)}, u32[]{:S(2)}) collective-permute-start(bf16[128,1024]{1,0:T(8,128)(2,1)S(1)} %shard_map.55.own_ref.block_ref), channel_id=1, source_target_pairs={{0,8},{8,0},{1,9},{9,1},{2,10},{10,2},{3,11},{11,3},{4,12},{12,4},... | collective-permute-start | bytes 786440 | tf_op jit(solution)/shard_map/ppermute | solution.py:205
  2.4 11.7 %collective-permute-start = (bf16[128,1024]{1,0:T(8,128)(2,1)S(1)}, bf16[128,1024]{1,0:T(8,128)(2,1)S(1)}, u32[]{:S(2)}, u32[]{:S(2)}) collective-permute-start(bf16[128,1024]{1,0:T(8,128)(2,1)S(1)} %shard_map.55.own_ref.block_ref), channel_id=1, source_target_pairs={{0,2},{1,0},{2,4},{3,1},{4,6},{5,3},{6,7},{7,5},{8,9},{9,11},{10,8... | collective-permute-start | bytes 786440 | tf_op jit(solution)/shard_map/ppermute | solution.py:203
  5.1 11.2 %collective-permute-start.2 = (bf16[128,1024]{1,0:T(8,128)(2,1)S(1)}, bf16[128,1024]{1,0:T(8,128)(2,1)S(1)}, u32[]{:S(2)}, u32[]{:S(2)}) collective-permute-start(bf16[128,1024]{1,0:T(8,128)(2,1)S(1)} %shard_map.55.own_ref.block_ref), channel_id=1, source_target_pairs={{8,2},{9,0},{10,4},{11,1},{12,6},{13,3},{14,7},{15,5},{0,9},{1,11}... | collective-permute-start | bytes 786440 | tf_op jit(solution)/shard_map/ppermute | solution.py:204
  6.3 2.8 %copy-start = (bf16[1024,3072]{1,0:T(8,128)(2,1)S(1)}, bf16[1024,3072]{1,0:T(8,128)(2,1)}, u32[]{:S(2)}) copy-start(bf16[1024,3072]{1,0:T(8,128)(2,1)} %w_ref.18) | copy-start | bytes 18874372
  9.1 0.7 %copy-start.4 = (f32[2,1024]{1,0:T(2,128)S(1)}, f32[2,1024]{1,0:T(2,128)}, u32[]{:S(2)}) copy-start(f32[2,1024]{1,0:T(2,128)} %gains_ref.17) | copy-start | bytes 24580
  9.8 2.8 %copy-start.1 = (bf16[1024,3072]{1,0:T(8,128)(2,1)S(1)}, bf16[1024,3072]{1,0:T(8,128)(2,1)}, u32[]{:S(2)}) copy-start(bf16[1024,3072]{1,0:T(8,128)(2,1)} %w_ref.18) | copy-start | bytes 18874372
  14.1 6.4 %collective-permute-start.3 = (bf16[128,1024]{1,0:T(8,128)(2,1)S(1)}, bf16[128,1024]{1,0:T(8,128)(2,1)S(1)}, u32[]{:S(2)}, u32[]{:S(2)}) collective-permute-start(bf16[128,1024]{1,0:T(8,128)(2,1)S(1)} %collective-permute-done.block_ref), channel_id=1, source_target_pairs={{0,2},{1,0},{2,4},{3,1},{4,6},{5,3},{6,7},{7,5},{8,9},{9,11},{10,8... | collective-permute-start | bytes 786440 | tf_op jit(solution)/shard_map/ppermute | solution.py:233
  16.3 7.1 %collective-permute-start.4 = (bf16[128,1024]{1,0:T(8,128)(2,1)S(1)}, bf16[128,1024]{1,0:T(8,128)(2,1)S(1)}, u32[]{:S(2)}, u32[]{:S(2)}) collective-permute-start(bf16[128,1024]{1,0:T(8,128)(2,1)S(1)} %collective-permute-done.2.block_ref), channel_id=1, source_target_pairs={{0,2},{1,0},{2,4},{3,1},{4,6},{5,3},{6,7},{7,5},{8,9},{9,11},{10,8... | collective-permute-start | bytes 786440 | tf_op jit(solution)/shard_map/ppermute | solution.py:237
  20.6 6.4 %collective-permute-start.5 = (bf16[128,1024]{1,0:T(8,128)(2,1)S(1)}, bf16[128,1024]{1,0:T(8,128)(2,1)S(1)}, u32[]{:S(2)}, u32[]{:S(2)}) collective-permute-start(bf16[128,1024]{1,0:T(8,128)(2,1)S(1)} %collective-permute-done.3.block_ref), channel_id=1, source_target_pairs={{0,2},{1,0},{2,4},{3,1},{4,6},{5,3},{6,7},{7,5},{8,9},{9,11},{10,8... | collective-permute-start | bytes 786440 | tf_op jit(solution)/shard_map/ppermute | solution.py:233
  23.4 6.4 %collective-permute-start.6 = (bf16[128,1024]{1,0:T(8,128)(2,1)S(1)}, bf16[128,1024]{1,0:T(8,128)(2,1)S(1)}, u32[]{:S(2)}, u32[]{:S(2)}) collective-permute-start(bf16[128,1024]{1,0:T(8,128)(2,1)S(1)} %collective-permute-done.4.block_ref), channel_id=1, source_target_pairs={{0,2},{1,0},{2,4},{3,1},{4,6},{5,3},{6,7},{7,5},{8,9},{9,11},{10,8... | collective-permute-start | bytes 786440 | tf_op jit(solution)/shard_map/ppermute | solution.py:237
  26.9 6.4 %collective-permute-start.7 = (bf16[128,1024]{1,0:T(8,128)(2,1)S(1)}, bf16[128,1024]{1,0:T(8,128)(2,1)S(1)}, u32[]{:S(2)}, u32[]{:S(2)}) collective-permute-start(bf16[128,1024]{1,0:T(8,128)(2,1)S(1)} %collective-permute-done.5.block_ref), channel_id=1, source_target_pairs={{0,2},{1,0},{2,4},{3,1},{4,6},{5,3},{6,7},{7,5},{8,9},{9,11},{10,8... | collective-permute-start | bytes 786440 | tf_op jit(solution)/shard_map/ppermute | solution.py:233
  29.1 4.2 %copy-start.5 = (f32[2,1024]{1,0:T(2,128)S(1)}, f32[2,1024]{1,0:T(2,128)}, u32[]{:S(2)}) copy-start(f32[2,1024]{1,0:T(2,128)} %gains_ref.17) | copy-start | bytes 24580
  31.3 5.6 %copy-start.2 = (bf16[1024,1024]{1,0:T(8,128)(2,1)S(1)}, bf16[1024,1024]{1,0:T(8,128)(2,1)}, u32[]{:S(2)}) copy-start(bf16[1024,1024]{1,0:T(8,128)(2,1)} %w_ref.19) | copy-start | bytes 6291460
  34.9 2.0 %collective-permute-start.8 = (f32[1056,128]{1,0:T(8,128)S(1)}, f32[1056,128]{1,0:T(8,128)S(1)}, u32[]{:S(2)}, u32[]{:S(2)}) collective-permute-start(f32[1056,128]{1,0:T(8,128)S(1)} %get-tuple-element.98), channel_id=1, source_target_pairs={{0,8},{8,0},{1,9},{9,1},{2,10},{10,2},{3,11},{11,3},{4,12},{12,4},... | collective-permute-start | bytes 1622024 | tf_op jit(solution)/shard_map/ppermute | solution.py:240

commit v3 on v2

--- a/solution.py
+++ b/solution.py
@@ -39,17 +39,17 @@
     return [place[c] for c in up + down]
 
 
-def normalise(x_ref, gain_ref, out_ref):
-    values = x_ref[...].astype(F32)
+def same_head_kernel(out_ref):
+    row = lax.broadcasted_iota(jnp.int32, out_ref.shape, 0) // HD
+    column = lax.broadcasted_iota(jnp.int32, out_ref.shape, 1) // HD
+    out_ref[...] = jnp.where(row == column, 1.0, 0.0).astype(BF16)
+
+
+def normalised(block, gain):
+    values = block.astype(F32)
     centre = values - jnp.mean(values, axis=-1, keepdims=True)
     variance = jnp.mean(centre * centre, axis=-1, keepdims=True)
-    out_ref[...] = (centre * lax.rsqrt(variance + 1e-05) * gain_ref[...]).astype(BF16)
-
-
-def same_head():
-    row = lax.broadcasted_iota(jnp.int32, (SPAN, SPAN), 0) // HD
-    column = lax.broadcasted_iota(jnp.int32, (SPAN, SPAN), 1) // HD
-    return jnp.where(row == column, 1.0, 0.0).astype(BF16)
+    return (centre * lax.rsqrt(variance + 1e-05) * gain).astype(BF16)
 
 
 def head_norm(columns, gain, ones):
@@ -57,22 +57,25 @@
     return (columns * lax.rsqrt(squares * (1.0 / HD) + 1e-06) * gain).astype(BF16)
 
 
-def query_kernel(own_ref, sibling_ref, w_ref, gains_ref, out_ref):
+def query_kernel(
+    own_ref, sibling_ref, w_ref, gain_ref, gains_ref, ones_ref, normed_ref, query_ref
+):
     rows, width = own_ref.shape
-    ones = same_head()
-    own, sibling = own_ref[...], sibling_ref[...]
+    ones = ones_ref[...]
     spans = [slice(at, at + SPAN) for at in range(0, width, SPAN)]
+    own = normalised(own_ref[...], gain_ref[...])
+    normed_ref[...] = own
     projected = [
         (i, span, jnp.dot(block, w_ref[:, span], preferred_element_type=F32))
-        for i, block in enumerate((own, sibling))
+        for i, block in enumerate((own, normalised(sibling_ref[...], gain_ref[...])))
         for span in spans
     ]
     for i, span, columns in projected:
         query = head_norm(columns, gains_ref[0:1, span], ones).astype(F32) * (HD**-0.5)
-        out_ref[span, i * rows : (i + 1) * rows] = query.T.astype(BF16)
-
-
-def absorb(first, last, block_ref, w_ref, gains_ref, q_ref, *refs):
+        query_ref[span, i * rows : (i + 1) * rows] = query.T.astype(BF16)
+
+
+def absorb(first, last, raw, block_ref, w_ref, gain_ref, gains_ref, ones_ref, q_ref, *refs):
     if first:
         outs = refs
     else:
@@ -80,8 +83,8 @@
         old_max, old_sum = max_ref[...], sum_ref[...]
     width, queries = q_ref.shape
     heads = SPAN // HD
-    block = block_ref[...]
-    ones = same_head()
+    block = normalised(block_ref[...], gain_ref[...]) if raw else block_ref[...]
+    ones = ones_ref[...]
     zeros = jnp.zeros((HD, queries), BF16)
     held = {}
     maxima, sums = [], []
@@ -173,7 +176,7 @@
     ).astype(BF16)
 
 
-def call(body, outs, operands, flops, exps):
+def call(body, outs, operands, flops, exps=0):
     moved = sum(a.size * a.dtype.itemsize for a in (*operands, *outs))
     return pl.pallas_call(
         body,
@@ -197,45 +200,45 @@
     cross = [((1 - h) * count + b, h * count + ahead(b, h)) for h in range(2) for b in range(count)]
     axes = ("head", "blk")
 
-    (normed,) = call(
-        normalise, [jax.ShapeDtypeStruct((rows, width), BF16)], (patches, ln_gain.reshape(1, width)), 0, 0
-    )
-    one = lax.ppermute(normed, axes, straight)
-    two = lax.ppermute(normed, axes, cross)
-    sibling = lax.ppermute(normed, "head", [(0, 1), (1, 0)])
-    (query,) = call(
+    shape = jax.ShapeDtypeStruct
+    tie = lax.optimization_barrier
+    (ones,) = call(same_head_kernel, [shape((SPAN, SPAN), BF16)], (), 10_000_000_000)
+    one = lax.ppermute(patches, axes, straight)
+    sibling = lax.ppermute(patches, "head", [(0, 1), (1, 0)])
+    gain = ln_gain.reshape(1, width)
+    normed, query = call(
         query_kernel,
-        [jax.ShapeDtypeStruct((width, 2 * rows), BF16)],
-        (normed, sibling, w_qkv, qk_gains),
+        [shape((rows, width), BF16), shape((width, 2 * rows), BF16)],
+        (patches, sibling, w_qkv, gain, qk_gains, ones),
         2 * 2 * rows * width * width,
-        0,
     )
     state_shapes = [
-        jax.ShapeDtypeStruct((H, 2 * rows), F32),
-        jax.ShapeDtypeStruct((H, 2 * rows), F32),
-        jax.ShapeDtypeStruct((width, 2 * rows), F32),
+        shape((H, 2 * rows), F32),
+        shape((H, 2 * rows), F32),
+        shape((width, 2 * rows), F32),
     ]
-    last_shapes = [jax.ShapeDtypeStruct((width + 2 * H, rows), F32)] * 2
+    last_shapes = [shape((width + 2 * H, rows), F32)] * 2
     flops = 2 * rows * width * 2 * width + 2 * 2 * rows * 2 * rows * width
-    exps = H * rows * 2 * rows
-
-    def take(block, state, last=False):
+
+    def take(block, state, raw=True, last=False):
         return call(
-            functools.partial(absorb, not state, last),
+            functools.partial(absorb, not state, last, raw),
             last_shapes if last else state_shapes,
-            (block, w_qkv, qk_gains, query, *state),
-            4 * flops,
-            exps,
+            (block, w_qkv, gain, qk_gains, ones, query, *state),
+            1 * flops,
+            H * rows * 2 * rows,
         )
 
-    state = take(normed, ())
+    later, query = tie((patches, query))
+    two = lax.ppermute(later, axes, cross)
+    state, one = tie((take(normed, (), raw=False), one))
     for turn in range(1, count // 2):
-        here, one = one, lax.ppermute(one, axes, straight)
-        state, two = lax.optimization_barrier((take(here, state), two))
-        here = two
+        here_one, here_two = one, two
+        one = lax.ppermute(here_one, axes, straight)
+        state, here_two = tie((take(here_one, state), here_two))
         if turn < count // 2 - 1:
-            two = lax.ppermute(two, axes, straight)
-        state, one = lax.optimization_barrier((take(here, state), one))
+            two = lax.ppermute(here_two, axes, straight)
+        state, one = tie((take(here_two, state), one))
     kept, sent = take(one, state, last=True)
     came = lax.ppermute(sent, "head", [(0, 1), (1, 0)])
     return call(
@@ -243,7 +246,6 @@
         [jax.ShapeDtypeStruct((rows, width), BF16)],
         (kept, came, w_out),
         2 * rows * width * width,
-        0,
     )[0]
 
 

time: 38.4 us -> 33.5 us (0.87)
  local copies, waits for them, and re-layouts: 6.77 us -> 0.02 us
  starting transfers between devices: 8.22 us -> 13.3 us
  waiting for transfers between devices: 7.74 us -> 3.47 us
  Pallas kernels: 15.3 us -> 16.4 us
    unnamed x14 -> x10, local copies, waits for them, and re-layouts: 6.77 us -> 0.02 us
    ppermute x8, starting transfers between devices: 8.15 us -> 13.2 us  [the longest x3 4.89 us: per_device(): one = lax.ppermute(here_one, axes, straight)]
    ppermute x8, waiting for transfers between devices: 5.82 us -> 1.55 us  [the longest x3 1.28 us: per_device(): one = lax.ppermute(here_one, axes, straight)]
    pallas_call x11, Pallas kernels: 15.3 us -> 16.4 us  [call(): pl.pallas_call(body, out_shape=outs, in_specs=[VMEM] * len(operands), out...]
  transfers between devices with their start and end apart: 9 -> 9, of which waited for: 6 -> 3; matrix products, arithmetic and copies ran while one was open for 0% -> 0% of each run, Pallas kernels for 32% -> 40%
where the time goes in v3:
time: 33.5 us; the launch traced here: 33.3 us
  Pallas kernels  16.4 us (49%)
  starting transfers between devices  13.3 us (40%)
  waiting for transfers between devices  3.47 us (10%)
    pallas_call x11, Pallas kernels, call(): pl.pallas_call(body, out_shape=outs, in_specs=[VMEM] * len(operands), out...  16.4 us
    ppermute x3, starting transfers between devices, per_device(): one = lax.ppermute(here_one, axes, straight)  4.89 us
    ppermute x2, starting transfers between devices, per_device(): two = lax.ppermute(here_two, axes, straight)  3.03 us
    ppermute x1, starting transfers between devices, per_device(): one = lax.ppermute(patches, axes, straight)  2.64 us
    ppermute x1, starting transfers between devices, per_device(): two = lax.ppermute(later, axes, cross)  2.11 us
    ppermute x1, waiting for transfers between devices, per_device(): came = lax.ppermute(sent, 'head', [(0, 1), (1, 0)])  1.92 us
    ppermute x3, waiting for transfers between devices, per_device(): one = lax.ppermute(here_one, axes, straight)  1.28 us
  transfers between devices with their start and end apart: 9, of which 3 were waited for; matrix products, arithmetic and copies ran while one was open for 0% of the time, Pallas kernels for 40%

profile of v3, /device:TPU:0, one launch (start us, length us, event | category | flops | bytes accessed | tf_op | source)
XLA Modules:
  0.0 33.3 jit_solution(3692848685154650328)
XLA Ops:
  0.0 0.5 %collective-permute-start = (bf16[128,1024]{1,0:T(8,128)(2,1)}, bf16[128,1024]{1,0:T(8,128)(2,1)S(1)}, u32[]{:S(2)}, u32[]{:S(2)}) collective-permute-start(bf16[128,1024]{1,0:T(8,128)(2,1)} %own_ref.1), channel_id=1, source_target_pairs={{0,8},{8,0},{1,9},{9,1},{2,10},{10,2},{3,11},{11,3},{4,12},{12,4},... | collective-permute-start | bytes 786440 | tf_op jit(solution)/shard_map/ppermute | solution.py:207
  0.5 2.6 %collective-permute-start.1 = (bf16[128,1024]{1,0:T(8,128)(2,1)}, bf16[128,1024]{1,0:T(8,128)(2,1)S(1)}, u32[]{:S(2)}, u32[]{:S(2)}) collective-permute-start(bf16[128,1024]{1,0:T(8,128)(2,1)} %own_ref.1), channel_id=1, source_target_pairs={{0,2},{1,0},{2,4},{3,1},{4,6},{5,3},{6,7},{7,5},{8,9},{9,11},{10,8... | collective-permute-start | bytes 786440 | tf_op jit(solution)/shard_map/ppermute | solution.py:206
  3.3 1.4 %shard_map.56 = (bf16[128,1024]{1,0:T(8,128)(2,1)S(1)}, bf16[1024,256]{1,0:T(8,128)(2,1)S(1)}) custom-call(bf16[128,1024]{1,0:T(8,128)(2,1)S(1)} %copy-done.4, bf16[128,1024]{1,0:T(8,128)(2,1)S(1)} %collective-permute-done.sibling_ref, bf16[1024,3072]{1,0:T(8,128)(2,1)S(1)} %copy-done, f32[1,1024]{1,0:T(1,128)S(1)} %bitcast.1, f32[2,1024]{1,0:T(2,128)S(1)} %copy-done.2, ...), custom_call_target="tpu_custom_call" | custom-call | flops 536870912 | bytes 7745536 | tf_op jit(solution)/shard_map/pallas_call | solution.py:181
  4.6 2.1 %collective-permute-start.2 = (bf16[128,1024]{1,0:T(8,128)(2,1)S(1)}, bf16[128,1024]{1,0:T(8,128)(2,1)S(1)}, u32[]{:S(2)}, u32[]{:S(2)}) collective-permute-start(bf16[128,1024]{1,0:T(8,128)(2,1)S(1)} %copy-done.4), channel_id=1, source_target_pairs={{8,2},{9,0},{10,4},{11,1},{12,6},{13,3},{14,7},{15,5},{0,9},{1,11}... | collective-permute-start | bytes 786440 | tf_op jit(solution)/shard_map/ppermute | solution.py:233
  6.8 1.5 %shard_map.57 = (f32[16,256]{1,0:T(8,128)S(1)}, f32[16,256]{1,0:T(8,128)S(1)}, f32[1024,256]{1,0:T(8,128)S(1)}) custom-call(bf16[128,1024]{1,0:T(8,128)(2,1)S(1)} %get-tuple-element.60.block_ref, bf16[1024,3072]{1,0:T(8,128)(2,1)S(1)} %copy-done, f32[1,1024]{1,0:T(1,128)S(1)} %bitcast.2, f32[2,1024]{1,0:T(2,128)S(1)} %copy-done.2, ...), custom_call_target="tpu_custom_call" | custom-call | flops 671088640 | bytes 8302592 | tf_op jit(solution)/shard_map/pallas_call | solution.py:181
  8.3 0.0 collective-permute-done.1.block_ref
  8.3 1.5 %collective-permute-start.3 = (bf16[128,1024]{1,0:T(8,128)(2,1)S(1)}, bf16[128,1024]{1,0:T(8,128)(2,1)S(1)}, u32[]{:S(2)}, u32[]{:S(2)}) collective-permute-start(bf16[128,1024]{1,0:T(8,128)(2,1)S(1)} %collective-permute-done.1.block_ref), channel_id=1, source_target_pairs={{0,2},{1,0},{2,4},{3,1},{4,6},{5,3},{6,7},{7,5},{8,9},{9,11},{10,8... | collective-permute-start | bytes 786440 | tf_op jit(solution)/shard_map/ppermute | solution.py:237
  9.8 1.7 %shard_map.58 = (f32[16,256]{1,0:T(8,128)S(1)}, f32[16,256]{1,0:T(8,128)S(1)}, f32[1024,256]{1,0:T(8,128)S(1)}) custom-call(bf16[128,1024]{1,0:T(8,128)(2,1)S(1)} %collective-permute-done.1.block_ref, bf16[1024,3072]{1,0:T(8,128)(2,1)S(1)} %copy-done, f32[1,1024]{1,0:T(1,128)S(1)} %bitcast.3, f32[2,1024]{1,0:T(2,128)S(1)} %copy-done.2, ...), custom_call_target="tpu_custom_call" | custom-call | flops 671088640 | bytes 9383936 | tf_op jit(solution)/shard_map/pallas_call | solution.py:181
  11.5 0.3 collective-permute-done.2.block_ref
  11.8 1.4 %collective-permute-start.4 = (bf16[128,1024]{1,0:T(8,128)(2,1)S(1)}, bf16[128,1024]{1,0:T(8,128)(2,1)S(1)}, u32[]{:S(2)}, u32[]{:S(2)}) collective-permute-start(bf16[128,1024]{1,0:T(8,128)(2,1)S(1)} %collective-permute-done.2.block_ref), channel_id=1, source_target_pairs={{0,2},{1,0},{2,4},{3,1},{4,6},{5,3},{6,7},{7,5},{8,9},{9,11},{10,8... | collective-permute-start | bytes 786440 | tf_op jit(solution)/shard_map/ppermute | solution.py:240
  13.2 1.8 %shard_map.59 = (f32[16,256]{1,0:T(8,128)S(1)}, f32[16,256]{1,0:T(8,128)S(1)}, f32[1024,256]{1,0:T(8,128)S(1)}) custom-call(bf16[128,1024]{1,0:T(8,128)(2,1)S(1)} %collective-permute-done.2.block_ref, bf16[1024,3072]{1,0:T(8,128)(2,1)S(1)} %copy-done, f32[1,1024]{1,0:T(1,128)S(1)} %bitcast.4, f32[2,1024]{1,0:T(2,128)S(1)} %copy-done.2, ...), custom_call_target="tpu_custom_call" | custom-call | flops 671088640 | bytes 9383936 | tf_op jit(solution)/shard_map/pallas_call | solution.py:181
  15.0 1.6 %collective-permute-start.5 = (bf16[128,1024]{1,0:T(8,128)(2,1)S(1)}, bf16[128,1024]{1,0:T(8,128)(2,1)S(1)}, u32[]{:S(2)}, u32[]{:S(2)}) collective-permute-start(bf16[128,1024]{1,0:T(8,128)(2,1)S(1)} %collective-permute-done.3.block_ref), channel_id=1, source_target_pairs={{0,2},{1,0},{2,4},{3,1},{4,6},{5,3},{6,7},{7,5},{8,9},{9,11},{10,8... | collective-permute-start | bytes 786440 | tf_op jit(solution)/shard_map/ppermute | solution.py:237
  16.6 1.7 %shard_map.60 = (f32[16,256]{1,0:T(8,128)S(1)}, f32[16,256]{1,0:T(8,128)S(1)}, f32[1024,256]{1,0:T(8,128)S(1)}) custom-call(bf16[128,1024]{1,0:T(8,128)(2,1)S(1)} %collective-permute-done.3.block_ref, bf16[1024,3072]{1,0:T(8,128)(2,1)S(1)} %copy-done, f32[1,1024]{1,0:T(1,128)S(1)} %bitcast.5, f32[2,1024]{1,0:T(2,128)S(1)} %copy-done.2, ...), custom_call_target="tpu_custom_call" | custom-call | flops 671088640 | bytes 9383936 | tf_op jit(solution)/shard_map/pallas_call | solution.py:181
  18.4 1.6 %collective-permute-start.6 = (bf16[128,1024]{1,0:T(8,128)(2,1)S(1)}, bf16[128,1024]{1,0:T(8,128)(2,1)S(1)}, u32[]{:S(2)}, u32[]{:S(2)}) collective-permute-start(bf16[128,1024]{1,0:T(8,128)(2,1)S(1)} %collective-permute-done.4.block_ref), channel_id=1, source_target_pairs={{0,2},{1,0},{2,4},{3,1},{4,6},{5,3},{6,7},{7,5},{8,9},{9,11},{10,8... | collective-permute-start | bytes 786440 | tf_op jit(solution)/shard_map/ppermute | solution.py:240
  20.0 1.8 %shard_map.61 = (f32[16,256]{1,0:T(8,128)S(1)}, f32[16,256]{1,0:T(8,128)S(1)}, f32[1024,256]{1,0:T(8,128)S(1)}) custom-call(bf16[128,1024]{1,0:T(8,128)(2,1)S(1)} %collective-permute-done.4.block_ref, bf16[1024,3072]{1,0:T(8,128)(2,1)S(1)} %copy-done, f32[1,1024]{1,0:T(1,128)S(1)} %bitcast.6, f32[2,1024]{1,0:T(2,128)S(1)} %copy-done.2, ...), custom_call_target="tpu_custom_call" | custom-call | flops 671088640 | bytes 9383936 | tf_op jit(solution)/shard_map/pallas_call | solution.py:181
  21.8 1.8 %collective-permute-start.7 = (bf16[128,1024]{1,0:T(8,128)(2,1)S(1)}, bf16[128,1024]{1,0:T(8,128)(2,1)S(1)}, u32[]{:S(2)}, u32[]{:S(2)}) collective-permute-start(bf16[128,1024]{1,0:T(8,128)(2,1)S(1)} %collective-permute-done.5.block_ref), channel_id=1, source_target_pairs={{0,2},{1,0},{2,4},{3,1},{4,6},{5,3},{6,7},{7,5},{8,9},{9,11},{10,8... | collective-permute-start | bytes 786440 | tf_op jit(solution)/shard_map/ppermute | solution.py:237
  23.5 1.7 %shard_map.62 = (f32[16,256]{1,0:T(8,128)S(1)}, f32[16,256]{1,0:T(8,128)S(1)}, f32[1024,256]{1,0:T(8,128)S(1)}) custom-call(bf16[128,1024]{1,0:T(8,128)(2,1)S(1)} %collective-permute-done.5.block_ref, bf16[1024,3072]{1,0:T(8,128)(2,1)S(1)} %copy-done, f32[1,1024]{1,0:T(1,128)S(1)} %bitcast.7, f32[2,1024]{1,0:T(2,128)S(1)} %copy-done.2, ...), custom_call_target="tpu_custom_call" | custom-call | flops 671088640 | bytes 9383936 | tf_op jit(solution)/shard_map/pallas_call | solution.py:181
  25.3 0.0 copy-start.1
  25.3 1.8 %shard_map.63 = (f32[16,256]{1,0:T(8,128)S(1)}, f32[16,256]{1,0:T(8,128)S(1)}, f32[1024,256]{1,0:T(8,128)S(1)}) custom-call(bf16[128,1024]{1,0:T(8,128)(2,1)S(1)} %collective-permute-done.6.block_ref, bf16[1024,3072]{1,0:T(8,128)(2,1)S(1)} %copy-done, f32[1,1024]{1,0:T(1,128)S(1)} %bitcast.8, f32[2,1024]{1,0:T(2,128)S(1)} %copy-done.2, ...), custom_call_target="tpu_custom_call" | custom-call | flops 671088640 | bytes 9383936 | tf_op jit(solution)/shard_map/pallas_call | solution.py:181
  27.1 1.3 %collective-permute-done.7.block_ref = bf16[128,1024]{1,0:T(8,128)(2,1)S(1)} collective-permute-done((bf16[128,1024]{1,0:T(8,128)(2,1)S(1)}, bf16[128,1024]{1,0:T(8,128)(2,1)S(1)}, u32[]{:S(2)}, u32[]{:S(2)}) %collective-permute-start.7) | collective-permute-done | bytes 262176 | tf_op jit(solution)/shard_map/ppermute | solution.py:237
  28.4 1.8 %shard_map.64 = (f32[1056,128]{1,0:T(8,128)S(1)}, f32[1056,128]{1,0:T(8,128)S(1)}) custom-call(bf16[128,1024]{1,0:T(8,128)(2,1)S(1)} %collective-permute-done.7.block_ref, bf16[1024,3072]{1,0:T(8,128)(2,1)S(1)} %copy-done, f32[1,1024]{1,0:T(1,128)S(1)} %bitcast.9, f32[2,1024]{1,0:T(2,128)S(1)} %copy-done.2, bf16[256,256]{1,0:T(8,128)(2,1)S(1)} %shard_map.55.ones_ref, ...), custom_call_target="tpu_custom_call" | custom-call | flops 671088640 | bytes 9383936 | tf_op jit(solution)/shard_map/pallas_call | solution.py:181
  30.1 0.1 collective-permute-start.8
  30.2 1.9 %collective-permute-done.8.came_ref = f32[1056,128]{1,0:T(8,128)S(1)} collective-permute-done((f32[1056,128]{1,0:T(8,128)S(1)}, f32[1056,128]{1,0:T(8,128)S(1)}, u32[]{:S(2)}, u32[]{:S(2)}) %collective-permute-start.8) | collective-permute-done | bytes 540704 | tf_op jit(solution)/shard_map/ppermute | solution.py:243
  32.1 1.2 %shard_map.65 = bf16[128,1024]{1,0:T(8,128)(2,1)} custom-call(f32[1056,128]{1,0:T(8,128)S(1)} %get-tuple-element.113.kept_ref, f32[1056,128]{1,0:T(8,128)S(1)} %collective-permute-done.8.came_ref, bf16[1024,1024]{1,0:T(8,128)(2,1)S(1)} %copy-done.1), custom_call_target="tpu_custom_call" | custom-call | flops 268435456 | bytes 3440640 | tf_op jit(solution)/shard_map/pallas_call | solution.py:181
  (15 shorter events, 0.1 us)
Async XLA Ops:
  0.0 3.2 %copy-start.4 = (bf16[128,1024]{1,0:T(8,128)(2,1)S(1)}, bf16[128,1024]{1,0:T(8,128)(2,1)}, u32[]{:S(2)}) copy-start(bf16[128,1024]{1,0:T(8,128)(2,1)} %own_ref.1) | copy-start | bytes 786436
  0.0 3.2 %copy-start.2 = (f32[2,1024]{1,0:T(2,128)S(1)}, f32[2,1024]{1,0:T(2,128)}, u32[]{:S(2)}) copy-start(f32[2,1024]{1,0:T(2,128)} %gains_ref.17) | copy-start | bytes 24580
  0.0 3.2 %copy-start = (bf16[1024,3072]{1,0:T(8,128)(2,1)S(1)}, bf16[1024,3072]{1,0:T(8,128)(2,1)}, u32[]{:S(2)}) copy-start(bf16[1024,3072]{1,0:T(8,128)(2,1)} %w_ref.18) | copy-start | bytes 18874372
  0.0 3.2 %copy-start.3 = (f32[1024]{0:T(1024)S(1)}, f32[1024]{0:T(1024)}, u32[]{:S(2)}) copy-start(f32[1024]{0:T(1024)} %param.6) | copy-start | bytes 12292
  0.0 3.2 %collective-permute-start = (bf16[128,1024]{1,0:T(8,128)(2,1)}, bf16[128,1024]{1,0:T(8,128)(2,1)S(1)}, u32[]{:S(2)}, u32[]{:S(2)}) collective-permute-start(bf16[128,1024]{1,0:T(8,128)(2,1)} %own_ref.1), channel_id=1, source_target_pairs={{0,8},{8,0},{1,9},{9,1},{2,10},{10,2},{3,11},{11,3},{4,12},{12,4},... | collective-permute-start | bytes 786440 | tf_op jit(solution)/shard_map/ppermute | solution.py:207
  0.5 7.7 %collective-permute-start.1 = (bf16[128,1024]{1,0:T(8,128)(2,1)}, bf16[128,1024]{1,0:T(8,128)(2,1)S(1)}, u32[]{:S(2)}, u32[]{:S(2)}) collective-permute-start(bf16[128,1024]{1,0:T(8,128)(2,1)} %own_ref.1), channel_id=1, source_target_pairs={{0,2},{1,0},{2,4},{3,1},{4,6},{5,3},{6,7},{7,5},{8,9},{9,11},{10,8... | collective-permute-start | bytes 786440 | tf_op jit(solution)/shard_map/ppermute | solution.py:206
  4.6 7.1 %collective-permute-start.2 = (bf16[128,1024]{1,0:T(8,128)(2,1)S(1)}, bf16[128,1024]{1,0:T(8,128)(2,1)S(1)}, u32[]{:S(2)}, u32[]{:S(2)}) collective-permute-start(bf16[128,1024]{1,0:T(8,128)(2,1)S(1)} %copy-done.4), channel_id=1, source_target_pairs={{8,2},{9,0},{10,4},{11,1},{12,6},{13,3},{14,7},{15,5},{0,9},{1,11}... | collective-permute-start | bytes 786440 | tf_op jit(solution)/shard_map/ppermute | solution.py:233
  8.3 6.7 %collective-permute-start.3 = (bf16[128,1024]{1,0:T(8,128)(2,1)S(1)}, bf16[128,1024]{1,0:T(8,128)(2,1)S(1)}, u32[]{:S(2)}, u32[]{:S(2)}) collective-permute-start(bf16[128,1024]{1,0:T(8,128)(2,1)S(1)} %collective-permute-done.1.block_ref), channel_id=1, source_target_pairs={{0,2},{1,0},{2,4},{3,1},{4,6},{5,3},{6,7},{7,5},{8,9},{9,11},{10,8... | collective-permute-start | bytes 786440 | tf_op jit(solution)/shard_map/ppermute | solution.py:237
  11.8 6.6 %collective-permute-start.4 = (bf16[128,1024]{1,0:T(8,128)(2,1)S(1)}, bf16[128,1024]{1,0:T(8,128)(2,1)S(1)}, u32[]{:S(2)}, u32[]{:S(2)}) collective-permute-start(bf16[128,1024]{1,0:T(8,128)(2,1)S(1)} %collective-permute-done.2.block_ref), channel_id=1, source_target_pairs={{0,2},{1,0},{2,4},{3,1},{4,6},{5,3},{6,7},{7,5},{8,9},{9,11},{10,8... | collective-permute-start | bytes 786440 | tf_op jit(solution)/shard_map/ppermute | solution.py:240
  15.0 6.8 %collective-permute-start.5 = (bf16[128,1024]{1,0:T(8,128)(2,1)S(1)}, bf16[128,1024]{1,0:T(8,128)(2,1)S(1)}, u32[]{:S(2)}, u32[]{:S(2)}) collective-permute-start(bf16[128,1024]{1,0:T(8,128)(2,1)S(1)} %collective-permute-done.3.block_ref), channel_id=1, source_target_pairs={{0,2},{1,0},{2,4},{3,1},{4,6},{5,3},{6,7},{7,5},{8,9},{9,11},{10,8... | collective-permute-start | bytes 786440 | tf_op jit(solution)/shard_map/ppermute | solution.py:237
  18.4 6.9 %collective-permute-start.6 = (bf16[128,1024]{1,0:T(8,128)(2,1)S(1)}, bf16[128,1024]{1,0:T(8,128)(2,1)S(1)}, u32[]{:S(2)}, u32[]{:S(2)}) collective-permute-start(bf16[128,1024]{1,0:T(8,128)(2,1)S(1)} %collective-permute-done.4.block_ref), channel_id=1, source_target_pairs={{0,2},{1,0},{2,4},{3,1},{4,6},{5,3},{6,7},{7,5},{8,9},{9,11},{10,8... | collective-permute-start | bytes 786440 | tf_op jit(solution)/shard_map/ppermute | solution.py:240
  21.8 6.6 %collective-permute-start.7 = (bf16[128,1024]{1,0:T(8,128)(2,1)S(1)}, bf16[128,1024]{1,0:T(8,128)(2,1)S(1)}, u32[]{:S(2)}, u32[]{:S(2)}) collective-permute-start(bf16[128,1024]{1,0:T(8,128)(2,1)S(1)} %collective-permute-done.5.block_ref), channel_id=1, source_target_pairs={{0,2},{1,0},{2,4},{3,1},{4,6},{5,3},{6,7},{7,5},{8,9},{9,11},{10,8... | collective-permute-start | bytes 786440 | tf_op jit(solution)/shard_map/ppermute | solution.py:237
  25.3 6.8 %copy-start.1 = (bf16[1024,1024]{1,0:T(8,128)(2,1)S(1)}, bf16[1024,1024]{1,0:T(8,128)(2,1)}, u32[]{:S(2)}) copy-start(bf16[1024,1024]{1,0:T(8,128)(2,1)} %w_ref.19) | copy-start | bytes 6291460
  30.1 2.0 %collective-permute-start.8 = (f32[1056,128]{1,0:T(8,128)S(1)}, f32[1056,128]{1,0:T(8,128)S(1)}, u32[]{:S(2)}, u32[]{:S(2)}) collective-permute-start(f32[1056,128]{1,0:T(8,128)S(1)} %get-tuple-element.114), channel_id=1, source_target_pairs={{0,8},{8,0},{1,9},{9,1},{2,10},{10,2},{3,11},{11,3},{4,12},{12,4},... | collective-permute-start | bytes 1622024 | tf_op jit(solution)/shard_map/ppermute | solution.py:243

commit v4 on v3

--- a/solution.py
+++ b/solution.py
@@ -1,4 +1,5 @@
 import functools
+import math
 
 import jax
 import jax.numpy as jnp
@@ -11,6 +12,7 @@
 HD = 64
 PAIR = 2 * HD
 SPAN = 4 * HD
+SCALE = HD**-0.5 * math.log2(math.e)
 F32 = jnp.float32
 BF16 = jnp.bfloat16
 VMEM = pl.BlockSpec(memory_space=pltpu.VMEM)
@@ -71,8 +73,8 @@
         for span in spans
     ]
     for i, span, columns in projected:
-        query = head_norm(columns, gains_ref[0:1, span], ones).astype(F32) * (HD**-0.5)
-        query_ref[span, i * rows : (i + 1) * rows] = query.T.astype(BF16)
+        query = head_norm(columns, gains_ref[0:1, span] * SCALE, ones)
+        query_ref[span, i * rows : (i + 1) * rows] = query.astype(F32).T.astype(BF16)
 
 
 def absorb(first, last, raw, block_ref, w_ref, gain_ref, gains_ref, ones_ref, q_ref, *refs):
@@ -82,10 +84,12 @@
         (max_ref, sum_ref, acc_ref), outs = refs[:3], refs[3:]
         old_max, old_sum = max_ref[...], sum_ref[...]
     width, queries = q_ref.shape
+    half = queries // 2
     heads = SPAN // HD
     block = normalised(block_ref[...], gain_ref[...]) if raw else block_ref[...]
     ones = ones_ref[...]
     zeros = jnp.zeros((HD, queries), BF16)
+    counts = jnp.ones((16, block.shape[0]), BF16)
     held = {}
     maxima, sums = [], []
 
@@ -116,13 +120,9 @@
         if not first:
             before = old_max[i * heads : (i + 1) * heads]
             top = jnp.maximum(top, before)
-            held["shrink", i] = jnp.exp(before - top)
-        exponents = [jnp.exp(s - top[j : j + 1]) for j, s in enumerate(scores)]
-        total = jnp.concatenate([jnp.sum(e, axis=0, keepdims=True) for e in exponents], axis=0)
-        if not first:
-            total = total + old_sum[i * heads : (i + 1) * heads] * held["shrink", i]
+            held["shrink", i] = jnp.exp2(before - top)
+        exponents = [jnp.exp2(s - top[j : j + 1]) for j, s in enumerate(scores)]
         maxima.append(top)
-        sums.append(total)
         for j, exponent in enumerate(exponents):
             held["weight", i, j] = exponent.astype(BF16)
 
@@ -131,19 +131,23 @@
         for j in range(heads):
             at = i * SPAN + j * HD
             added = jnp.dot(
-                values[j * HD : (j + 1) * HD],
+                jnp.concatenate([values[j * HD : (j + 1) * HD], counts], axis=0),
                 held.pop(("weight", i, j)),
                 preferred_element_type=F32,
             )
+            total, added = added[HD : HD + 1], added[:HD]
             if not first:
-                added = added + acc_ref[at : at + HD, :] * held["shrink", i][j : j + 1]
+                shrink = held["shrink", i][j : j + 1]
+                total = total + old_sum[i * heads + j : i * heads + j + 1] * shrink
+                added = added + acc_ref[at : at + HD, :] * shrink
+            sums.append(total)
             if last:
-                for ref, part in zip(outs, halves):
-                    ref[at : at + HD, :] = added[:, part]
+                for ref, part in zip(outs[:2], halves):
+                    ref[at : at + HD, :] = added[:, part].astype(ref.dtype)
             else:
                 outs[2][at : at + HD, :] = added
 
-    halves = (slice(0, queries // 2), slice(queries // 2, queries))
+    halves = (slice(0, half), slice(half, queries))
     stages = (project, norm, score, soften, weigh)
     for turn in range(width // SPAN + len(stages) - 1):
         for behind, stage in enumerate(stages):
@@ -151,29 +155,31 @@
                 stage(turn - behind)
     top, total = jnp.concatenate(maxima, axis=0), jnp.concatenate(sums, axis=0)
     if last:
-        for ref, part in zip(outs, halves):
-            ref[width : width + H, :] = top[:, part]
-            ref[width + H : width + 2 * H, :] = total[:, part]
+        for ref, part in zip(outs[2:], halves):
+            ref[:H, :] = top[:, part]
+            ref[H:, :] = total[:, part]
     else:
         outs[0][...] = top
         outs[1][...] = total
 
 
-def finish_kernel(kept_ref, came_ref, w_ref, out_ref):
-    width = H * HD
-    heads = []
-    for h in range(H):
-        at = slice(h * HD, (h + 1) * HD)
-        m, s = slice(width + h, width + h + 1), slice(width + H + h, width + H + h + 1)
-        top = jnp.maximum(kept_ref[m, :], came_ref[m, :])
-        mine, theirs = jnp.exp(kept_ref[m, :] - top), jnp.exp(came_ref[m, :] - top)
-        total = kept_ref[s, :] * mine + came_ref[s, :] * theirs
-        summed = kept_ref[at, :] * mine + came_ref[at, :] * theirs
-        heads.append((summed / total).astype(BF16))
-    attended = jnp.concatenate(heads, axis=0)
-    out_ref[...] = lax.dot_general(
-        attended, w_ref[...], (((0,), (0,)), ((), ())), preferred_element_type=F32
-    ).astype(BF16)
+def finish_kernel(mine_ref, theirs_ref, my_state_ref, their_state_ref, w_ref, out_ref):
+    width = mine_ref.shape[0]
+    top = jnp.maximum(my_state_ref[:H, :], their_state_ref[:H, :])
+    mine = jnp.exp2(my_state_ref[:H, :] - top)
+    theirs = jnp.exp2(their_state_ref[:H, :] - top)
+    total = my_state_ref[H:, :] * mine + their_state_ref[H:, :] * theirs
+    mine, theirs = mine / total, theirs / total
+    spans = []
+    for at in range(0, width, SPAN):
+        merged = [
+            mine_ref[h * HD : (h + 1) * HD, :] * mine[h : h + 1]
+            + theirs_ref[h * HD : (h + 1) * HD, :].astype(F32) * theirs[h : h + 1]
+            for h in range(at // HD, (at + SPAN) // HD)
+        ]
+        spans.append(jnp.concatenate(merged, axis=0).T.astype(BF16))
+    attended = jnp.concatenate(spans, axis=1)
+    out_ref[...] = jnp.dot(attended, w_ref[...], preferred_element_type=F32).astype(BF16)
 
 
 def call(body, outs, operands, flops, exps=0):
@@ -193,18 +199,22 @@
     count = lax.axis_size("blk")
     place = {index: i for i, index in enumerate(order)}
 
-    def ahead(index, head):
-        return order[(place[index] + (1 if head == 0 else -1)) % count]
-
-    straight = [(h * count + b, h * count + ahead(b, h)) for h in range(2) for b in range(count)]
-    cross = [((1 - h) * count + b, h * count + ahead(b, h)) for h in range(2) for b in range(count)]
+    def onward(right_core):
+        return [
+            (h * count + b, (1 - h) * count + order[(place[b] + step) % count])
+            for b in range(count)
+            for h, step in ((right_core, 1), (1 - right_core, -1))
+        ]
+
+    hops = (onward(0), onward(1))
     axes = ("head", "blk")
+    swap = [(0, 1), (1, 0)]
 
     shape = jax.ShapeDtypeStruct
     tie = lax.optimization_barrier
     (ones,) = call(same_head_kernel, [shape((SPAN, SPAN), BF16)], (), 10_000_000_000)
-    one = lax.ppermute(patches, axes, straight)
-    sibling = lax.ppermute(patches, "head", [(0, 1), (1, 0)])
+    one = lax.ppermute(patches, axes, hops[0])
+    sibling = lax.ppermute(patches, "head", swap)
     gain = ln_gain.reshape(1, width)
     normed, query = call(
         query_kernel,
@@ -212,12 +222,19 @@
         (patches, sibling, w_qkv, gain, qk_gains, ones),
         2 * 2 * rows * width * width,
     )
+    later, query = tie((patches, query))
+    two = lax.ppermute(later, axes, hops[1])
     state_shapes = [
         shape((H, 2 * rows), F32),
         shape((H, 2 * rows), F32),
         shape((width, 2 * rows), F32),
     ]
-    last_shapes = [shape((width + 2 * H, rows), F32)] * 2
+    last_shapes = [
+        shape((width, rows), F32),
+        shape((width, rows), BF16),
+        shape((2 * H, rows), F32),
+        shape((2 * H, rows), F32),
+    ]
     flops = 2 * rows * width * 2 * width + 2 * 2 * rows * 2 * rows * width
 
     def take(block, state, raw=True, last=False):
@@ -229,22 +246,21 @@
             H * rows * 2 * rows,
         )
 
-    later, query = tie((patches, query))
-    two = lax.ppermute(later, axes, cross)
     state, one = tie((take(normed, (), raw=False), one))
     for turn in range(1, count // 2):
         here_one, here_two = one, two
-        one = lax.ppermute(here_one, axes, straight)
+        one = lax.ppermute(here_one, axes, hops[turn % 2])
         state, here_two = tie((take(here_one, state), here_two))
         if turn < count // 2 - 1:
-            two = lax.ppermute(here_two, axes, straight)
+            two = lax.ppermute(here_two, axes, hops[(turn + 1) % 2])
         state, one = tie((take(here_two, state), one))
-    kept, sent = take(one, state, last=True)
-    came = lax.ppermute(sent, "head", [(0, 1), (1, 0)])
+    mine, theirs, my_state, their_state = take(one, state, last=True)
+    theirs = lax.ppermute(theirs, "head", swap)
+    their_state = lax.ppermute(their_state, "head", swap)
     return call(
         finish_kernel,
-        [jax.ShapeDtypeStruct((rows, width), BF16)],
-        (kept, came, w_out),
+        [shape((rows, width), BF16)],
+        (mine, theirs, my_state, their_state, w_out),
         2 * rows * width * width,
     )[0]
 

time: 33.5 us -> 32.2 us (0.961)
  waiting for transfers between devices: 3.47 us -> 2.37 us
    ppermute x9 -> x10, waiting for transfers between devices: 3.47 us -> 2.37 us  [the longest x1 1.11 us: per_device(): their_state = lax.ppermute(their_state, 'head', swap)]
    ppermute x9 -> x10, starting transfers between devices: 13.3 us -> 13.4 us  [the longest x3 4.79 us: per_device(): one = lax.ppermute(here_one, axes, hops[turn % 2])]
  transfers between devices with their start and end apart: 9 -> 10, of which waited for: 3 -> 3; matrix products, arithmetic and copies ran while one was open for 0% -> 0% of each run, Pallas kernels for 40% -> 41%
where the time goes in v4:
time: 32.2 us; the launch traced here: 32.1 us
  Pallas kernels  16.1 us (50%)
  starting transfers between devices  13.4 us (42%)
  waiting for transfers between devices  2.37 us (7%)
    pallas_call x11, Pallas kernels, call(): pl.pallas_call(body, out_shape=outs, in_specs=[VMEM] * len(operands), out...  16.1 us
    ppermute x3, starting transfers between devices, per_device(): one = lax.ppermute(here_one, axes, hops[turn % 2])  4.79 us
    ppermute x1, starting transfers between devices, per_device(): one = lax.ppermute(patches, axes, hops[0])  2.69 us
    ppermute x2, starting transfers between devices, per_device(): two = lax.ppermute(here_two, axes, hops[(turn + 1) % 2])  2.65 us
    ppermute x1, starting transfers between devices, per_device(): two = lax.ppermute(later, axes, hops[1])  2.06 us
    ppermute x1, waiting for transfers between devices, per_device(): their_state = lax.ppermute(their_state, 'head', swap)  1.11 us
    ppermute x3, waiting for transfers between devices, per_device(): one = lax.ppermute(here_one, axes, hops[turn % 2])  0.94 us
  transfers between devices with their start and end apart: 10, of which 3 were waited for; matrix products, arithmetic and copies ran while one was open for 0% of the time, Pallas kernels for 41%

profile of v4, /device:TPU:0, one launch (start us, length us, event | category | flops | bytes accessed | tf_op | source)
XLA Modules:
  0.0 32.1 jit_solution(1695048407733318223)
XLA Ops:
  0.0 0.5 %collective-permute-start = (bf16[128,1024]{1,0:T(8,128)(2,1)}, bf16[128,1024]{1,0:T(8,128)(2,1)S(1)}, u32[]{:S(2)}, u32[]{:S(2)}) collective-permute-start(bf16[128,1024]{1,0:T(8,128)(2,1)} %own_ref.1), channel_id=1, source_target_pairs={{0,8},{8,0},{1,9},{9,1},{2,10},{10,2},{3,11},{11,3},{4,12},{12,4},... | collective-permute-start | bytes 786440 | tf_op jit(solution)/shard_map/ppermute | solution.py:217
  0.5 2.7 %collective-permute-start.1 = (bf16[128,1024]{1,0:T(8,128)(2,1)}, bf16[128,1024]{1,0:T(8,128)(2,1)S(1)}, u32[]{:S(2)}, u32[]{:S(2)}) collective-permute-start(bf16[128,1024]{1,0:T(8,128)(2,1)} %own_ref.1), channel_id=1, source_target_pairs={{0,10},{8,1},{1,8},{9,3},{2,12},{10,0},{3,9},{11,5},{4,14},{12,2},... | collective-permute-start | bytes 786440 | tf_op jit(solution)/shard_map/ppermute | solution.py:216
  3.3 1.3 %shard_map.56 = (bf16[128,1024]{1,0:T(8,128)(2,1)S(1)}, bf16[1024,256]{1,0:T(8,128)(2,1)S(1)}) custom-call(bf16[128,1024]{1,0:T(8,128)(2,1)S(1)} %copy-done.4, bf16[128,1024]{1,0:T(8,128)(2,1)S(1)} %collective-permute-done.sibling_ref, bf16[1024,3072]{1,0:T(8,128)(2,1)S(1)} %copy-done, f32[1,1024]{1,0:T(1,128)S(1)} %bitcast.1, f32[2,1024]{1,0:T(2,128)S(1)} %copy-done.2, ...), custom_call_target="tpu_custom_call" | custom-call | flops 536870912 | bytes 7745536 | tf_op jit(solution)/shard_map/pallas_call | solution.py:187
  4.6 2.1 %collective-permute-start.2 = (bf16[128,1024]{1,0:T(8,128)(2,1)S(1)}, bf16[128,1024]{1,0:T(8,128)(2,1)S(1)}, u32[]{:S(2)}, u32[]{:S(2)}) collective-permute-start(bf16[128,1024]{1,0:T(8,128)(2,1)S(1)} %copy-done.4), channel_id=1, source_target_pairs={{8,2},{0,9},{9,0},{1,11},{10,4},{2,8},{11,1},{3,13},{12,6},{4,10},... | collective-permute-start | bytes 786440 | tf_op jit(solution)/shard_map/ppermute | solution.py:226
  6.7 1.5 %shard_map.57 = (f32[16,256]{1,0:T(8,128)S(1)}, f32[16,256]{1,0:T(8,128)S(1)}, f32[1024,256]{1,0:T(8,128)S(1)}) custom-call(bf16[128,1024]{1,0:T(8,128)(2,1)S(1)} %get-tuple-element.62.block_ref, bf16[1024,3072]{1,0:T(8,128)(2,1)S(1)} %copy-done, f32[1,1024]{1,0:T(1,128)S(1)} %bitcast.2, f32[2,1024]{1,0:T(2,128)S(1)} %copy-done.2, ...), custom_call_target="tpu_custom_call" | custom-call | flops 671088640 | bytes 8302592 | tf_op jit(solution)/shard_map/pallas_call | solution.py:187
  8.2 1.0 %collective-permute-start.3 = (bf16[128,1024]{1,0:T(8,128)(2,1)S(1)}, bf16[128,1024]{1,0:T(8,128)(2,1)S(1)}, u32[]{:S(2)}, u32[]{:S(2)}) collective-permute-start(bf16[128,1024]{1,0:T(8,128)(2,1)S(1)} %collective-permute-done.1.block_ref), channel_id=1, source_target_pairs={{8,2},{0,9},{9,0},{1,11},{10,4},{2,8},{11,1},{3,13},{12,6},{4,10},... | collective-permute-start | bytes 786440 | tf_op jit(solution)/shard_map/ppermute | solution.py:252
  9.2 1.7 %shard_map.58 = (f32[16,256]{1,0:T(8,128)S(1)}, f32[16,256]{1,0:T(8,128)S(1)}, f32[1024,256]{1,0:T(8,128)S(1)}) custom-call(bf16[128,1024]{1,0:T(8,128)(2,1)S(1)} %collective-permute-done.1.block_ref, bf16[1024,3072]{1,0:T(8,128)(2,1)S(1)} %copy-done, f32[1,1024]{1,0:T(1,128)S(1)} %bitcast.3, f32[2,1024]{1,0:T(2,128)S(1)} %copy-done.2, ...), custom_call_target="tpu_custom_call" | custom-call | flops 671088640 | bytes 9383936 | tf_op jit(solution)/shard_map/pallas_call | solution.py:187
  10.9 2.1 %collective-permute-start.4 = (bf16[128,1024]{1,0:T(8,128)(2,1)S(1)}, bf16[128,1024]{1,0:T(8,128)(2,1)S(1)}, u32[]{:S(2)}, u32[]{:S(2)}) collective-permute-start(bf16[128,1024]{1,0:T(8,128)(2,1)S(1)} %collective-permute-done.2.block_ref), channel_id=1, source_target_pairs={{0,10},{8,1},{1,8},{9,3},{2,12},{10,0},{3,9},{11,5},{4,14},{12,2},... | collective-permute-start | bytes 786440 | tf_op jit(solution)/shard_map/ppermute | solution.py:255
  13.0 1.7 %shard_map.59 = (f32[16,256]{1,0:T(8,128)S(1)}, f32[16,256]{1,0:T(8,128)S(1)}, f32[1024,256]{1,0:T(8,128)S(1)}) custom-call(bf16[128,1024]{1,0:T(8,128)(2,1)S(1)} %collective-permute-done.2.block_ref, bf16[1024,3072]{1,0:T(8,128)(2,1)S(1)} %copy-done, f32[1,1024]{1,0:T(1,128)S(1)} %bitcast.4, f32[2,1024]{1,0:T(2,128)S(1)} %copy-done.2, ...), custom_call_target="tpu_custom_call" | custom-call | flops 671088640 | bytes 9383936 | tf_op jit(solution)/shard_map/pallas_call | solution.py:187
  14.7 1.9 %collective-permute-start.5 = (bf16[128,1024]{1,0:T(8,128)(2,1)S(1)}, bf16[128,1024]{1,0:T(8,128)(2,1)S(1)}, u32[]{:S(2)}, u32[]{:S(2)}) collective-permute-start(bf16[128,1024]{1,0:T(8,128)(2,1)S(1)} %collective-permute-done.3.block_ref), channel_id=1, source_target_pairs={{0,10},{8,1},{1,8},{9,3},{2,12},{10,0},{3,9},{11,5},{4,14},{12,2},... | collective-permute-start | bytes 786440 | tf_op jit(solution)/shard_map/ppermute | solution.py:252
  16.6 1.7 %shard_map.60 = (f32[16,256]{1,0:T(8,128)S(1)}, f32[16,256]{1,0:T(8,128)S(1)}, f32[1024,256]{1,0:T(8,128)S(1)}) custom-call(bf16[128,1024]{1,0:T(8,128)(2,1)S(1)} %collective-permute-done.3.block_ref, bf16[1024,3072]{1,0:T(8,128)(2,1)S(1)} %copy-done, f32[1,1024]{1,0:T(1,128)S(1)} %bitcast.5, f32[2,1024]{1,0:T(2,128)S(1)} %copy-done.2, ...), custom_call_target="tpu_custom_call" | custom-call | flops 671088640 | bytes 9383936 | tf_op jit(solution)/shard_map/pallas_call | solution.py:187
  18.3 0.6 %collective-permute-start.6 = (bf16[128,1024]{1,0:T(8,128)(2,1)S(1)}, bf16[128,1024]{1,0:T(8,128)(2,1)S(1)}, u32[]{:S(2)}, u32[]{:S(2)}) collective-permute-start(bf16[128,1024]{1,0:T(8,128)(2,1)S(1)} %collective-permute-done.4.block_ref), channel_id=1, source_target_pairs={{8,2},{0,9},{9,0},{1,11},{10,4},{2,8},{11,1},{3,13},{12,6},{4,10},... | collective-permute-start | bytes 786440 | tf_op jit(solution)/shard_map/ppermute | solution.py:255
  18.9 1.7 %shard_map.61 = (f32[16,256]{1,0:T(8,128)S(1)}, f32[16,256]{1,0:T(8,128)S(1)}, f32[1024,256]{1,0:T(8,128)S(1)}) custom-call(bf16[128,1024]{1,0:T(8,128)(2,1)S(1)} %collective-permute-done.4.block_ref, bf16[1024,3072]{1,0:T(8,128)(2,1)S(1)} %copy-done, f32[1,1024]{1,0:T(1,128)S(1)} %bitcast.6, f32[2,1024]{1,0:T(2,128)S(1)} %copy-done.2, ...), custom_call_target="tpu_custom_call" | custom-call | flops 671088640 | bytes 9383936 | tf_op jit(solution)/shard_map/pallas_call | solution.py:187
  20.6 0.0 collective-permute-done.5.block_ref
  20.7 1.8 %collective-permute-start.7 = (bf16[128,1024]{1,0:T(8,128)(2,1)S(1)}, bf16[128,1024]{1,0:T(8,128)(2,1)S(1)}, u32[]{:S(2)}, u32[]{:S(2)}) collective-permute-start(bf16[128,1024]{1,0:T(8,128)(2,1)S(1)} %collective-permute-done.5.block_ref), channel_id=1, source_target_pairs={{8,2},{0,9},{9,0},{1,11},{10,4},{2,8},{11,1},{3,13},{12,6},{4,10},... | collective-permute-start | bytes 786440 | tf_op jit(solution)/shard_map/ppermute | solution.py:252
  22.5 1.7 %shard_map.62 = (f32[16,256]{1,0:T(8,128)S(1)}, f32[16,256]{1,0:T(8,128)S(1)}, f32[1024,256]{1,0:T(8,128)S(1)}) custom-call(bf16[128,1024]{1,0:T(8,128)(2,1)S(1)} %collective-permute-done.5.block_ref, bf16[1024,3072]{1,0:T(8,128)(2,1)S(1)} %copy-done, f32[1,1024]{1,0:T(1,128)S(1)} %bitcast.7, f32[2,1024]{1,0:T(2,128)S(1)} %copy-done.2, ...), custom_call_target="tpu_custom_call" | custom-call | flops 671088640 | bytes 9383936 | tf_op jit(solution)/shard_map/pallas_call | solution.py:187
  24.2 0.3 collective-permute-done.6.block_ref
  24.5 1.9 %shard_map.63 = (f32[16,256]{1,0:T(8,128)S(1)}, f32[16,256]{1,0:T(8,128)S(1)}, f32[1024,256]{1,0:T(8,128)S(1)}) custom-call(bf16[128,1024]{1,0:T(8,128)(2,1)S(1)} %collective-permute-done.6.block_ref, bf16[1024,3072]{1,0:T(8,128)(2,1)S(1)} %copy-done, f32[1,1024]{1,0:T(1,128)S(1)} %bitcast.8, f32[2,1024]{1,0:T(2,128)S(1)} %copy-done.2, ...), custom_call_target="tpu_custom_call" | custom-call | flops 671088640 | bytes 9383936 | tf_op jit(solution)/shard_map/pallas_call | solution.py:187
  26.4 0.9 %collective-permute-done.7.block_ref = bf16[128,1024]{1,0:T(8,128)(2,1)S(1)} collective-permute-done((bf16[128,1024]{1,0:T(8,128)(2,1)S(1)}, bf16[128,1024]{1,0:T(8,128)(2,1)S(1)}, u32[]{:S(2)}, u32[]{:S(2)}) %collective-permute-start.7) | collective-permute-done | bytes 262176 | tf_op jit(solution)/shard_map/ppermute | solution.py:252
  27.4 1.7 %shard_map.64 = (f32[1024,128]{1,0:T(8,128)S(1)}, bf16[1024,128]{1,0:T(8,128)(2,1)S(1)}, f32[32,128]{1,0:T(8,128)S(1)}, f32[32,128]{1,0:T(8,128)S(1)}) custom-call(bf16[128,1024]{1,0:T(8,128)(2,1)S(1)} %collective-permute-done.7.block_ref, bf16[1024,3072]{1,0:T(8,128)(2,1)S(1)} %copy-done, f32[1,1024]{1,0:T(1,128)S(1)} %bitcast.9, f32[2,1024]{1,0:T(2,128)S(1)} %copy-done.2, ...), custom_call_target="tpu_custom_call" | custom-call | flops 671088640 | bytes 9121792 | tf_op jit(solution)/shard_map/pallas_call | solution.py:187
  29.1 0.6 %collective-permute-start.8 = (bf16[1024,128]{1,0:T(8,128)(2,1)S(1)}, bf16[1024,128]{1,0:T(8,128)(2,1)S(1)}, u32[]{:S(2)}, u32[]{:S(2)}) collective-permute-start(bf16[1024,128]{1,0:T(8,128)(2,1)S(1)} %get-tuple-element.116), channel_id=1, source_target_pairs={{0,8},{8,0},{1,9},{9,1},{2,10},{10,2},{3,11},{11,3},{4,12},{12,4},... | collective-permute-start | bytes 786440 | tf_op jit(solution)/shard_map/ppermute | solution.py:258
  29.7 0.1 collective-permute-start.9
  29.8 1.1 %collective-permute-done.9.their_state_ref = f32[32,128]{1,0:T(8,128)S(1)} collective-permute-done((f32[32,128]{1,0:T(8,128)S(1)}, f32[32,128]{1,0:T(8,128)S(1)}, u32[]{:S(2)}, u32[]{:S(2)}) %collective-permute-start.9) | collective-permute-done | bytes 16416 | tf_op jit(solution)/shard_map/ppermute | solution.py:259
  30.9 1.2 %shard_map.65 = bf16[128,1024]{1,0:T(8,128)(2,1)} custom-call(f32[1024,128]{1,0:T(8,128)S(1)} %get-tuple-element.115.mine_ref, bf16[1024,128]{1,0:T(8,128)(2,1)S(1)} %collective-permute-done.8.theirs_ref, f32[32,128]{1,0:T(8,128)S(1)} %get-tuple-element.117.my_state_ref, f32[32,128]{1,0:T(8,128)S(1)} %collective-permute-done.9.their_state_ref, ...), custom_call_target="tpu_custom_call" | custom-call | flops 268435456 | bytes 3178496 | tf_op jit(solution)/shard_map/pallas_call | solution.py:187
  (17 shorter events, 0.1 us)
Async XLA Ops:
  0.0 3.3 %copy-start.4 = (bf16[128,1024]{1,0:T(8,128)(2,1)S(1)}, bf16[128,1024]{1,0:T(8,128)(2,1)}, u32[]{:S(2)}) copy-start(bf16[128,1024]{1,0:T(8,128)(2,1)} %own_ref.1) | copy-start | bytes 786436
  0.0 3.3 %copy-start.2 = (f32[2,1024]{1,0:T(2,128)S(1)}, f32[2,1024]{1,0:T(2,128)}, u32[]{:S(2)}) copy-start(f32[2,1024]{1,0:T(2,128)} %gains_ref.17) | copy-start | bytes 24580
  0.0 3.3 %copy-start = (bf16[1024,3072]{1,0:T(8,128)(2,1)S(1)}, bf16[1024,3072]{1,0:T(8,128)(2,1)}, u32[]{:S(2)}) copy-start(bf16[1024,3072]{1,0:T(8,128)(2,1)} %w_ref.18) | copy-start | bytes 18874372
  0.0 3.3 %copy-start.3 = (f32[1024]{0:T(1024)S(1)}, f32[1024]{0:T(1024)}, u32[]{:S(2)}) copy-start(f32[1024]{0:T(1024)} %param.6) | copy-start | bytes 12292
  0.0 3.3 %collective-permute-start = (bf16[128,1024]{1,0:T(8,128)(2,1)}, bf16[128,1024]{1,0:T(8,128)(2,1)S(1)}, u32[]{:S(2)}, u32[]{:S(2)}) collective-permute-start(bf16[128,1024]{1,0:T(8,128)(2,1)} %own_ref.1), channel_id=1, source_target_pairs={{0,8},{8,0},{1,9},{9,1},{2,10},{10,2},{3,11},{11,3},{4,12},{12,4},... | collective-permute-start | bytes 786440 | tf_op jit(solution)/shard_map/ppermute | solution.py:217
  0.5 7.6 %collective-permute-start.1 = (bf16[128,1024]{1,0:T(8,128)(2,1)}, bf16[128,1024]{1,0:T(8,128)(2,1)S(1)}, u32[]{:S(2)}, u32[]{:S(2)}) collective-permute-start(bf16[128,1024]{1,0:T(8,128)(2,1)} %own_ref.1), channel_id=1, source_target_pairs={{0,10},{8,1},{1,8},{9,3},{2,12},{10,0},{3,9},{11,5},{4,14},{12,2},... | collective-permute-start | bytes 786440 | tf_op jit(solution)/shard_map/ppermute | solution.py:216
  4.6 6.3 %collective-permute-start.2 = (bf16[128,1024]{1,0:T(8,128)(2,1)S(1)}, bf16[128,1024]{1,0:T(8,128)(2,1)S(1)}, u32[]{:S(2)}, u32[]{:S(2)}) collective-permute-start(bf16[128,1024]{1,0:T(8,128)(2,1)S(1)} %copy-done.4), channel_id=1, source_target_pairs={{8,2},{0,9},{9,0},{1,11},{10,4},{2,8},{11,1},{3,13},{12,6},{4,10},... | collective-permute-start | bytes 786440 | tf_op jit(solution)/shard_map/ppermute | solution.py:226
  8.2 6.5 %collective-permute-start.3 = (bf16[128,1024]{1,0:T(8,128)(2,1)S(1)}, bf16[128,1024]{1,0:T(8,128)(2,1)S(1)}, u32[]{:S(2)}, u32[]{:S(2)}) collective-permute-start(bf16[128,1024]{1,0:T(8,128)(2,1)S(1)} %collective-permute-done.1.block_ref), channel_id=1, source_target_pairs={{8,2},{0,9},{9,0},{1,11},{10,4},{2,8},{11,1},{3,13},{12,6},{4,10},... | collective-permute-start | bytes 786440 | tf_op jit(solution)/shard_map/ppermute | solution.py:252
  10.9 7.4 %collective-permute-start.4 = (bf16[128,1024]{1,0:T(8,128)(2,1)S(1)}, bf16[128,1024]{1,0:T(8,128)(2,1)S(1)}, u32[]{:S(2)}, u32[]{:S(2)}) collective-permute-start(bf16[128,1024]{1,0:T(8,128)(2,1)S(1)} %collective-permute-done.2.block_ref), channel_id=1, source_target_pairs={{0,10},{8,1},{1,8},{9,3},{2,12},{10,0},{3,9},{11,5},{4,14},{12,2},... | collective-permute-start | bytes 786440 | tf_op jit(solution)/shard_map/ppermute | solution.py:255
  14.7 6.0 %collective-permute-start.5 = (bf16[128,1024]{1,0:T(8,128)(2,1)S(1)}, bf16[128,1024]{1,0:T(8,128)(2,1)S(1)}, u32[]{:S(2)}, u32[]{:S(2)}) collective-permute-start(bf16[128,1024]{1,0:T(8,128)(2,1)S(1)} %collective-permute-done.3.block_ref), channel_id=1, source_target_pairs={{0,10},{8,1},{1,8},{9,3},{2,12},{10,0},{3,9},{11,5},{4,14},{12,2},... | collective-permute-start | bytes 786440 | tf_op jit(solution)/shard_map/ppermute | solution.py:252
  18.3 6.2 %collective-permute-start.6 = (bf16[128,1024]{1,0:T(8,128)(2,1)S(1)}, bf16[128,1024]{1,0:T(8,128)(2,1)S(1)}, u32[]{:S(2)}, u32[]{:S(2)}) collective-permute-start(bf16[128,1024]{1,0:T(8,128)(2,1)S(1)} %collective-permute-done.4.block_ref), channel_id=1, source_target_pairs={{8,2},{0,9},{9,0},{1,11},{10,4},{2,8},{11,1},{3,13},{12,6},{4,10},... | collective-permute-start | bytes 786440 | tf_op jit(solution)/shard_map/ppermute | solution.py:255
  20.7 6.7 %collective-permute-start.7 = (bf16[128,1024]{1,0:T(8,128)(2,1)S(1)}, bf16[128,1024]{1,0:T(8,128)(2,1)S(1)}, u32[]{:S(2)}, u32[]{:S(2)}) collective-permute-start(bf16[128,1024]{1,0:T(8,128)(2,1)S(1)} %collective-permute-done.5.block_ref), channel_id=1, source_target_pairs={{8,2},{0,9},{9,0},{1,11},{10,4},{2,8},{11,1},{3,13},{12,6},{4,10},... | collective-permute-start | bytes 786440 | tf_op jit(solution)/shard_map/ppermute | solution.py:252
  24.5 6.3 %copy-start.1 = (bf16[1024,1024]{1,0:T(8,128)(2,1)S(1)}, bf16[1024,1024]{1,0:T(8,128)(2,1)}, u32[]{:S(2)}) copy-start(bf16[1024,1024]{1,0:T(8,128)(2,1)} %w_ref.19) | copy-start | bytes 6291460
  29.1 1.8 %collective-permute-start.8 = (bf16[1024,128]{1,0:T(8,128)(2,1)S(1)}, bf16[1024,128]{1,0:T(8,128)(2,1)S(1)}, u32[]{:S(2)}, u32[]{:S(2)}) collective-permute-start(bf16[1024,128]{1,0:T(8,128)(2,1)S(1)} %get-tuple-element.116), channel_id=1, source_target_pairs={{0,8},{8,0},{1,9},{9,1},{2,10},{10,2},{3,11},{11,3},{4,12},{12,4},... | collective-permute-start | bytes 786440 | tf_op jit(solution)/shard_map/ppermute | solution.py:258
  29.7 1.2 %collective-permute-start.9 = (f32[32,128]{1,0:T(8,128)S(1)}, f32[32,128]{1,0:T(8,128)S(1)}, u32[]{:S(2)}, u32[]{:S(2)}) collective-permute-start(f32[32,128]{1,0:T(8,128)S(1)} %get-tuple-element.118), channel_id=1, source_target_pairs={{0,8},{8,0},{1,9},{9,1},{2,10},{10,2},{3,11},{11,3},{4,12},{12,4},... | collective-permute-start | bytes 49160 | tf_op jit(solution)/shard_map/ppermute | solution.py:259

commit v5 on v4

--- a/solution.py
+++ b/solution.py
@@ -77,16 +77,21 @@
         query_ref[span, i * rows : (i + 1) * rows] = query.astype(F32).T.astype(BF16)
 
 
-def absorb(first, last, raw, block_ref, w_ref, gain_ref, gains_ref, ones_ref, q_ref, *refs):
+def absorb(first, last, raws, *refs):
+    blocks, refs = refs[: len(raws)], refs[len(raws) :]
+    w_ref, gain_ref, gains_ref, ones_ref, q_ref = refs[:5]
     if first:
-        outs = refs
+        outs = refs[5:]
     else:
-        (max_ref, sum_ref, acc_ref), outs = refs[:3], refs[3:]
+        (max_ref, sum_ref, acc_ref), outs = refs[5:8], refs[8:]
         old_max, old_sum = max_ref[...], sum_ref[...]
     width, queries = q_ref.shape
     half = queries // 2
     heads = SPAN // HD
-    block = normalised(block_ref[...], gain_ref[...]) if raw else block_ref[...]
+    blocks = [
+        normalised(ref[...], gain_ref[...]) if raw else ref[...] for ref, raw in zip(blocks, raws)
+    ]
+    block = jnp.concatenate(blocks, axis=0) if len(blocks) > 1 else blocks[0]
     ones = ones_ref[...]
     zeros = jnp.zeros((HD, queries), BF16)
     counts = jnp.ones((16, block.shape[0]), BF16)
@@ -222,7 +227,7 @@
         (patches, sibling, w_qkv, gain, qk_gains, ones),
         2 * 2 * rows * width * width,
     )
-    later, query = tie((patches, query))
+    later, query = tie((normed, query))
     two = lax.ppermute(later, axes, hops[1])
     state_shapes = [
         shape((H, 2 * rows), F32),
@@ -237,24 +242,29 @@
     ]
     flops = 2 * rows * width * 2 * width + 2 * 2 * rows * 2 * rows * width
 
-    def take(block, state, raw=True, last=False):
+    def take(blocks, state, last=False):
+        arrays, raws = zip(*blocks)
         return call(
-            functools.partial(absorb, not state, last, raw),
+            functools.partial(absorb, not state, last, raws),
             last_shapes if last else state_shapes,
-            (block, w_qkv, gain, qk_gains, ones, query, *state),
-            1 * flops,
-            H * rows * 2 * rows,
+            (*arrays, w_qkv, gain, qk_gains, ones, query, *state),
+            len(blocks) * flops,
+            len(blocks) * H * rows * 2 * rows,
         )
 
-    state, one = tie((take(normed, (), raw=False), one))
+    one, query = tie((one, query))
+    late, state = (normed, False), ()
     for turn in range(1, count // 2):
         here_one, here_two = one, two
         one = lax.ppermute(here_one, axes, hops[turn % 2])
-        state, here_two = tie((take(here_one, state), here_two))
         if turn < count // 2 - 1:
+            state, here_two = tie((take([late], state), here_two))
             two = lax.ppermute(here_two, axes, hops[(turn + 1) % 2])
-        state, one = tie((take(here_two, state), one))
-    mine, theirs, my_state, their_state = take(one, state, last=True)
+            state, one = tie((take([(here_one, True)], state), one))
+            late = here_two, False
+    state, here_two = tie((take([late, (here_one, True)], state), here_two))
+    state, one = tie((take([(here_two, False)], state), one))
+    mine, theirs, my_state, their_state = take([(one, True)], state, last=True)
     theirs = lax.ppermute(theirs, "head", swap)
     their_state = lax.ppermute(their_state, "head", swap)
     return call(

time: 32.2 us -> 32 us (level)
  starting transfers between devices: 13.4 us -> 14.5 us
  Pallas kernels: 16.1 us -> 15.1 us
    ppermute x2, starting transfers between devices: 2.65 us -> 3.8 us  [per_device(): two = lax.ppermute(here_two, axes, hops[(turn + 1) % 2])]
    pallas_call x11 -> x10, Pallas kernels: 16.1 us -> 15.1 us  [call(): pl.pallas_call(body, out_shape=outs, in_specs=[VMEM] * len(operands), out...]
    ppermute x3, waiting for transfers between devices: 0.94 us -> 0.01 us  [per_device(): one = lax.ppermute(here_one, axes, hops[turn % 2])]
    ppermute x1, waiting for transfers between devices: 0.01 us -> 0.81 us  [per_device(): one = lax.ppermute(patches, axes, hops[0])]
    ppermute x1, starting transfers between devices: 0.62 us -> 0.21 us  [per_device(): theirs = lax.ppermute(theirs, 'head', swap)]
  transfers between devices with their start and end apart: 10 -> 10, of which waited for: 3 -> 4; matrix products, arithmetic and copies ran while one was open for 0% -> 0% of each run, Pallas kernels for 41% -> 38%
where the time goes in v5:
time: 32 us; the launch traced here: 31.8 us
  Pallas kernels  15.1 us (47%)
  starting transfers between devices  14.5 us (45%)
  waiting for transfers between devices  2.07 us (6%)
    pallas_call x10, Pallas kernels, call(): pl.pallas_call(body, out_shape=outs, in_specs=[VMEM] * len(operands), out...  15.1 us
    ppermute x3, starting transfers between devices, per_device(): one = lax.ppermute(here_one, axes, hops[turn % 2])  4.87 us
    ppermute x2, starting transfers between devices, per_device(): two = lax.ppermute(here_two, axes, hops[(turn + 1) % 2])  3.8 us
    ppermute x1, starting transfers between devices, per_device(): one = lax.ppermute(patches, axes, hops[0])  2.69 us
    ppermute x1, starting transfers between devices, per_device(): two = lax.ppermute(later, axes, hops[1])  2.06 us
    ppermute x1, waiting for transfers between devices, per_device(): their_state = lax.ppermute(their_state, 'head', swap)  1.05 us
    ppermute x1, waiting for transfers between devices, per_device(): one = lax.ppermute(patches, axes, hops[0])  0.81 us
  transfers between devices with their start and end apart: 10, of which 4 were waited for; matrix products, arithmetic and copies ran while one was open for 0% of the time, Pallas kernels for 38%

profile of v5, /device:TPU:0, one launch (start us, length us, event | category | flops | bytes accessed | tf_op | source)
XLA Modules:
  0.0 31.8 jit_solution(2348763696155675623)
XLA Ops:
  0.0 0.5 %collective-permute-start = (bf16[128,1024]{1,0:T(8,128)(2,1)}, bf16[128,1024]{1,0:T(8,128)(2,1)S(1)}, u32[]{:S(2)}, u32[]{:S(2)}) collective-permute-start(bf16[128,1024]{1,0:T(8,128)(2,1)} %own_ref.1), channel_id=1, source_target_pairs={{0,8},{8,0},{1,9},{9,1},{2,10},{10,2},{3,11},{11,3},{4,12},{12,4},... | collective-permute-start | bytes 786440 | tf_op jit(solution)/shard_map/ppermute | solution.py:222
  0.5 2.7 %collective-permute-start.1 = (bf16[128,1024]{1,0:T(8,128)(2,1)}, bf16[128,1024]{1,0:T(8,128)(2,1)S(1)}, u32[]{:S(2)}, u32[]{:S(2)}) collective-permute-start(bf16[128,1024]{1,0:T(8,128)(2,1)} %own_ref.1), channel_id=1, source_target_pairs={{0,10},{8,1},{1,8},{9,3},{2,12},{10,0},{3,9},{11,5},{4,14},{12,2},... | collective-permute-start | bytes 786440 | tf_op jit(solution)/shard_map/ppermute | solution.py:221
  3.3 1.3 %shard_map.56 = (bf16[128,1024]{1,0:T(8,128)(2,1)S(1)}, bf16[1024,256]{1,0:T(8,128)(2,1)S(1)}) custom-call(bf16[128,1024]{1,0:T(8,128)(2,1)S(1)} %copy-done.4, bf16[128,1024]{1,0:T(8,128)(2,1)S(1)} %collective-permute-done.sibling_ref, bf16[1024,3072]{1,0:T(8,128)(2,1)S(1)} %copy-done, f32[1,1024]{1,0:T(1,128)S(1)} %bitcast.1, f32[2,1024]{1,0:T(2,128)S(1)} %copy-done.2, ...), custom_call_target="tpu_custom_call" | custom-call | flops 536870912 | bytes 7745536 | tf_op jit(solution)/shard_map/pallas_call | solution.py:192
  4.6 2.1 %collective-permute-start.2 = (bf16[128,1024]{1,0:T(8,128)(2,1)S(1)}, bf16[128,1024]{1,0:T(8,128)(2,1)S(1)}, u32[]{:S(2)}, u32[]{:S(2)}) collective-permute-start(bf16[128,1024]{1,0:T(8,128)(2,1)S(1)} %get-tuple-element.56.refs_0_), channel_id=1, source_target_pairs={{8,2},{0,9},{9,0},{1,11},{10,4},{2,8},{11,1},{3,13},{12,6},{4,10},... | collective-permute-start | bytes 786440 | tf_op jit(solution)/shard_map/ppermute | solution.py:231
  6.7 0.8 %collective-permute-done.1.refs_0_ = bf16[128,1024]{1,0:T(8,128)(2,1)S(1)} collective-permute-done((bf16[128,1024]{1,0:T(8,128)(2,1)}, bf16[128,1024]{1,0:T(8,128)(2,1)S(1)}, u32[]{:S(2)}, u32[]{:S(2)}) %collective-permute-start.1) | collective-permute-done | bytes 262176 | tf_op jit(solution)/shard_map/ppermute | solution.py:221
  7.5 1.7 %collective-permute-start.3 = (bf16[128,1024]{1,0:T(8,128)(2,1)S(1)}, bf16[128,1024]{1,0:T(8,128)(2,1)S(1)}, u32[]{:S(2)}, u32[]{:S(2)}) collective-permute-start(bf16[128,1024]{1,0:T(8,128)(2,1)S(1)} %collective-permute-done.1.refs_0_), channel_id=1, source_target_pairs={{8,2},{0,9},{9,0},{1,11},{10,4},{2,8},{11,1},{3,13},{12,6},{4,10},... | collective-permute-start | bytes 786440 | tf_op jit(solution)/shard_map/ppermute | solution.py:259
  9.2 1.5 %shard_map.57 = (f32[16,256]{1,0:T(8,128)S(1)}, f32[16,256]{1,0:T(8,128)S(1)}, f32[1024,256]{1,0:T(8,128)S(1)}) custom-call(bf16[128,1024]{1,0:T(8,128)(2,1)S(1)} %get-tuple-element.56.refs_0_, bf16[1024,3072]{1,0:T(8,128)(2,1)S(1)} %copy-done, f32[1,1024]{1,0:T(1,128)S(1)} %bitcast.2, f32[2,1024]{1,0:T(2,128)S(1)} %copy-done.2, ...), custom_call_target="tpu_custom_call" | custom-call | flops 671088640 | bytes 8302592 | tf_op jit(solution)/shard_map/pallas_call | solution.py:192
  10.7 0.1 collective-permute-done.2.refs_0_
  10.7 2.2 %collective-permute-start.4 = (bf16[128,1024]{1,0:T(8,128)(2,1)S(1)}, bf16[128,1024]{1,0:T(8,128)(2,1)S(1)}, u32[]{:S(2)}, u32[]{:S(2)}) collective-permute-start(bf16[128,1024]{1,0:T(8,128)(2,1)S(1)} %collective-permute-done.2.refs_0_), channel_id=1, source_target_pairs={{0,10},{8,1},{1,8},{9,3},{2,12},{10,0},{3,9},{11,5},{4,14},{12,2},... | collective-permute-start | bytes 786440 | tf_op jit(solution)/shard_map/ppermute | solution.py:262
  12.9 1.7 %shard_map.58 = (f32[16,256]{1,0:T(8,128)S(1)}, f32[16,256]{1,0:T(8,128)S(1)}, f32[1024,256]{1,0:T(8,128)S(1)}) custom-call(bf16[128,1024]{1,0:T(8,128)(2,1)S(1)} %collective-permute-done.1.refs_0_, bf16[1024,3072]{1,0:T(8,128)(2,1)S(1)} %copy-done, f32[1,1024]{1,0:T(1,128)S(1)} %bitcast.3, f32[2,1024]{1,0:T(2,128)S(1)} %copy-done.2, ...), custom_call_target="tpu_custom_call" | custom-call | flops 671088640 | bytes 9383936 | tf_op jit(solution)/shard_map/pallas_call | solution.py:192
  14.7 1.0 %collective-permute-start.5 = (bf16[128,1024]{1,0:T(8,128)(2,1)S(1)}, bf16[128,1024]{1,0:T(8,128)(2,1)S(1)}, u32[]{:S(2)}, u32[]{:S(2)}) collective-permute-start(bf16[128,1024]{1,0:T(8,128)(2,1)S(1)} %collective-permute-done.3.refs_0_), channel_id=1, source_target_pairs={{0,10},{8,1},{1,8},{9,3},{2,12},{10,0},{3,9},{11,5},{4,14},{12,2},... | collective-permute-start | bytes 786440 | tf_op jit(solution)/shard_map/ppermute | solution.py:259
  15.6 1.5 %shard_map.59 = (f32[16,256]{1,0:T(8,128)S(1)}, f32[16,256]{1,0:T(8,128)S(1)}, f32[1024,256]{1,0:T(8,128)S(1)}) custom-call(bf16[128,1024]{1,0:T(8,128)(2,1)S(1)} %collective-permute-done.2.refs_0_, bf16[1024,3072]{1,0:T(8,128)(2,1)S(1)} %copy-done, f32[1,1024]{1,0:T(1,128)S(1)} %bitcast.4, f32[2,1024]{1,0:T(2,128)S(1)} %copy-done.2, ...), custom_call_target="tpu_custom_call" | custom-call | flops 671088640 | bytes 9383936 | tf_op jit(solution)/shard_map/pallas_call | solution.py:192
  17.1 0.1 collective-permute-done.4.refs_0_
  17.3 1.6 %collective-permute-start.6 = (bf16[128,1024]{1,0:T(8,128)(2,1)S(1)}, bf16[128,1024]{1,0:T(8,128)(2,1)S(1)}, u32[]{:S(2)}, u32[]{:S(2)}) collective-permute-start(bf16[128,1024]{1,0:T(8,128)(2,1)S(1)} %collective-permute-done.4.refs_0_), channel_id=1, source_target_pairs={{8,2},{0,9},{9,0},{1,11},{10,4},{2,8},{11,1},{3,13},{12,6},{4,10},... | collective-permute-start | bytes 786440 | tf_op jit(solution)/shard_map/ppermute | solution.py:262
  18.9 1.7 %shard_map.60 = (f32[16,256]{1,0:T(8,128)S(1)}, f32[16,256]{1,0:T(8,128)S(1)}, f32[1024,256]{1,0:T(8,128)S(1)}) custom-call(bf16[128,1024]{1,0:T(8,128)(2,1)S(1)} %collective-permute-done.3.refs_0_, bf16[1024,3072]{1,0:T(8,128)(2,1)S(1)} %copy-done, f32[1,1024]{1,0:T(1,128)S(1)} %bitcast.5, f32[2,1024]{1,0:T(2,128)S(1)} %copy-done.2, ...), custom_call_target="tpu_custom_call" | custom-call | flops 671088640 | bytes 9383936 | tf_op jit(solution)/shard_map/pallas_call | solution.py:192
  20.6 2.2 %collective-permute-start.7 = (bf16[128,1024]{1,0:T(8,128)(2,1)S(1)}, bf16[128,1024]{1,0:T(8,128)(2,1)S(1)}, u32[]{:S(2)}, u32[]{:S(2)}) collective-permute-start(bf16[128,1024]{1,0:T(8,128)(2,1)S(1)} %collective-permute-done.5.refs_1_), channel_id=1, source_target_pairs={{8,2},{0,9},{9,0},{1,11},{10,4},{2,8},{11,1},{3,13},{12,6},{4,10},... | collective-permute-start | bytes 786440 | tf_op jit(solution)/shard_map/ppermute | solution.py:259
  22.8 2.9 %shard_map.61 = (f32[16,256]{1,0:T(8,128)S(1)}, f32[16,256]{1,0:T(8,128)S(1)}, f32[1024,256]{1,0:T(8,128)S(1)}) custom-call(bf16[128,1024]{1,0:T(8,128)(2,1)S(1)} %collective-permute-done.4.refs_0_, bf16[128,1024]{1,0:T(8,128)(2,1)S(1)} %collective-permute-done.5.refs_1_, bf16[1024,3072]{1,0:T(8,128)(2,1)S(1)} %copy-done, f32[1,1024]{1,0:T(1,128)S(1)} %bitcast.6, ...), custom_call_target="tpu_custom_call" | custom-call | flops 1342177280 | bytes 9646080 | tf_op jit(solution)/shard_map/pallas_call | solution.py:192
  25.7 0.0 copy-start.1
  25.8 1.5 %shard_map.62 = (f32[16,256]{1,0:T(8,128)S(1)}, f32[16,256]{1,0:T(8,128)S(1)}, f32[1024,256]{1,0:T(8,128)S(1)}) custom-call(bf16[128,1024]{1,0:T(8,128)(2,1)S(1)} %collective-permute-done.6.refs_0_, bf16[1024,3072]{1,0:T(8,128)(2,1)S(1)} %copy-done, f32[1,1024]{1,0:T(1,128)S(1)} %bitcast.7, f32[2,1024]{1,0:T(2,128)S(1)} %copy-done.2, ...), custom_call_target="tpu_custom_call" | custom-call | flops 671088640 | bytes 9383936 | tf_op jit(solution)/shard_map/pallas_call | solution.py:192
  27.3 1.7 %shard_map.63 = (f32[1024,128]{1,0:T(8,128)S(1)}, bf16[1024,128]{1,0:T(8,128)(2,1)S(1)}, f32[32,128]{1,0:T(8,128)S(1)}, f32[32,128]{1,0:T(8,128)S(1)}) custom-call(bf16[128,1024]{1,0:T(8,128)(2,1)S(1)} %collective-permute-done.7.refs_0_, bf16[1024,3072]{1,0:T(8,128)(2,1)S(1)} %copy-done, f32[1,1024]{1,0:T(1,128)S(1)} %bitcast.8, f32[2,1024]{1,0:T(2,128)S(1)} %copy-done.2, ...), custom_call_target="tpu_custom_call" | custom-call | flops 671088640 | bytes 9121792 | tf_op jit(solution)/shard_map/pallas_call | solution.py:192
  29.0 0.2 collective-permute-start.8
  29.2 0.4 %collective-permute-start.9 = (f32[32,128]{1,0:T(8,128)S(1)}, f32[32,128]{1,0:T(8,128)S(1)}, u32[]{:S(2)}, u32[]{:S(2)}) collective-permute-start(f32[32,128]{1,0:T(8,128)S(1)} %get-tuple-element.106), channel_id=1, source_target_pairs={{0,8},{8,0},{1,9},{9,1},{2,10},{10,2},{3,11},{11,3},{4,12},{12,4},... | collective-permute-start | bytes 49160 | tf_op jit(solution)/shard_map/ppermute | solution.py:269
  29.6 1.0 %collective-permute-done.9.their_state_ref = f32[32,128]{1,0:T(8,128)S(1)} collective-permute-done((f32[32,128]{1,0:T(8,128)S(1)}, f32[32,128]{1,0:T(8,128)S(1)}, u32[]{:S(2)}, u32[]{:S(2)}) %collective-permute-start.9) | collective-permute-done | bytes 16416 | tf_op jit(solution)/shard_map/ppermute | solution.py:269
  30.6 1.2 %shard_map.64 = bf16[128,1024]{1,0:T(8,128)(2,1)} custom-call(f32[1024,128]{1,0:T(8,128)S(1)} %get-tuple-element.103.mine_ref, bf16[1024,128]{1,0:T(8,128)(2,1)S(1)} %collective-permute-done.8.theirs_ref, f32[32,128]{1,0:T(8,128)S(1)} %get-tuple-element.105.my_state_ref, f32[32,128]{1,0:T(8,128)S(1)} %collective-permute-done.9.their_state_ref, ...), custom_call_target="tpu_custom_call" | custom-call | flops 268435456 | bytes 3178496 | tf_op jit(solution)/shard_map/pallas_call | solution.py:192
  (16 shorter events, 0.1 us)
Async XLA Ops:
  0.0 3.3 %copy-start.4 = (bf16[128,1024]{1,0:T(8,128)(2,1)S(1)}, bf16[128,1024]{1,0:T(8,128)(2,1)}, u32[]{:S(2)}) copy-start(bf16[128,1024]{1,0:T(8,128)(2,1)} %own_ref.1) | copy-start | bytes 786436
  0.0 3.3 %copy-start.3 = (f32[1024]{0:T(1024)S(1)}, f32[1024]{0:T(1024)}, u32[]{:S(2)}) copy-start(f32[1024]{0:T(1024)} %param.6) | copy-start | bytes 12292
  0.0 3.3 %copy-start = (bf16[1024,3072]{1,0:T(8,128)(2,1)S(1)}, bf16[1024,3072]{1,0:T(8,128)(2,1)}, u32[]{:S(2)}) copy-start(bf16[1024,3072]{1,0:T(8,128)(2,1)} %refs_1_.11) | copy-start | bytes 18874372
  0.0 3.3 %copy-start.2 = (f32[2,1024]{1,0:T(2,128)S(1)}, f32[2,1024]{1,0:T(2,128)}, u32[]{:S(2)}) copy-start(f32[2,1024]{1,0:T(2,128)} %refs_3_.11) | copy-start | bytes 24580
  0.0 3.3 %collective-permute-start = (bf16[128,1024]{1,0:T(8,128)(2,1)}, bf16[128,1024]{1,0:T(8,128)(2,1)S(1)}, u32[]{:S(2)}, u32[]{:S(2)}) collective-permute-start(bf16[128,1024]{1,0:T(8,128)(2,1)} %own_ref.1), channel_id=1, source_target_pairs={{0,8},{8,0},{1,9},{9,1},{2,10},{10,2},{3,11},{11,3},{4,12},{12,4},... | collective-permute-start | bytes 786440 | tf_op jit(solution)/shard_map/ppermute | solution.py:222
  0.5 7.0 %collective-permute-start.1 = (bf16[128,1024]{1,0:T(8,128)(2,1)}, bf16[128,1024]{1,0:T(8,128)(2,1)S(1)}, u32[]{:S(2)}, u32[]{:S(2)}) collective-permute-start(bf16[128,1024]{1,0:T(8,128)(2,1)} %own_ref.1), channel_id=1, source_target_pairs={{0,10},{8,1},{1,8},{9,3},{2,12},{10,0},{3,9},{11,5},{4,14},{12,2},... | collective-permute-start | bytes 786440 | tf_op jit(solution)/shard_map/ppermute | solution.py:221
  4.6 6.1 %collective-permute-start.2 = (bf16[128,1024]{1,0:T(8,128)(2,1)S(1)}, bf16[128,1024]{1,0:T(8,128)(2,1)S(1)}, u32[]{:S(2)}, u32[]{:S(2)}) collective-permute-start(bf16[128,1024]{1,0:T(8,128)(2,1)S(1)} %get-tuple-element.56.refs_0_), channel_id=1, source_target_pairs={{8,2},{0,9},{9,0},{1,11},{10,4},{2,8},{11,1},{3,13},{12,6},{4,10},... | collective-permute-start | bytes 786440 | tf_op jit(solution)/shard_map/ppermute | solution.py:231
  7.5 7.2 %collective-permute-start.3 = (bf16[128,1024]{1,0:T(8,128)(2,1)S(1)}, bf16[128,1024]{1,0:T(8,128)(2,1)S(1)}, u32[]{:S(2)}, u32[]{:S(2)}) collective-permute-start(bf16[128,1024]{1,0:T(8,128)(2,1)S(1)} %collective-permute-done.1.refs_0_), channel_id=1, source_target_pairs={{8,2},{0,9},{9,0},{1,11},{10,4},{2,8},{11,1},{3,13},{12,6},{4,10},... | collective-permute-start | bytes 786440 | tf_op jit(solution)/shard_map/ppermute | solution.py:259
  10.7 6.5 %collective-permute-start.4 = (bf16[128,1024]{1,0:T(8,128)(2,1)S(1)}, bf16[128,1024]{1,0:T(8,128)(2,1)S(1)}, u32[]{:S(2)}, u32[]{:S(2)}) collective-permute-start(bf16[128,1024]{1,0:T(8,128)(2,1)S(1)} %collective-permute-done.2.refs_0_), channel_id=1, source_target_pairs={{0,10},{8,1},{1,8},{9,3},{2,12},{10,0},{3,9},{11,5},{4,14},{12,2},... | collective-permute-start | bytes 786440 | tf_op jit(solution)/shard_map/ppermute | solution.py:262
  14.7 5.9 %collective-permute-start.5 = (bf16[128,1024]{1,0:T(8,128)(2,1)S(1)}, bf16[128,1024]{1,0:T(8,128)(2,1)S(1)}, u32[]{:S(2)}, u32[]{:S(2)}) collective-permute-start(bf16[128,1024]{1,0:T(8,128)(2,1)S(1)} %collective-permute-done.3.refs_0_), channel_id=1, source_target_pairs={{0,10},{8,1},{1,8},{9,3},{2,12},{10,0},{3,9},{11,5},{4,14},{12,2},... | collective-permute-start | bytes 786440 | tf_op jit(solution)/shard_map/ppermute | solution.py:259
  17.3 8.5 %collective-permute-start.6 = (bf16[128,1024]{1,0:T(8,128)(2,1)S(1)}, bf16[128,1024]{1,0:T(8,128)(2,1)S(1)}, u32[]{:S(2)}, u32[]{:S(2)}) collective-permute-start(bf16[128,1024]{1,0:T(8,128)(2,1)S(1)} %collective-permute-done.4.refs_0_), channel_id=1, source_target_pairs={{8,2},{0,9},{9,0},{1,11},{10,4},{2,8},{11,1},{3,13},{12,6},{4,10},... | collective-permute-start | bytes 786440 | tf_op jit(solution)/shard_map/ppermute | solution.py:262
  20.6 6.7 %collective-permute-start.7 = (bf16[128,1024]{1,0:T(8,128)(2,1)S(1)}, bf16[128,1024]{1,0:T(8,128)(2,1)S(1)}, u32[]{:S(2)}, u32[]{:S(2)}) collective-permute-start(bf16[128,1024]{1,0:T(8,128)(2,1)S(1)} %collective-permute-done.5.refs_1_), channel_id=1, source_target_pairs={{8,2},{0,9},{9,0},{1,11},{10,4},{2,8},{11,1},{3,13},{12,6},{4,10},... | collective-permute-start | bytes 786440 | tf_op jit(solution)/shard_map/ppermute | solution.py:259
  25.7 4.9 %copy-start.1 = (bf16[1024,1024]{1,0:T(8,128)(2,1)S(1)}, bf16[1024,1024]{1,0:T(8,128)(2,1)}, u32[]{:S(2)}) copy-start(bf16[1024,1024]{1,0:T(8,128)(2,1)} %w_ref.3) | copy-start | bytes 6291460
  29.0 1.6 %collective-permute-start.8 = (bf16[1024,128]{1,0:T(8,128)(2,1)S(1)}, bf16[1024,128]{1,0:T(8,128)(2,1)S(1)}, u32[]{:S(2)}, u32[]{:S(2)}) collective-permute-start(bf16[1024,128]{1,0:T(8,128)(2,1)S(1)} %get-tuple-element.104), channel_id=1, source_target_pairs={{0,8},{8,0},{1,9},{9,1},{2,10},{10,2},{3,11},{11,3},{4,12},{12,4},... | collective-permute-start | bytes 786440 | tf_op jit(solution)/shard_map/ppermute | solution.py:268
  29.2 1.4 %collective-permute-start.9 = (f32[32,128]{1,0:T(8,128)S(1)}, f32[32,128]{1,0:T(8,128)S(1)}, u32[]{:S(2)}, u32[]{:S(2)}) collective-permute-start(f32[32,128]{1,0:T(8,128)S(1)} %get-tuple-element.106), channel_id=1, source_target_pairs={{0,8},{8,0},{1,9},{9,1},{2,10},{10,2},{3,11},{11,3},{4,12},{12,4},... | collective-permute-start | bytes 49160 | tf_op jit(solution)/shard_map/ppermute | solution.py:269

commit v6 on v5

--- a/solution.py
+++ b/solution.py
@@ -59,17 +59,18 @@
     return (columns * lax.rsqrt(squares * (1.0 / HD) + 1e-06) * gain).astype(BF16)
 
 
-def query_kernel(
-    own_ref, sibling_ref, w_ref, gain_ref, gains_ref, ones_ref, normed_ref, query_ref
-):
+def normalise_kernel(own_ref, sibling_ref, gain_ref, w_ref, out_ref, other_ref):
+    for ref, block_ref in ((out_ref, own_ref), (other_ref, sibling_ref)):
+        ref[...] = normalised(block_ref[...], gain_ref[...])
+
+
+def query_kernel(own_ref, sibling_ref, w_ref, gains_ref, ones_ref, query_ref):
     rows, width = own_ref.shape
     ones = ones_ref[...]
     spans = [slice(at, at + SPAN) for at in range(0, width, SPAN)]
-    own = normalised(own_ref[...], gain_ref[...])
-    normed_ref[...] = own
     projected = [
-        (i, span, jnp.dot(block, w_ref[:, span], preferred_element_type=F32))
-        for i, block in enumerate((own, normalised(sibling_ref[...], gain_ref[...])))
+        (i, span, jnp.dot(ref[...], w_ref[:, span], preferred_element_type=F32))
+        for i, ref in enumerate((own_ref, sibling_ref))
         for span in spans
     ]
     for i, span, columns in projected:
@@ -221,14 +222,20 @@
     one = lax.ppermute(patches, axes, hops[0])
     sibling = lax.ppermute(patches, "head", swap)
     gain = ln_gain.reshape(1, width)
-    normed, query = call(
+    gain, ones = tie((gain, ones))
+    normed, other = call(
+        normalise_kernel,
+        [shape((rows, width), BF16)] * 2,
+        (patches, sibling, gain, w_qkv),
+        0,
+    )
+    two = lax.ppermute(normed, axes, hops[1])
+    (query,) = call(
         query_kernel,
-        [shape((rows, width), BF16), shape((width, 2 * rows), BF16)],
-        (patches, sibling, w_qkv, gain, qk_gains, ones),
+        [shape((width, 2 * rows), BF16)],
+        (normed, other, w_qkv, qk_gains, ones),
         2 * 2 * rows * width * width,
     )
-    later, query = tie((normed, query))
-    two = lax.ppermute(later, axes, hops[1])
     state_shapes = [
         shape((H, 2 * rows), F32),
         shape((H, 2 * rows), F32),

time: 32 us -> 31.9 us (level)
  starting transfers between devices: 14.5 us -> 13.8 us
  waiting for transfers between devices: 2.07 us -> 2.41 us
    ppermute x2, starting transfers between devices: 3.8 us -> 1.37 us  [per_device(): two = lax.ppermute(here_two, axes, hops[(turn + 1) % 2])]
    ppermute x3, starting transfers between devices: 4.87 us -> 6.58 us  [per_device(): one = lax.ppermute(here_one, axes, hops[turn % 2])]
    pallas_call x10 -> x11, Pallas kernels: 15.1 us -> 15.4 us  [call(): pl.pallas_call(body, out_shape=outs, in_specs=[VMEM] * len(operands), out...]
  transfers between devices with their start and end apart: 10 -> 10, of which waited for: 4 -> 3; matrix products, arithmetic and copies ran while one was open for 0% -> 0% of each run, Pallas kernels for 38% -> 39%
where the time goes in v6:
time: 31.9 us; the launch traced here: 31.7 us
  Pallas kernels  15.4 us (48%)
  starting transfers between devices  13.8 us (43%)
  waiting for transfers between devices  2.41 us (8%)
    pallas_call x11, Pallas kernels, call(): pl.pallas_call(body, out_shape=outs, in_specs=[VMEM] * len(operands), out...  15.4 us
    ppermute x3, starting transfers between devices, per_device(): one = lax.ppermute(here_one, axes, hops[turn % 2])  6.58 us
    ppermute x1, starting transfers between devices, per_device(): one = lax.ppermute(patches, axes, hops[0])  2.69 us
    ppermute x1, starting transfers between devices, per_device(): two = lax.ppermute(normed, axes, hops[1])  2.07 us
    ppermute x2, starting transfers between devices, per_device(): two = lax.ppermute(here_two, axes, hops[(turn + 1) % 2])  1.37 us
    ppermute x1, waiting for transfers between devices, per_device(): their_state = lax.ppermute(their_state, 'head', swap)  1.11 us
    ppermute x1, waiting for transfers between devices, per_device(): one = lax.ppermute(patches, axes, hops[0])  0.99 us
  transfers between devices with their start and end apart: 10, of which 3 were waited for; matrix products, arithmetic and copies ran while one was open for 0% of the time, Pallas kernels for 39%

profile of v6, /device:TPU:0, one launch (start us, length us, event | category | flops | bytes accessed | tf_op | source)
XLA Modules:
  0.0 31.7 jit_solution(8980489073495566983)
XLA Ops:
  0.0 0.5 %collective-permute-start = (bf16[128,1024]{1,0:T(8,128)(2,1)}, bf16[128,1024]{1,0:T(8,128)(2,1)S(1)}, u32[]{:S(2)}, u32[]{:S(2)}) collective-permute-start(bf16[128,1024]{1,0:T(8,128)(2,1)} %own_ref.1), channel_id=1, source_target_pairs={{0,8},{8,0},{1,9},{9,1},{2,10},{10,2},{3,11},{11,3},{4,12},{12,4},... | collective-permute-start | bytes 786440 | tf_op jit(solution)/shard_map/ppermute | solution.py:223
  0.5 2.7 %collective-permute-start.1 = (bf16[128,1024]{1,0:T(8,128)(2,1)}, bf16[128,1024]{1,0:T(8,128)(2,1)S(1)}, u32[]{:S(2)}, u32[]{:S(2)}) collective-permute-start(bf16[128,1024]{1,0:T(8,128)(2,1)} %own_ref.1), channel_id=1, source_target_pairs={{0,10},{8,1},{1,8},{9,3},{2,12},{10,0},{3,9},{11,5},{4,14},{12,2},... | collective-permute-start | bytes 786440 | tf_op jit(solution)/shard_map/ppermute | solution.py:222
  3.2 0.0 copy-start.2
  3.3 0.4 %shard_map.56 = (bf16[128,1024]{1,0:T(8,128)(2,1)S(1)}, bf16[128,1024]{1,0:T(8,128)(2,1)S(1)}) custom-call(bf16[128,1024]{1,0:T(8,128)(2,1)S(1)} %copy-done.4, bf16[128,1024]{1,0:T(8,128)(2,1)S(1)} %collective-permute-done.sibling_ref, f32[1,1024]{1,0:T(1,128)S(1)} %bitcast.1, bf16[1024,3072]{1,0:T(8,128)(2,1)S(1)} %copy-done), custom_call_target="tpu_custom_call" | custom-call | bytes 7344128 | tf_op jit(solution)/shard_map/pallas_call | solution.py:193
  3.7 2.1 %collective-permute-start.2 = (bf16[128,1024]{1,0:T(8,128)(2,1)S(1)}, bf16[128,1024]{1,0:T(8,128)(2,1)S(1)}, u32[]{:S(2)}, u32[]{:S(2)}) collective-permute-start(bf16[128,1024]{1,0:T(8,128)(2,1)S(1)} %get-tuple-element.58.own_ref.refs_0_), channel_id=1, source_target_pairs={{8,2},{0,9},{9,0},{1,11},{10,4},{2,8},{11,1},{3,13},{12,6},{4,10},... | collective-permute-start | bytes 786440 | tf_op jit(solution)/shard_map/ppermute | solution.py:232
  5.7 1.1 %shard_map.57.refs_5_.refs_6_ = bf16[1024,256]{1,0:T(8,128)(2,1)S(1)} custom-call(bf16[128,1024]{1,0:T(8,128)(2,1)S(1)} %get-tuple-element.58.own_ref.refs_0_, bf16[128,1024]{1,0:T(8,128)(2,1)S(1)} %get-tuple-element.60.sibling_ref, bf16[1024,3072]{1,0:T(8,128)(2,1)S(1)} %copy-done, f32[2,1024]{1,0:T(2,128)S(1)} %copy-done.2, ...), custom_call_target="tpu_custom_call" | custom-call | flops 536870912 | bytes 7479296 | tf_op jit(solution)/shard_map/pallas_call | solution.py:193
  6.8 1.0 %collective-permute-done.1.refs_0_ = bf16[128,1024]{1,0:T(8,128)(2,1)S(1)} collective-permute-done((bf16[128,1024]{1,0:T(8,128)(2,1)}, bf16[128,1024]{1,0:T(8,128)(2,1)S(1)}, u32[]{:S(2)}, u32[]{:S(2)}) %collective-permute-start.1) | collective-permute-done | bytes 262176 | tf_op jit(solution)/shard_map/ppermute | solution.py:222
  7.8 2.0 %collective-permute-start.3 = (bf16[128,1024]{1,0:T(8,128)(2,1)S(1)}, bf16[128,1024]{1,0:T(8,128)(2,1)S(1)}, u32[]{:S(2)}, u32[]{:S(2)}) collective-permute-start(bf16[128,1024]{1,0:T(8,128)(2,1)S(1)} %collective-permute-done.1.refs_0_), channel_id=1, source_target_pairs={{8,2},{0,9},{9,0},{1,11},{10,4},{2,8},{11,1},{3,13},{12,6},{4,10},... | collective-permute-start | bytes 786440 | tf_op jit(solution)/shard_map/ppermute | solution.py:266
  9.8 1.5 %shard_map.58 = (f32[16,256]{1,0:T(8,128)S(1)}, f32[16,256]{1,0:T(8,128)S(1)}, f32[1024,256]{1,0:T(8,128)S(1)}) custom-call(bf16[128,1024]{1,0:T(8,128)(2,1)S(1)} %get-tuple-element.58.own_ref.refs_0_, bf16[1024,3072]{1,0:T(8,128)(2,1)S(1)} %copy-done, f32[1,1024]{1,0:T(1,128)S(1)} %bitcast.2, f32[2,1024]{1,0:T(2,128)S(1)} %copy-done.2, ...), custom_call_target="tpu_custom_call" | custom-call | flops 671088640 | bytes 8302592 | tf_op jit(solution)/shard_map/pallas_call | solution.py:193
  11.4 0.9 %collective-permute-start.4 = (bf16[128,1024]{1,0:T(8,128)(2,1)S(1)}, bf16[128,1024]{1,0:T(8,128)(2,1)S(1)}, u32[]{:S(2)}, u32[]{:S(2)}) collective-permute-start(bf16[128,1024]{1,0:T(8,128)(2,1)S(1)} %collective-permute-done.2.refs_0_), channel_id=1, source_target_pairs={{0,10},{8,1},{1,8},{9,3},{2,12},{10,0},{3,9},{11,5},{4,14},{12,2},... | collective-permute-start | bytes 786440 | tf_op jit(solution)/shard_map/ppermute | solution.py:269
  12.3 1.7 %shard_map.59 = (f32[16,256]{1,0:T(8,128)S(1)}, f32[16,256]{1,0:T(8,128)S(1)}, f32[1024,256]{1,0:T(8,128)S(1)}) custom-call(bf16[128,1024]{1,0:T(8,128)(2,1)S(1)} %collective-permute-done.1.refs_0_, bf16[1024,3072]{1,0:T(8,128)(2,1)S(1)} %copy-done, f32[1,1024]{1,0:T(1,128)S(1)} %bitcast.3, f32[2,1024]{1,0:T(2,128)S(1)} %copy-done.2, ...), custom_call_target="tpu_custom_call" | custom-call | flops 671088640 | bytes 9383936 | tf_op jit(solution)/shard_map/pallas_call | solution.py:193
  14.0 2.6 %collective-permute-start.5 = (bf16[128,1024]{1,0:T(8,128)(2,1)S(1)}, bf16[128,1024]{1,0:T(8,128)(2,1)S(1)}, u32[]{:S(2)}, u32[]{:S(2)}) collective-permute-start(bf16[128,1024]{1,0:T(8,128)(2,1)S(1)} %collective-permute-done.3.refs_0_), channel_id=1, source_target_pairs={{0,10},{8,1},{1,8},{9,3},{2,12},{10,0},{3,9},{11,5},{4,14},{12,2},... | collective-permute-start | bytes 786440 | tf_op jit(solution)/shard_map/ppermute | solution.py:266
  16.6 1.5 %shard_map.60 = (f32[16,256]{1,0:T(8,128)S(1)}, f32[16,256]{1,0:T(8,128)S(1)}, f32[1024,256]{1,0:T(8,128)S(1)}) custom-call(bf16[128,1024]{1,0:T(8,128)(2,1)S(1)} %collective-permute-done.2.refs_0_, bf16[1024,3072]{1,0:T(8,128)(2,1)S(1)} %copy-done, f32[1,1024]{1,0:T(1,128)S(1)} %bitcast.4, f32[2,1024]{1,0:T(2,128)S(1)} %copy-done.2, ...), custom_call_target="tpu_custom_call" | custom-call | flops 671088640 | bytes 9383936 | tf_op jit(solution)/shard_map/pallas_call | solution.py:193
  18.2 0.5 %collective-permute-start.6 = (bf16[128,1024]{1,0:T(8,128)(2,1)S(1)}, bf16[128,1024]{1,0:T(8,128)(2,1)S(1)}, u32[]{:S(2)}, u32[]{:S(2)}) collective-permute-start(bf16[128,1024]{1,0:T(8,128)(2,1)S(1)} %collective-permute-done.4.refs_0_), channel_id=1, source_target_pairs={{8,2},{0,9},{9,0},{1,11},{10,4},{2,8},{11,1},{3,13},{12,6},{4,10},... | collective-permute-start | bytes 786440 | tf_op jit(solution)/shard_map/ppermute | solution.py:269
  18.6 1.7 %shard_map.61 = (f32[16,256]{1,0:T(8,128)S(1)}, f32[16,256]{1,0:T(8,128)S(1)}, f32[1024,256]{1,0:T(8,128)S(1)}) custom-call(bf16[128,1024]{1,0:T(8,128)(2,1)S(1)} %collective-permute-done.3.refs_0_, bf16[1024,3072]{1,0:T(8,128)(2,1)S(1)} %copy-done, f32[1,1024]{1,0:T(1,128)S(1)} %bitcast.5, f32[2,1024]{1,0:T(2,128)S(1)} %copy-done.2, ...), custom_call_target="tpu_custom_call" | custom-call | flops 671088640 | bytes 9383936 | tf_op jit(solution)/shard_map/pallas_call | solution.py:193
  20.4 0.3 collective-permute-done.5.refs_1_
  20.7 1.9 %collective-permute-start.7 = (bf16[128,1024]{1,0:T(8,128)(2,1)S(1)}, bf16[128,1024]{1,0:T(8,128)(2,1)S(1)}, u32[]{:S(2)}, u32[]{:S(2)}) collective-permute-start(bf16[128,1024]{1,0:T(8,128)(2,1)S(1)} %collective-permute-done.5.refs_1_), channel_id=1, source_target_pairs={{8,2},{0,9},{9,0},{1,11},{10,4},{2,8},{11,1},{3,13},{12,6},{4,10},... | collective-permute-start | bytes 786440 | tf_op jit(solution)/shard_map/ppermute | solution.py:266
  22.6 2.9 %shard_map.62 = (f32[16,256]{1,0:T(8,128)S(1)}, f32[16,256]{1,0:T(8,128)S(1)}, f32[1024,256]{1,0:T(8,128)S(1)}) custom-call(bf16[128,1024]{1,0:T(8,128)(2,1)S(1)} %collective-permute-done.4.refs_0_, bf16[128,1024]{1,0:T(8,128)(2,1)S(1)} %collective-permute-done.5.refs_1_, bf16[1024,3072]{1,0:T(8,128)(2,1)S(1)} %copy-done, f32[1,1024]{1,0:T(1,128)S(1)} %bitcast.6, ...), custom_call_target="tpu_custom_call" | custom-call | flops 1342177280 | bytes 9646080 | tf_op jit(solution)/shard_map/pallas_call | solution.py:193
  25.6 1.5 %shard_map.63 = (f32[16,256]{1,0:T(8,128)S(1)}, f32[16,256]{1,0:T(8,128)S(1)}, f32[1024,256]{1,0:T(8,128)S(1)}) custom-call(bf16[128,1024]{1,0:T(8,128)(2,1)S(1)} %collective-permute-done.6.refs_0_, bf16[1024,3072]{1,0:T(8,128)(2,1)S(1)} %copy-done, f32[1,1024]{1,0:T(1,128)S(1)} %bitcast.7, f32[2,1024]{1,0:T(2,128)S(1)} %copy-done.2, ...), custom_call_target="tpu_custom_call" | custom-call | flops 671088640 | bytes 9383936 | tf_op jit(solution)/shard_map/pallas_call | solution.py:193
  27.1 1.7 %shard_map.64 = (f32[1024,128]{1,0:T(8,128)S(1)}, bf16[1024,128]{1,0:T(8,128)(2,1)S(1)}, f32[32,128]{1,0:T(8,128)S(1)}, f32[32,128]{1,0:T(8,128)S(1)}) custom-call(bf16[128,1024]{1,0:T(8,128)(2,1)S(1)} %collective-permute-done.7.refs_0_, bf16[1024,3072]{1,0:T(8,128)(2,1)S(1)} %copy-done, f32[1,1024]{1,0:T(1,128)S(1)} %bitcast.8, f32[2,1024]{1,0:T(2,128)S(1)} %copy-done.2, ...), custom_call_target="tpu_custom_call" | custom-call | flops 671088640 | bytes 9121792 | tf_op jit(solution)/shard_map/pallas_call | solution.py:193
  28.8 0.5 %collective-permute-start.8 = (bf16[1024,128]{1,0:T(8,128)(2,1)S(1)}, bf16[1024,128]{1,0:T(8,128)(2,1)S(1)}, u32[]{:S(2)}, u32[]{:S(2)}) collective-permute-start(bf16[1024,128]{1,0:T(8,128)(2,1)S(1)} %get-tuple-element.106), channel_id=1, source_target_pairs={{0,8},{8,0},{1,9},{9,1},{2,10},{10,2},{3,11},{11,3},{4,12},{12,4},... | collective-permute-start | bytes 786440 | tf_op jit(solution)/shard_map/ppermute | solution.py:275
  29.3 0.1 collective-permute-start.9
  29.4 1.1 %collective-permute-done.9.their_state_ref = f32[32,128]{1,0:T(8,128)S(1)} collective-permute-done((f32[32,128]{1,0:T(8,128)S(1)}, f32[32,128]{1,0:T(8,128)S(1)}, u32[]{:S(2)}, u32[]{:S(2)}) %collective-permute-start.9) | collective-permute-done | bytes 16416 | tf_op jit(solution)/shard_map/ppermute | solution.py:276
  30.5 1.2 %shard_map.65 = bf16[128,1024]{1,0:T(8,128)(2,1)} custom-call(f32[1024,128]{1,0:T(8,128)S(1)} %get-tuple-element.105.mine_ref, bf16[1024,128]{1,0:T(8,128)(2,1)S(1)} %collective-permute-done.8.theirs_ref, f32[32,128]{1,0:T(8,128)S(1)} %get-tuple-element.107.my_state_ref, f32[32,128]{1,0:T(8,128)S(1)} %collective-permute-done.9.their_state_ref, ...), custom_call_target="tpu_custom_call" | custom-call | flops 268435456 | bytes 3178496 | tf_op jit(solution)/shard_map/pallas_call | solution.py:193
  (17 shorter events, 0.1 us)
Async XLA Ops:
  0.0 3.3 %copy-start.4 = (bf16[128,1024]{1,0:T(8,128)(2,1)S(1)}, bf16[128,1024]{1,0:T(8,128)(2,1)}, u32[]{:S(2)}) copy-start(bf16[128,1024]{1,0:T(8,128)(2,1)} %own_ref.1) | copy-start | bytes 786436
  0.0 3.3 %copy-start.3 = (f32[1024]{0:T(1024)S(1)}, f32[1024]{0:T(1024)}, u32[]{:S(2)}) copy-start(f32[1024]{0:T(1024)} %param.6) | copy-start | bytes 12292
  0.0 3.3 %copy-start = (bf16[1024,3072]{1,0:T(8,128)(2,1)S(1)}, bf16[1024,3072]{1,0:T(8,128)(2,1)}, u32[]{:S(2)}) copy-start(bf16[1024,3072]{1,0:T(8,128)(2,1)} %refs_1_.11) | copy-start | bytes 18874372
  0.0 3.3 %collective-permute-start = (bf16[128,1024]{1,0:T(8,128)(2,1)}, bf16[128,1024]{1,0:T(8,128)(2,1)S(1)}, u32[]{:S(2)}, u32[]{:S(2)}) collective-permute-start(bf16[128,1024]{1,0:T(8,128)(2,1)} %own_ref.1), channel_id=1, source_target_pairs={{0,8},{8,0},{1,9},{9,1},{2,10},{10,2},{3,11},{11,3},{4,12},{12,4},... | collective-permute-start | bytes 786440 | tf_op jit(solution)/shard_map/ppermute | solution.py:223
  0.5 7.3 %collective-permute-start.1 = (bf16[128,1024]{1,0:T(8,128)(2,1)}, bf16[128,1024]{1,0:T(8,128)(2,1)S(1)}, u32[]{:S(2)}, u32[]{:S(2)}) collective-permute-start(bf16[128,1024]{1,0:T(8,128)(2,1)} %own_ref.1), channel_id=1, source_target_pairs={{0,10},{8,1},{1,8},{9,3},{2,12},{10,0},{3,9},{11,5},{4,14},{12,2},... | collective-permute-start | bytes 786440 | tf_op jit(solution)/shard_map/ppermute | solution.py:222
  3.2 2.5 %copy-start.2 = (f32[2,1024]{1,0:T(2,128)S(1)}, f32[2,1024]{1,0:T(2,128)}, u32[]{:S(2)}) copy-start(f32[2,1024]{1,0:T(2,128)} %refs_3_.11) | copy-start | bytes 24580
  3.7 7.7 %collective-permute-start.2 = (bf16[128,1024]{1,0:T(8,128)(2,1)S(1)}, bf16[128,1024]{1,0:T(8,128)(2,1)S(1)}, u32[]{:S(2)}, u32[]{:S(2)}) collective-permute-start(bf16[128,1024]{1,0:T(8,128)(2,1)S(1)} %get-tuple-element.58.own_ref.refs_0_), channel_id=1, source_target_pairs={{8,2},{0,9},{9,0},{1,11},{10,4},{2,8},{11,1},{3,13},{12,6},{4,10},... | collective-permute-start | bytes 786440 | tf_op jit(solution)/shard_map/ppermute | solution.py:232
  7.8 6.2 %collective-permute-start.3 = (bf16[128,1024]{1,0:T(8,128)(2,1)S(1)}, bf16[128,1024]{1,0:T(8,128)(2,1)S(1)}, u32[]{:S(2)}, u32[]{:S(2)}) collective-permute-start(bf16[128,1024]{1,0:T(8,128)(2,1)S(1)} %collective-permute-done.1.refs_0_), channel_id=1, source_target_pairs={{8,2},{0,9},{9,0},{1,11},{10,4},{2,8},{11,1},{3,13},{12,6},{4,10},... | collective-permute-start | bytes 786440 | tf_op jit(solution)/shard_map/ppermute | solution.py:266
  11.4 6.8 %collective-permute-start.4 = (bf16[128,1024]{1,0:T(8,128)(2,1)S(1)}, bf16[128,1024]{1,0:T(8,128)(2,1)S(1)}, u32[]{:S(2)}, u32[]{:S(2)}) collective-permute-start(bf16[128,1024]{1,0:T(8,128)(2,1)S(1)} %collective-permute-done.2.refs_0_), channel_id=1, source_target_pairs={{0,10},{8,1},{1,8},{9,3},{2,12},{10,0},{3,9},{11,5},{4,14},{12,2},... | collective-permute-start | bytes 786440 | tf_op jit(solution)/shard_map/ppermute | solution.py:269
  14.0 6.7 %collective-permute-start.5 = (bf16[128,1024]{1,0:T(8,128)(2,1)S(1)}, bf16[128,1024]{1,0:T(8,128)(2,1)S(1)}, u32[]{:S(2)}, u32[]{:S(2)}) collective-permute-start(bf16[128,1024]{1,0:T(8,128)(2,1)S(1)} %collective-permute-done.3.refs_0_), channel_id=1, source_target_pairs={{0,10},{8,1},{1,8},{9,3},{2,12},{10,0},{3,9},{11,5},{4,14},{12,2},... | collective-permute-start | bytes 786440 | tf_op jit(solution)/shard_map/ppermute | solution.py:266
  18.2 7.4 %collective-permute-start.6 = (bf16[128,1024]{1,0:T(8,128)(2,1)S(1)}, bf16[128,1024]{1,0:T(8,128)(2,1)S(1)}, u32[]{:S(2)}, u32[]{:S(2)}) collective-permute-start(bf16[128,1024]{1,0:T(8,128)(2,1)S(1)} %collective-permute-done.4.refs_0_), channel_id=1, source_target_pairs={{8,2},{0,9},{9,0},{1,11},{10,4},{2,8},{11,1},{3,13},{12,6},{4,10},... | collective-permute-start | bytes 786440 | tf_op jit(solution)/shard_map/ppermute | solution.py:269
  20.7 6.4 %collective-permute-start.7 = (bf16[128,1024]{1,0:T(8,128)(2,1)S(1)}, bf16[128,1024]{1,0:T(8,128)(2,1)S(1)}, u32[]{:S(2)}, u32[]{:S(2)}) collective-permute-start(bf16[128,1024]{1,0:T(8,128)(2,1)S(1)} %collective-permute-done.5.refs_1_), channel_id=1, source_target_pairs={{8,2},{0,9},{9,0},{1,11},{10,4},{2,8},{11,1},{3,13},{12,6},{4,10},... | collective-permute-start | bytes 786440 | tf_op jit(solution)/shard_map/ppermute | solution.py:266
  25.5 5.0 %copy-start.1 = (bf16[1024,1024]{1,0:T(8,128)(2,1)S(1)}, bf16[1024,1024]{1,0:T(8,128)(2,1)}, u32[]{:S(2)}) copy-start(bf16[1024,1024]{1,0:T(8,128)(2,1)} %w_ref.5) | copy-start | bytes 6291460
  28.8 1.7 %collective-permute-start.8 = (bf16[1024,128]{1,0:T(8,128)(2,1)S(1)}, bf16[1024,128]{1,0:T(8,128)(2,1)S(1)}, u32[]{:S(2)}, u32[]{:S(2)}) collective-permute-start(bf16[1024,128]{1,0:T(8,128)(2,1)S(1)} %get-tuple-element.106), channel_id=1, source_target_pairs={{0,8},{8,0},{1,9},{9,1},{2,10},{10,2},{3,11},{11,3},{4,12},{12,4},... | collective-permute-start | bytes 786440 | tf_op jit(solution)/shard_map/ppermute | solution.py:275
  29.3 1.2 %collective-permute-start.9 = (f32[32,128]{1,0:T(8,128)S(1)}, f32[32,128]{1,0:T(8,128)S(1)}, u32[]{:S(2)}, u32[]{:S(2)}) collective-permute-start(f32[32,128]{1,0:T(8,128)S(1)} %get-tuple-element.108), channel_id=1, source_target_pairs={{0,8},{8,0},{1,9},{9,1},{2,10},{10,2},{3,11},{11,3},{4,12},{12,4},... | collective-permute-start | bytes 49160 | tf_op jit(solution)/shard_map/ppermute | solution.py:276

commit v7 on v6

--- a/solution.py
+++ b/solution.py
@@ -212,7 +212,7 @@
             for h, step in ((right_core, 1), (1 - right_core, -1))
         ]
 
-    hops = (onward(0), onward(1))
+    hops = (onward(1), onward(0))
     axes = ("head", "blk")
     swap = [(0, 1), (1, 0)]
 
@@ -229,7 +229,7 @@
         (patches, sibling, gain, w_qkv),
         0,
     )
-    two = lax.ppermute(normed, axes, hops[1])
+    two = lax.ppermute(other, axes, hops[0])
     (query,) = call(
         query_kernel,
         [shape((width, 2 * rows), BF16)],
@@ -266,7 +266,7 @@
         one = lax.ppermute(here_one, axes, hops[turn % 2])
         if turn < count // 2 - 1:
             state, here_two = tie((take([late], state), here_two))
-            two = lax.ppermute(here_two, axes, hops[(turn + 1) % 2])
+            two = lax.ppermute(here_two, axes, hops[turn % 2])
             state, one = tie((take([(here_one, True)], state), one))
             late = here_two, False
     state, here_two = tie((take([late, (here_one, True)], state), here_two))

time: 31.9 us -> 31.6 us (level)
    ppermute x3, starting transfers between devices: 6.58 us -> 4.05 us  [per_device(): one = lax.ppermute(here_one, axes, hops[turn % 2])]
    ppermute x3, starting transfers between devices: 3.44 us -> 5.8 us  [the longest x2 3.67 us: per_device(): two = lax.ppermute(here_two, axes, hops[turn % 2])]
    ppermute x3, waiting for transfers between devices: 0.3 us -> 0.69 us  [per_device(): one = lax.ppermute(here_one, axes, hops[turn % 2])]
    ppermute x1, waiting for transfers between devices: 0.99 us -> 0.62 us  [per_device(): one = lax.ppermute(patches, axes, hops[0])]
where the time goes in v7:
time: 31.6 us; the launch traced here: 31.5 us
  Pallas kernels  15.4 us (49%)
  starting transfers between devices  13.6 us (43%)
  waiting for transfers between devices  2.4 us (8%)
    pallas_call x11, Pallas kernels, call(): pl.pallas_call(body, out_shape=outs, in_specs=[VMEM] * len(operands), out...  15.4 us
    ppermute x3, starting transfers between devices, per_device(): one = lax.ppermute(here_one, axes, hops[turn % 2])  4.05 us
    ppermute x2, starting transfers between devices, per_device(): two = lax.ppermute(here_two, axes, hops[turn % 2])  3.67 us
    ppermute x1, starting transfers between devices, per_device(): one = lax.ppermute(patches, axes, hops[0])  2.63 us
    ppermute x1, starting transfers between devices, per_device(): two = lax.ppermute(other, axes, hops[0])  2.12 us
    ppermute x1, waiting for transfers between devices, per_device(): their_state = lax.ppermute(their_state, 'head', swap)  1.08 us
    ppermute x3, waiting for transfers between devices, per_device(): one = lax.ppermute(here_one, axes, hops[turn % 2])  0.69 us
  transfers between devices with their start and end apart: 10, of which 3 were waited for; matrix products, arithmetic and copies ran while one was open for 0% of the time, Pallas kernels for 39%

profile of v7, /device:TPU:0, one launch (start us, length us, event | category | flops | bytes accessed | tf_op | source)
XLA Modules:
  0.0 31.5 jit_solution(11813682691962663405)
XLA Ops:
  0.0 0.5 %collective-permute-start = (bf16[128,1024]{1,0:T(8,128)(2,1)}, bf16[128,1024]{1,0:T(8,128)(2,1)S(1)}, u32[]{:S(2)}, u32[]{:S(2)}) collective-permute-start(bf16[128,1024]{1,0:T(8,128)(2,1)} %own_ref.1), channel_id=1, source_target_pairs={{0,8},{8,0},{1,9},{9,1},{2,10},{10,2},{3,11},{11,3},{4,12},{12,4},... | collective-permute-start | bytes 786440 | tf_op jit(solution)/shard_map/ppermute | solution.py:223
  0.5 2.6 %collective-permute-start.1 = (bf16[128,1024]{1,0:T(8,128)(2,1)}, bf16[128,1024]{1,0:T(8,128)(2,1)S(1)}, u32[]{:S(2)}, u32[]{:S(2)}) collective-permute-start(bf16[128,1024]{1,0:T(8,128)(2,1)} %own_ref.1), channel_id=1, source_target_pairs={{8,2},{0,9},{9,0},{1,11},{10,4},{2,8},{11,1},{3,13},{12,6},{4,10},... | collective-permute-start | bytes 786440 | tf_op jit(solution)/shard_map/ppermute | solution.py:222
  3.2 0.0 copy-start.2
  3.2 0.4 %shard_map.56 = (bf16[128,1024]{1,0:T(8,128)(2,1)S(1)}, bf16[128,1024]{1,0:T(8,128)(2,1)S(1)}) custom-call(bf16[128,1024]{1,0:T(8,128)(2,1)S(1)} %copy-done.4, bf16[128,1024]{1,0:T(8,128)(2,1)S(1)} %collective-permute-done.sibling_ref, f32[1,1024]{1,0:T(1,128)S(1)} %bitcast.1, bf16[1024,3072]{1,0:T(8,128)(2,1)S(1)} %copy-done), custom_call_target="tpu_custom_call" | custom-call | bytes 7344128 | tf_op jit(solution)/shard_map/pallas_call | solution.py:193
  3.6 2.1 %collective-permute-start.2 = (bf16[128,1024]{1,0:T(8,128)(2,1)S(1)}, bf16[128,1024]{1,0:T(8,128)(2,1)S(1)}, u32[]{:S(2)}, u32[]{:S(2)}) collective-permute-start(bf16[128,1024]{1,0:T(8,128)(2,1)S(1)} %get-tuple-element.60.sibling_ref), channel_id=1, source_target_pairs={{8,2},{0,9},{9,0},{1,11},{10,4},{2,8},{11,1},{3,13},{12,6},{4,10},... | collective-permute-start | bytes 786440 | tf_op jit(solution)/shard_map/ppermute | solution.py:232
  5.7 1.1 %shard_map.57.refs_5_.refs_6_ = bf16[1024,256]{1,0:T(8,128)(2,1)S(1)} custom-call(bf16[128,1024]{1,0:T(8,128)(2,1)S(1)} %get-tuple-element.58.own_ref.refs_0_, bf16[128,1024]{1,0:T(8,128)(2,1)S(1)} %get-tuple-element.60.sibling_ref, bf16[1024,3072]{1,0:T(8,128)(2,1)S(1)} %copy-done, f32[2,1024]{1,0:T(2,128)S(1)} %copy-done.2, ...), custom_call_target="tpu_custom_call" | custom-call | flops 536870912 | bytes 7479296 | tf_op jit(solution)/shard_map/pallas_call | solution.py:193
  6.8 0.6 %collective-permute-done.1.refs_0_ = bf16[128,1024]{1,0:T(8,128)(2,1)S(1)} collective-permute-done((bf16[128,1024]{1,0:T(8,128)(2,1)}, bf16[128,1024]{1,0:T(8,128)(2,1)S(1)}, u32[]{:S(2)}, u32[]{:S(2)}) %collective-permute-start.1) | collective-permute-done | bytes 262176 | tf_op jit(solution)/shard_map/ppermute | solution.py:222
  7.4 2.1 %collective-permute-start.3 = (bf16[128,1024]{1,0:T(8,128)(2,1)S(1)}, bf16[128,1024]{1,0:T(8,128)(2,1)S(1)}, u32[]{:S(2)}, u32[]{:S(2)}) collective-permute-start(bf16[128,1024]{1,0:T(8,128)(2,1)S(1)} %collective-permute-done.1.refs_0_), channel_id=1, source_target_pairs={{0,10},{8,1},{1,8},{9,3},{2,12},{10,0},{3,9},{11,5},{4,14},{12,2},... | collective-permute-start | bytes 786440 | tf_op jit(solution)/shard_map/ppermute | solution.py:266
  9.5 1.5 %shard_map.58 = (f32[16,256]{1,0:T(8,128)S(1)}, f32[16,256]{1,0:T(8,128)S(1)}, f32[1024,256]{1,0:T(8,128)S(1)}) custom-call(bf16[128,1024]{1,0:T(8,128)(2,1)S(1)} %get-tuple-element.58.own_ref.refs_0_, bf16[1024,3072]{1,0:T(8,128)(2,1)S(1)} %copy-done, f32[1,1024]{1,0:T(1,128)S(1)} %bitcast.2, f32[2,1024]{1,0:T(2,128)S(1)} %copy-done.2, ...), custom_call_target="tpu_custom_call" | custom-call | flops 671088640 | bytes 8302592 | tf_op jit(solution)/shard_map/pallas_call | solution.py:193
  11.0 1.5 %collective-permute-start.4 = (bf16[128,1024]{1,0:T(8,128)(2,1)S(1)}, bf16[128,1024]{1,0:T(8,128)(2,1)S(1)}, u32[]{:S(2)}, u32[]{:S(2)}) collective-permute-start(bf16[128,1024]{1,0:T(8,128)(2,1)S(1)} %collective-permute-done.2.refs_0_), channel_id=1, source_target_pairs={{0,10},{8,1},{1,8},{9,3},{2,12},{10,0},{3,9},{11,5},{4,14},{12,2},... | collective-permute-start | bytes 786440 | tf_op jit(solution)/shard_map/ppermute | solution.py:269
  12.5 1.7 %shard_map.59 = (f32[16,256]{1,0:T(8,128)S(1)}, f32[16,256]{1,0:T(8,128)S(1)}, f32[1024,256]{1,0:T(8,128)S(1)}) custom-call(bf16[128,1024]{1,0:T(8,128)(2,1)S(1)} %collective-permute-done.1.refs_0_, bf16[1024,3072]{1,0:T(8,128)(2,1)S(1)} %copy-done, f32[1,1024]{1,0:T(1,128)S(1)} %bitcast.3, f32[2,1024]{1,0:T(2,128)S(1)} %copy-done.2, ...), custom_call_target="tpu_custom_call" | custom-call | flops 671088640 | bytes 9383936 | tf_op jit(solution)/shard_map/pallas_call | solution.py:193
  14.3 1.3 %collective-permute-start.5 = (bf16[128,1024]{1,0:T(8,128)(2,1)S(1)}, bf16[128,1024]{1,0:T(8,128)(2,1)S(1)}, u32[]{:S(2)}, u32[]{:S(2)}) collective-permute-start(bf16[128,1024]{1,0:T(8,128)(2,1)S(1)} %collective-permute-done.3.refs_0_), channel_id=1, source_target_pairs={{8,2},{0,9},{9,0},{1,11},{10,4},{2,8},{11,1},{3,13},{12,6},{4,10},... | collective-permute-start | bytes 786440 | tf_op jit(solution)/shard_map/ppermute | solution.py:266
  15.6 1.5 %shard_map.60 = (f32[16,256]{1,0:T(8,128)S(1)}, f32[16,256]{1,0:T(8,128)S(1)}, f32[1024,256]{1,0:T(8,128)S(1)}) custom-call(bf16[128,1024]{1,0:T(8,128)(2,1)S(1)} %collective-permute-done.2.refs_0_, bf16[1024,3072]{1,0:T(8,128)(2,1)S(1)} %copy-done, f32[1,1024]{1,0:T(1,128)S(1)} %bitcast.4, f32[2,1024]{1,0:T(2,128)S(1)} %copy-done.2, ...), custom_call_target="tpu_custom_call" | custom-call | flops 671088640 | bytes 9383936 | tf_op jit(solution)/shard_map/pallas_call | solution.py:193
  17.1 2.2 %collective-permute-start.6 = (bf16[128,1024]{1,0:T(8,128)(2,1)S(1)}, bf16[128,1024]{1,0:T(8,128)(2,1)S(1)}, u32[]{:S(2)}, u32[]{:S(2)}) collective-permute-start(bf16[128,1024]{1,0:T(8,128)(2,1)S(1)} %collective-permute-done.4.refs_0_), channel_id=1, source_target_pairs={{8,2},{0,9},{9,0},{1,11},{10,4},{2,8},{11,1},{3,13},{12,6},{4,10},... | collective-permute-start | bytes 786440 | tf_op jit(solution)/shard_map/ppermute | solution.py:269
  19.3 1.7 %shard_map.61 = (f32[16,256]{1,0:T(8,128)S(1)}, f32[16,256]{1,0:T(8,128)S(1)}, f32[1024,256]{1,0:T(8,128)S(1)}) custom-call(bf16[128,1024]{1,0:T(8,128)(2,1)S(1)} %collective-permute-done.3.refs_0_, bf16[1024,3072]{1,0:T(8,128)(2,1)S(1)} %copy-done, f32[1,1024]{1,0:T(1,128)S(1)} %bitcast.5, f32[2,1024]{1,0:T(2,128)S(1)} %copy-done.2, ...), custom_call_target="tpu_custom_call" | custom-call | flops 671088640 | bytes 9383936 | tf_op jit(solution)/shard_map/pallas_call | solution.py:193
  21.0 0.7 %collective-permute-start.7 = (bf16[128,1024]{1,0:T(8,128)(2,1)S(1)}, bf16[128,1024]{1,0:T(8,128)(2,1)S(1)}, u32[]{:S(2)}, u32[]{:S(2)}) collective-permute-start(bf16[128,1024]{1,0:T(8,128)(2,1)S(1)} %collective-permute-done.5.refs_1_), channel_id=1, source_target_pairs={{0,10},{8,1},{1,8},{9,3},{2,12},{10,0},{3,9},{11,5},{4,14},{12,2},... | collective-permute-start | bytes 786440 | tf_op jit(solution)/shard_map/ppermute | solution.py:266
  21.7 2.9 %shard_map.62 = (f32[16,256]{1,0:T(8,128)S(1)}, f32[16,256]{1,0:T(8,128)S(1)}, f32[1024,256]{1,0:T(8,128)S(1)}) custom-call(bf16[128,1024]{1,0:T(8,128)(2,1)S(1)} %collective-permute-done.4.refs_0_, bf16[128,1024]{1,0:T(8,128)(2,1)S(1)} %collective-permute-done.5.refs_1_, bf16[1024,3072]{1,0:T(8,128)(2,1)S(1)} %copy-done, f32[1,1024]{1,0:T(1,128)S(1)} %bitcast.6, ...), custom_call_target="tpu_custom_call" | custom-call | flops 1342177280 | bytes 9646080 | tf_op jit(solution)/shard_map/pallas_call | solution.py:193
  24.7 1.5 %shard_map.63 = (f32[16,256]{1,0:T(8,128)S(1)}, f32[16,256]{1,0:T(8,128)S(1)}, f32[1024,256]{1,0:T(8,128)S(1)}) custom-call(bf16[128,1024]{1,0:T(8,128)(2,1)S(1)} %collective-permute-done.6.refs_0_, bf16[1024,3072]{1,0:T(8,128)(2,1)S(1)} %copy-done, f32[1,1024]{1,0:T(1,128)S(1)} %bitcast.7, f32[2,1024]{1,0:T(2,128)S(1)} %copy-done.2, ...), custom_call_target="tpu_custom_call" | custom-call | flops 671088640 | bytes 9383936 | tf_op jit(solution)/shard_map/pallas_call | solution.py:193
  26.2 0.7 %collective-permute-done.7.refs_0_ = bf16[128,1024]{1,0:T(8,128)(2,1)S(1)} collective-permute-done((bf16[128,1024]{1,0:T(8,128)(2,1)S(1)}, bf16[128,1024]{1,0:T(8,128)(2,1)S(1)}, u32[]{:S(2)}, u32[]{:S(2)}) %collective-permute-start.7) | collective-permute-done | bytes 262176 | tf_op jit(solution)/shard_map/ppermute | solution.py:266
  26.9 1.7 %shard_map.64 = (f32[1024,128]{1,0:T(8,128)S(1)}, bf16[1024,128]{1,0:T(8,128)(2,1)S(1)}, f32[32,128]{1,0:T(8,128)S(1)}, f32[32,128]{1,0:T(8,128)S(1)}) custom-call(bf16[128,1024]{1,0:T(8,128)(2,1)S(1)} %collective-permute-done.7.refs_0_, bf16[1024,3072]{1,0:T(8,128)(2,1)S(1)} %copy-done, f32[1,1024]{1,0:T(1,128)S(1)} %bitcast.8, f32[2,1024]{1,0:T(2,128)S(1)} %copy-done.2, ...), custom_call_target="tpu_custom_call" | custom-call | flops 671088640 | bytes 9121792 | tf_op jit(solution)/shard_map/pallas_call | solution.py:193
  28.6 0.5 %collective-permute-start.8 = (bf16[1024,128]{1,0:T(8,128)(2,1)S(1)}, bf16[1024,128]{1,0:T(8,128)(2,1)S(1)}, u32[]{:S(2)}, u32[]{:S(2)}) collective-permute-start(bf16[1024,128]{1,0:T(8,128)(2,1)S(1)} %get-tuple-element.106), channel_id=1, source_target_pairs={{0,8},{8,0},{1,9},{9,1},{2,10},{10,2},{3,11},{11,3},{4,12},{12,4},... | collective-permute-start | bytes 786440 | tf_op jit(solution)/shard_map/ppermute | solution.py:275
  29.1 0.1 collective-permute-start.9
  29.2 1.1 %collective-permute-done.9.their_state_ref = f32[32,128]{1,0:T(8,128)S(1)} collective-permute-done((f32[32,128]{1,0:T(8,128)S(1)}, f32[32,128]{1,0:T(8,128)S(1)}, u32[]{:S(2)}, u32[]{:S(2)}) %collective-permute-start.9) | collective-permute-done | bytes 16416 | tf_op jit(solution)/shard_map/ppermute | solution.py:276
  30.3 1.2 %shard_map.65 = bf16[128,1024]{1,0:T(8,128)(2,1)} custom-call(f32[1024,128]{1,0:T(8,128)S(1)} %get-tuple-element.105.mine_ref, bf16[1024,128]{1,0:T(8,128)(2,1)S(1)} %collective-permute-done.8.theirs_ref, f32[32,128]{1,0:T(8,128)S(1)} %get-tuple-element.107.my_state_ref, f32[32,128]{1,0:T(8,128)S(1)} %collective-permute-done.9.their_state_ref, ...), custom_call_target="tpu_custom_call" | custom-call | flops 268435456 | bytes 3178496 | tf_op jit(solution)/shard_map/pallas_call | solution.py:193
  (17 shorter events, 0.1 us)
Async XLA Ops:
  0.0 3.2 %copy-start.4 = (bf16[128,1024]{1,0:T(8,128)(2,1)S(1)}, bf16[128,1024]{1,0:T(8,128)(2,1)}, u32[]{:S(2)}) copy-start(bf16[128,1024]{1,0:T(8,128)(2,1)} %own_ref.1) | copy-start | bytes 786436
  0.0 3.2 %copy-start.3 = (f32[1024]{0:T(1024)S(1)}, f32[1024]{0:T(1024)}, u32[]{:S(2)}) copy-start(f32[1024]{0:T(1024)} %param.6) | copy-start | bytes 12292
  0.0 3.2 %copy-start = (bf16[1024,3072]{1,0:T(8,128)(2,1)S(1)}, bf16[1024,3072]{1,0:T(8,128)(2,1)}, u32[]{:S(2)}) copy-start(bf16[1024,3072]{1,0:T(8,128)(2,1)} %refs_1_.11) | copy-start | bytes 18874372
  0.0 3.2 %collective-permute-start = (bf16[128,1024]{1,0:T(8,128)(2,1)}, bf16[128,1024]{1,0:T(8,128)(2,1)S(1)}, u32[]{:S(2)}, u32[]{:S(2)}) collective-permute-start(bf16[128,1024]{1,0:T(8,128)(2,1)} %own_ref.1), channel_id=1, source_target_pairs={{0,8},{8,0},{1,9},{9,1},{2,10},{10,2},{3,11},{11,3},{4,12},{12,4},... | collective-permute-start | bytes 786440 | tf_op jit(solution)/shard_map/ppermute | solution.py:223
  0.5 6.9 %collective-permute-start.1 = (bf16[128,1024]{1,0:T(8,128)(2,1)}, bf16[128,1024]{1,0:T(8,128)(2,1)S(1)}, u32[]{:S(2)}, u32[]{:S(2)}) collective-permute-start(bf16[128,1024]{1,0:T(8,128)(2,1)} %own_ref.1), channel_id=1, source_target_pairs={{8,2},{0,9},{9,0},{1,11},{10,4},{2,8},{11,1},{3,13},{12,6},{4,10},... | collective-permute-start | bytes 786440 | tf_op jit(solution)/shard_map/ppermute | solution.py:222
  3.2 2.5 %copy-start.2 = (f32[2,1024]{1,0:T(2,128)S(1)}, f32[2,1024]{1,0:T(2,128)}, u32[]{:S(2)}) copy-start(f32[2,1024]{1,0:T(2,128)} %refs_3_.11) | copy-start | bytes 24580
  3.6 7.4 %collective-permute-start.2 = (bf16[128,1024]{1,0:T(8,128)(2,1)S(1)}, bf16[128,1024]{1,0:T(8,128)(2,1)S(1)}, u32[]{:S(2)}, u32[]{:S(2)}) collective-permute-start(bf16[128,1024]{1,0:T(8,128)(2,1)S(1)} %get-tuple-element.60.sibling_ref), channel_id=1, source_target_pairs={{8,2},{0,9},{9,0},{1,11},{10,4},{2,8},{11,1},{3,13},{12,6},{4,10},... | collective-permute-start | bytes 786440 | tf_op jit(solution)/shard_map/ppermute | solution.py:232
  7.4 6.8 %collective-permute-start.3 = (bf16[128,1024]{1,0:T(8,128)(2,1)S(1)}, bf16[128,1024]{1,0:T(8,128)(2,1)S(1)}, u32[]{:S(2)}, u32[]{:S(2)}) collective-permute-start(bf16[128,1024]{1,0:T(8,128)(2,1)S(1)} %collective-permute-done.1.refs_0_), channel_id=1, source_target_pairs={{0,10},{8,1},{1,8},{9,3},{2,12},{10,0},{3,9},{11,5},{4,14},{12,2},... | collective-permute-start | bytes 786440 | tf_op jit(solution)/shard_map/ppermute | solution.py:266
  11.0 6.1 %collective-permute-start.4 = (bf16[128,1024]{1,0:T(8,128)(2,1)S(1)}, bf16[128,1024]{1,0:T(8,128)(2,1)S(1)}, u32[]{:S(2)}, u32[]{:S(2)}) collective-permute-start(bf16[128,1024]{1,0:T(8,128)(2,1)S(1)} %collective-permute-done.2.refs_0_), channel_id=1, source_target_pairs={{0,10},{8,1},{1,8},{9,3},{2,12},{10,0},{3,9},{11,5},{4,14},{12,2},... | collective-permute-start | bytes 786440 | tf_op jit(solution)/shard_map/ppermute | solution.py:269
  14.3 6.8 %collective-permute-start.5 = (bf16[128,1024]{1,0:T(8,128)(2,1)S(1)}, bf16[128,1024]{1,0:T(8,128)(2,1)S(1)}, u32[]{:S(2)}, u32[]{:S(2)}) collective-permute-start(bf16[128,1024]{1,0:T(8,128)(2,1)S(1)} %collective-permute-done.3.refs_0_), channel_id=1, source_target_pairs={{8,2},{0,9},{9,0},{1,11},{10,4},{2,8},{11,1},{3,13},{12,6},{4,10},... | collective-permute-start | bytes 786440 | tf_op jit(solution)/shard_map/ppermute | solution.py:266
  17.1 7.5 %collective-permute-start.6 = (bf16[128,1024]{1,0:T(8,128)(2,1)S(1)}, bf16[128,1024]{1,0:T(8,128)(2,1)S(1)}, u32[]{:S(2)}, u32[]{:S(2)}) collective-permute-start(bf16[128,1024]{1,0:T(8,128)(2,1)S(1)} %collective-permute-done.4.refs_0_), channel_id=1, source_target_pairs={{8,2},{0,9},{9,0},{1,11},{10,4},{2,8},{11,1},{3,13},{12,6},{4,10},... | collective-permute-start | bytes 786440 | tf_op jit(solution)/shard_map/ppermute | solution.py:269
  21.0 5.9 %collective-permute-start.7 = (bf16[128,1024]{1,0:T(8,128)(2,1)S(1)}, bf16[128,1024]{1,0:T(8,128)(2,1)S(1)}, u32[]{:S(2)}, u32[]{:S(2)}) collective-permute-start(bf16[128,1024]{1,0:T(8,128)(2,1)S(1)} %collective-permute-done.5.refs_1_), channel_id=1, source_target_pairs={{0,10},{8,1},{1,8},{9,3},{2,12},{10,0},{3,9},{11,5},{4,14},{12,2},... | collective-permute-start | bytes 786440 | tf_op jit(solution)/shard_map/ppermute | solution.py:266
  24.7 5.6 %copy-start.1 = (bf16[1024,1024]{1,0:T(8,128)(2,1)S(1)}, bf16[1024,1024]{1,0:T(8,128)(2,1)}, u32[]{:S(2)}) copy-start(bf16[1024,1024]{1,0:T(8,128)(2,1)} %w_ref.5) | copy-start | bytes 6291460
  28.6 1.7 %collective-permute-start.8 = (bf16[1024,128]{1,0:T(8,128)(2,1)S(1)}, bf16[1024,128]{1,0:T(8,128)(2,1)S(1)}, u32[]{:S(2)}, u32[]{:S(2)}) collective-permute-start(bf16[1024,128]{1,0:T(8,128)(2,1)S(1)} %get-tuple-element.106), channel_id=1, source_target_pairs={{0,8},{8,0},{1,9},{9,1},{2,10},{10,2},{3,11},{11,3},{4,12},{12,4},... | collective-permute-start | bytes 786440 | tf_op jit(solution)/shard_map/ppermute | solution.py:275
  29.1 1.2 %collective-permute-start.9 = (f32[32,128]{1,0:T(8,128)S(1)}, f32[32,128]{1,0:T(8,128)S(1)}, u32[]{:S(2)}, u32[]{:S(2)}) collective-permute-start(f32[32,128]{1,0:T(8,128)S(1)} %get-tuple-element.108), channel_id=1, source_target_pairs={{0,8},{8,0},{1,9},{9,1},{2,10},{10,2},{3,11},{11,3},{4,12},{12,4},... | collective-permute-start | bytes 49160 | tf_op jit(solution)/shard_map/ppermute | solution.py:276

commit v8 on v7

--- a/solution.py
+++ b/solution.py
@@ -78,7 +78,14 @@
         query_ref[span, i * rows : (i + 1) * rows] = query.astype(F32).T.astype(BF16)
 
 
-def absorb(first, last, raws, *refs):
+def pipeline(stages, count):
+    for turn in range(count + len(stages) - 1):
+        for behind, stage in enumerate(stages):
+            if 0 <= turn - behind < count:
+                stage(turn - behind)
+
+
+def absorb(first, raws, *refs):
     blocks, refs = refs[: len(raws)], refs[len(raws) :]
     w_ref, gain_ref, gains_ref, ones_ref, q_ref = refs[:5]
     if first:
@@ -87,7 +94,6 @@
         (max_ref, sum_ref, acc_ref), outs = refs[5:8], refs[8:]
         old_max, old_sum = max_ref[...], sum_ref[...]
     width, queries = q_ref.shape
-    half = queries // 2
     heads = SPAN // HD
     blocks = [
         normalised(ref[...], gain_ref[...]) if raw else ref[...] for ref, raw in zip(blocks, raws)
@@ -147,26 +153,111 @@
                 total = total + old_sum[i * heads + j : i * heads + j + 1] * shrink
                 added = added + acc_ref[at : at + HD, :] * shrink
             sums.append(total)
-            if last:
-                for ref, part in zip(outs[:2], halves):
-                    ref[at : at + HD, :] = added[:, part].astype(ref.dtype)
-            else:
-                outs[2][at : at + HD, :] = added
-
-    halves = (slice(0, half), slice(half, queries))
-    stages = (project, norm, score, soften, weigh)
-    for turn in range(width // SPAN + len(stages) - 1):
-        for behind, stage in enumerate(stages):
-            if 0 <= turn - behind < width // SPAN:
-                stage(turn - behind)
+            outs[2][at : at + HD, :] = added
+
+    pipeline((project, norm, score, soften, weigh), width // SPAN)
     top, total = jnp.concatenate(maxima, axis=0), jnp.concatenate(sums, axis=0)
-    if last:
-        for ref, part in zip(outs[2:], halves):
-            ref[:H, :] = top[:, part]
-            ref[H:, :] = total[:, part]
-    else:
-        outs[0][...] = top
-        outs[1][...] = total
+    outs[0][...] = top
+    outs[1][...] = total
+
+
+def half_stages(held, part, q_ref, max_ref, sum_ref, acc_ref, put):
+    old_max, old_sum = max_ref[:, part], sum_ref[:, part]
+    half = old_max.shape[1]
+    zeros = jnp.zeros((HD, half), BF16)
+    pairs = [(j, slice(j * PAIR, (j + 1) * PAIR)) for j in range(SPAN // PAIR)]
+    maxima, sums = [], []
+
+    def beside(rows, i, j):
+        head = (i * SPAN + j * PAIR) // HD
+        return jnp.concatenate([rows[head : head + 1], rows[head + 1 : head + 2]], axis=1)
+
+    def score(i):
+        keys = held.pop(("key", i))
+        for j, pair in pairs:
+            at = i * SPAN + j * PAIR
+            even, odd = q_ref[at : at + HD, part], q_ref[at + HD : at + PAIR, part]
+            query = jnp.concatenate(
+                [jnp.concatenate([even, zeros], axis=1), jnp.concatenate([zeros, odd], axis=1)],
+                axis=0,
+            )
+            held["score", i, j] = jnp.dot(keys[:, pair], query, preferred_element_type=F32)
+
+    def soften(i):
+        for j, _ in pairs:
+            scores, before = held.pop(("score", i, j)), beside(old_max, i, j)
+            top = jnp.maximum(jnp.max(scores, axis=0, keepdims=True), before)
+            held["shrink", i, j] = jnp.exp2(before - top)
+            held["weight", i, j] = jnp.exp2(scores - top).astype(BF16)
+            maxima.extend([top[:, :half], top[:, half:]])
+
+    def weigh(i):
+        values = held.pop(("value", i))
+        counts = jnp.ones((16, values.shape[1]), BF16)
+        for j, pair in pairs:
+            both = jnp.dot(
+                jnp.concatenate([values[pair], counts], axis=0),
+                held.pop(("weight", i, j)),
+                preferred_element_type=F32,
+            )
+            shrink = held.pop(("shrink", i, j))
+            total = both[PAIR : PAIR + 1] + beside(old_sum, i, j) * shrink
+            sums.extend([total[:, :half], total[:, half:]])
+            for k, side in enumerate((slice(0, half), slice(half, 2 * half))):
+                at = i * SPAN + j * PAIR + k * HD
+                added = both[k * HD : (k + 1) * HD, side]
+                put(at, added + acc_ref[at : at + HD, part] * shrink[:, side])
+
+    return (score, soften, weigh), maxima, sums
+
+
+def send_kernel(
+    block_ref, w_ref, gain_ref, gains_ref, ones_ref, q_ref, max_ref, sum_ref, acc_ref,
+    sent_ref, sent_state_ref, keys_ref, values_ref,
+):
+    width, queries = q_ref.shape
+    block = normalised(block_ref[...], gain_ref[...])
+    ones = ones_ref[...]
+    held = {}
+
+    def project(i):
+        for name, at in (("key", width), ("value", 2 * width)):
+            span = slice(at + i * SPAN, at + (i + 1) * SPAN)
+            held[name, i] = jnp.dot(block, w_ref[:, span], preferred_element_type=F32)
+
+    def norm(i):
+        span = slice(i * SPAN, (i + 1) * SPAN)
+        keys_ref[:, span] = held["key", i] = head_norm(held["key", i], gains_ref[1:2, span], ones)
+        values_ref[span, :] = held["value", i] = held["value", i].T.astype(BF16)
+
+    def put(at, rows):
+        sent_ref[at : at + HD, :] = rows.astype(BF16)
+
+    part = slice(queries // 2, queries)
+    stages, maxima, sums = half_stages(held, part, q_ref, max_ref, sum_ref, acc_ref, put)
+    pipeline((project, norm, *stages), width // SPAN)
+    top, total = jnp.concatenate(maxima, axis=0), jnp.concatenate(sums, axis=0)
+    sent_state_ref[:H, :] = top
+    sent_state_ref[H:, :] = total
+
+
+def keep_kernel(
+    keys_ref, values_ref, q_ref, max_ref, sum_ref, acc_ref, mine_ref, state_ref
+):
+    width, queries = q_ref.shape
+    held = {}
+    for i in range(width // SPAN):
+        span = slice(i * SPAN, (i + 1) * SPAN)
+        held["key", i], held["value", i] = keys_ref[:, span], values_ref[span, :]
+
+    def put(at, rows):
+        mine_ref[at : at + HD, :] = rows
+
+    part = slice(0, queries // 2)
+    stages, maxima, sums = half_stages(held, part, q_ref, max_ref, sum_ref, acc_ref, put)
+    pipeline(stages, width // SPAN)
+    state_ref[:H, :] = jnp.concatenate(maxima, axis=0)
+    state_ref[H:, :] = jnp.concatenate(sums, axis=0)
 
 
 def finish_kernel(mine_ref, theirs_ref, my_state_ref, their_state_ref, w_ref, out_ref):
@@ -241,19 +332,13 @@
         shape((H, 2 * rows), F32),
         shape((width, 2 * rows), F32),
     ]
-    last_shapes = [
-        shape((width, rows), F32),
-        shape((width, rows), BF16),
-        shape((2 * H, rows), F32),
-        shape((2 * H, rows), F32),
-    ]
     flops = 2 * rows * width * 2 * width + 2 * 2 * rows * 2 * rows * width
 
-    def take(blocks, state, last=False):
+    def take(blocks, state):
         arrays, raws = zip(*blocks)
         return call(
-            functools.partial(absorb, not state, last, raws),
-            last_shapes if last else state_shapes,
+            functools.partial(absorb, not state, raws),
+            state_shapes,
             (*arrays, w_qkv, gain, qk_gains, ones, query, *state),
             len(blocks) * flops,
             len(blocks) * H * rows * 2 * rows,
@@ -271,9 +356,27 @@
             late = here_two, False
     state, here_two = tie((take([late, (here_one, True)], state), here_two))
     state, one = tie((take([(here_two, False)], state), one))
-    mine, theirs, my_state, their_state = take([(one, True)], state, last=True)
-    theirs = lax.ppermute(theirs, "head", swap)
-    their_state = lax.ppermute(their_state, "head", swap)
+    sent, sent_state, keys, values = call(
+        send_kernel,
+        [
+            shape((width, rows), BF16),
+            shape((2 * H, rows), F32),
+            shape((rows, width), BF16),
+            shape((width, rows), BF16),
+        ],
+        (one, w_qkv, gain, qk_gains, ones, query, *state),
+        flops,
+        H * rows * rows,
+    )
+    theirs = lax.ppermute(sent, "head", swap)
+    their_state = lax.ppermute(sent_state, "head", swap)
+    mine, my_state = call(
+        keep_kernel,
+        [shape((width, rows), F32), shape((2 * H, rows), F32)],
+        (keys, values, query, *state),
+        flops // 4,
+        H * rows * rows,
+    )
     return call(
         finish_kernel,
         [shape((rows, width), BF16)],

time: 31.6 us -> 31.5 us (level)
  waiting for transfers between devices: 2.4 us -> 1.73 us
  Pallas kernels: 15.4 us -> 15.8 us
    ppermute x2, waiting for transfers between devices: 1.08 us -> 0.42 us  [the longest x1 0.41 us: per_device(): their_state = lax.ppermute(sent_state, 'head', swap)]
    pallas_call x11 -> x12, Pallas kernels: 15.4 us -> 15.8 us  [call(): pl.pallas_call(body, out_shape=outs, in_specs=[VMEM] * len(operands), out...]
  transfers between devices with their start and end apart: 10 -> 10, of which waited for: 3 -> 3; matrix products, arithmetic and copies ran while one was open for 0% -> 0% of each run, Pallas kernels for 39% -> 42%
where the time goes in v8:
time: 31.5 us; the launch traced here: 31.3 us
  Pallas kernels  15.8 us (50%)
  starting transfers between devices  13.6 us (43%)
  waiting for transfers between devices  1.73 us (5%)
    pallas_call x12, Pallas kernels, call(): pl.pallas_call(body, out_shape=outs, in_specs=[VMEM] * len(operands), out...  15.8 us
    ppermute x3, starting transfers between devices, per_device(): one = lax.ppermute(here_one, axes, hops[turn % 2])  4.06 us
    ppermute x2, starting transfers between devices, per_device(): two = lax.ppermute(here_two, axes, hops[turn % 2])  3.69 us
    ppermute x1, starting transfers between devices, per_device(): one = lax.ppermute(patches, axes, hops[0])  2.63 us
    ppermute x1, starting transfers between devices, per_device(): two = lax.ppermute(other, axes, hops[0])  2.12 us
    ppermute x3, waiting for transfers between devices, per_device(): one = lax.ppermute(here_one, axes, hops[turn % 2])  0.7 us
  transfers between devices with their start and end apart: 10, of which 3 were waited for; matrix products, arithmetic and copies ran while one was open for 0% of the time, Pallas kernels for 42%

profile of v8, /device:TPU:0, one launch (start us, length us, event | category | flops | bytes accessed | tf_op | source)
XLA Modules:
  0.0 31.3 jit_solution(3918142479047528030)
XLA Ops:
  0.0 0.5 %collective-permute-start = (bf16[128,1024]{1,0:T(8,128)(2,1)}, bf16[128,1024]{1,0:T(8,128)(2,1)S(1)}, u32[]{:S(2)}, u32[]{:S(2)}) collective-permute-start(bf16[128,1024]{1,0:T(8,128)(2,1)} %own_ref.1), channel_id=1, source_target_pairs={{0,8},{8,0},{1,9},{9,1},{2,10},{10,2},{3,11},{11,3},{4,12},{12,4},... | collective-permute-start | bytes 786440 | tf_op jit(solution)/shard_map/ppermute | solution.py:314
  0.5 2.6 %collective-permute-start.1 = (bf16[128,1024]{1,0:T(8,128)(2,1)}, bf16[128,1024]{1,0:T(8,128)(2,1)S(1)}, u32[]{:S(2)}, u32[]{:S(2)}) collective-permute-start(bf16[128,1024]{1,0:T(8,128)(2,1)} %own_ref.1), channel_id=1, source_target_pairs={{8,2},{0,9},{9,0},{1,11},{10,4},{2,8},{11,1},{3,13},{12,6},{4,10},... | collective-permute-start | bytes 786440 | tf_op jit(solution)/shard_map/ppermute | solution.py:313
  3.2 0.4 %shard_map.56 = (bf16[128,1024]{1,0:T(8,128)(2,1)S(1)}, bf16[128,1024]{1,0:T(8,128)(2,1)S(1)}) custom-call(bf16[128,1024]{1,0:T(8,128)(2,1)S(1)} %copy-done.4, bf16[128,1024]{1,0:T(8,128)(2,1)S(1)} %collective-permute-done.sibling_ref, f32[1,1024]{1,0:T(1,128)S(1)} %bitcast.1, bf16[1024,3072]{1,0:T(8,128)(2,1)S(1)} %copy-done), custom_call_target="tpu_custom_call" | custom-call | bytes 7344128 | tf_op jit(solution)/shard_map/pallas_call | solution.py:284
  3.6 2.1 %collective-permute-start.2 = (bf16[128,1024]{1,0:T(8,128)(2,1)S(1)}, bf16[128,1024]{1,0:T(8,128)(2,1)S(1)}, u32[]{:S(2)}, u32[]{:S(2)}) collective-permute-start(bf16[128,1024]{1,0:T(8,128)(2,1)S(1)} %get-tuple-element.62.sibling_ref), channel_id=1, source_target_pairs={{8,2},{0,9},{9,0},{1,11},{10,4},{2,8},{11,1},{3,13},{12,6},{4,10},... | collective-permute-start | bytes 786440 | tf_op jit(solution)/shard_map/ppermute | solution.py:323
  5.7 1.1 %shard_map.57.refs_5_.refs_6_.q_ref = bf16[1024,256]{1,0:T(8,128)(2,1)S(1)} custom-call(bf16[128,1024]{1,0:T(8,128)(2,1)S(1)} %get-tuple-element.60.own_ref.refs_0_, bf16[128,1024]{1,0:T(8,128)(2,1)S(1)} %get-tuple-element.62.sibling_ref, bf16[1024,3072]{1,0:T(8,128)(2,1)S(1)} %copy-done, f32[2,1024]{1,0:T(2,128)S(1)} %copy-done.2, ...), custom_call_target="tpu_custom_call" | custom-call | flops 536870912 | bytes 7479296 | tf_op jit(solution)/shard_map/pallas_call | solution.py:284
  6.8 0.6 %collective-permute-done.1.refs_0_ = bf16[128,1024]{1,0:T(8,128)(2,1)S(1)} collective-permute-done((bf16[128,1024]{1,0:T(8,128)(2,1)}, bf16[128,1024]{1,0:T(8,128)(2,1)S(1)}, u32[]{:S(2)}, u32[]{:S(2)}) %collective-permute-start.1) | collective-permute-done | bytes 262176 | tf_op jit(solution)/shard_map/ppermute | solution.py:313
  7.4 2.1 %collective-permute-start.3 = (bf16[128,1024]{1,0:T(8,128)(2,1)S(1)}, bf16[128,1024]{1,0:T(8,128)(2,1)S(1)}, u32[]{:S(2)}, u32[]{:S(2)}) collective-permute-start(bf16[128,1024]{1,0:T(8,128)(2,1)S(1)} %collective-permute-done.1.refs_0_), channel_id=1, source_target_pairs={{0,10},{8,1},{1,8},{9,3},{2,12},{10,0},{3,9},{11,5},{4,14},{12,2},... | collective-permute-start | bytes 786440 | tf_op jit(solution)/shard_map/ppermute | solution.py:351
  9.5 1.5 %shard_map.58 = (f32[16,256]{1,0:T(8,128)S(1)}, f32[16,256]{1,0:T(8,128)S(1)}, f32[1024,256]{1,0:T(8,128)S(1)}) custom-call(bf16[128,1024]{1,0:T(8,128)(2,1)S(1)} %get-tuple-element.60.own_ref.refs_0_, bf16[1024,3072]{1,0:T(8,128)(2,1)S(1)} %copy-done, f32[1,1024]{1,0:T(1,128)S(1)} %bitcast.2, f32[2,1024]{1,0:T(2,128)S(1)} %copy-done.2, ...), custom_call_target="tpu_custom_call" | custom-call | flops 671088640 | bytes 8302592 | tf_op jit(solution)/shard_map/pallas_call | solution.py:284
  11.0 1.5 %collective-permute-start.4 = (bf16[128,1024]{1,0:T(8,128)(2,1)S(1)}, bf16[128,1024]{1,0:T(8,128)(2,1)S(1)}, u32[]{:S(2)}, u32[]{:S(2)}) collective-permute-start(bf16[128,1024]{1,0:T(8,128)(2,1)S(1)} %collective-permute-done.2.refs_0_), channel_id=1, source_target_pairs={{0,10},{8,1},{1,8},{9,3},{2,12},{10,0},{3,9},{11,5},{4,14},{12,2},... | collective-permute-start | bytes 786440 | tf_op jit(solution)/shard_map/ppermute | solution.py:354
  12.5 1.7 %shard_map.59 = (f32[16,256]{1,0:T(8,128)S(1)}, f32[16,256]{1,0:T(8,128)S(1)}, f32[1024,256]{1,0:T(8,128)S(1)}) custom-call(bf16[128,1024]{1,0:T(8,128)(2,1)S(1)} %collective-permute-done.1.refs_0_, bf16[1024,3072]{1,0:T(8,128)(2,1)S(1)} %copy-done, f32[1,1024]{1,0:T(1,128)S(1)} %bitcast.3, f32[2,1024]{1,0:T(2,128)S(1)} %copy-done.2, ...), custom_call_target="tpu_custom_call" | custom-call | flops 671088640 | bytes 9383936 | tf_op jit(solution)/shard_map/pallas_call | solution.py:284
  14.3 1.3 %collective-permute-start.5 = (bf16[128,1024]{1,0:T(8,128)(2,1)S(1)}, bf16[128,1024]{1,0:T(8,128)(2,1)S(1)}, u32[]{:S(2)}, u32[]{:S(2)}) collective-permute-start(bf16[128,1024]{1,0:T(8,128)(2,1)S(1)} %collective-permute-done.3.refs_0_), channel_id=1, source_target_pairs={{8,2},{0,9},{9,0},{1,11},{10,4},{2,8},{11,1},{3,13},{12,6},{4,10},... | collective-permute-start | bytes 786440 | tf_op jit(solution)/shard_map/ppermute | solution.py:351
  15.6 1.5 %shard_map.60 = (f32[16,256]{1,0:T(8,128)S(1)}, f32[16,256]{1,0:T(8,128)S(1)}, f32[1024,256]{1,0:T(8,128)S(1)}) custom-call(bf16[128,1024]{1,0:T(8,128)(2,1)S(1)} %collective-permute-done.2.refs_0_, bf16[1024,3072]{1,0:T(8,128)(2,1)S(1)} %copy-done, f32[1,1024]{1,0:T(1,128)S(1)} %bitcast.4, f32[2,1024]{1,0:T(2,128)S(1)} %copy-done.2, ...), custom_call_target="tpu_custom_call" | custom-call | flops 671088640 | bytes 9383936 | tf_op jit(solution)/shard_map/pallas_call | solution.py:284
  17.1 2.2 %collective-permute-start.6 = (bf16[128,1024]{1,0:T(8,128)(2,1)S(1)}, bf16[128,1024]{1,0:T(8,128)(2,1)S(1)}, u32[]{:S(2)}, u32[]{:S(2)}) collective-permute-start(bf16[128,1024]{1,0:T(8,128)(2,1)S(1)} %collective-permute-done.4.refs_0_), channel_id=1, source_target_pairs={{8,2},{0,9},{9,0},{1,11},{10,4},{2,8},{11,1},{3,13},{12,6},{4,10},... | collective-permute-start | bytes 786440 | tf_op jit(solution)/shard_map/ppermute | solution.py:354
  19.3 1.7 %shard_map.61 = (f32[16,256]{1,0:T(8,128)S(1)}, f32[16,256]{1,0:T(8,128)S(1)}, f32[1024,256]{1,0:T(8,128)S(1)}) custom-call(bf16[128,1024]{1,0:T(8,128)(2,1)S(1)} %collective-permute-done.3.refs_0_, bf16[1024,3072]{1,0:T(8,128)(2,1)S(1)} %copy-done, f32[1,1024]{1,0:T(1,128)S(1)} %bitcast.5, f32[2,1024]{1,0:T(2,128)S(1)} %copy-done.2, ...), custom_call_target="tpu_custom_call" | custom-call | flops 671088640 | bytes 9383936 | tf_op jit(solution)/shard_map/pallas_call | solution.py:284
  21.0 0.7 %collective-permute-start.7 = (bf16[128,1024]{1,0:T(8,128)(2,1)S(1)}, bf16[128,1024]{1,0:T(8,128)(2,1)S(1)}, u32[]{:S(2)}, u32[]{:S(2)}) collective-permute-start(bf16[128,1024]{1,0:T(8,128)(2,1)S(1)} %collective-permute-done.5.refs_1_), channel_id=1, source_target_pairs={{0,10},{8,1},{1,8},{9,3},{2,12},{10,0},{3,9},{11,5},{4,14},{12,2},... | collective-permute-start | bytes 786440 | tf_op jit(solution)/shard_map/ppermute | solution.py:351
  21.7 2.9 %shard_map.62 = (f32[16,256]{1,0:T(8,128)S(1)}, f32[16,256]{1,0:T(8,128)S(1)}, f32[1024,256]{1,0:T(8,128)S(1)}) custom-call(bf16[128,1024]{1,0:T(8,128)(2,1)S(1)} %collective-permute-done.4.refs_0_, bf16[128,1024]{1,0:T(8,128)(2,1)S(1)} %collective-permute-done.5.refs_1_, bf16[1024,3072]{1,0:T(8,128)(2,1)S(1)} %copy-done, f32[1,1024]{1,0:T(1,128)S(1)} %bitcast.6, ...), custom_call_target="tpu_custom_call" | custom-call | flops 1342177280 | bytes 9646080 | tf_op jit(solution)/shard_map/pallas_call | solution.py:284
  24.6 1.5 %shard_map.63 = (f32[16,256]{1,0:T(8,128)S(1)}, f32[16,256]{1,0:T(8,128)S(1)}, f32[1024,256]{1,0:T(8,128)S(1)}) custom-call(bf16[128,1024]{1,0:T(8,128)(2,1)S(1)} %collective-permute-done.6.refs_0_, bf16[1024,3072]{1,0:T(8,128)(2,1)S(1)} %copy-done, f32[1,1024]{1,0:T(1,128)S(1)} %bitcast.7, f32[2,1024]{1,0:T(2,128)S(1)} %copy-done.2, ...), custom_call_target="tpu_custom_call" | custom-call | flops 671088640 | bytes 9383936 | tf_op jit(solution)/shard_map/pallas_call | solution.py:284
  26.2 0.7 %collective-permute-done.7.block_ref = bf16[128,1024]{1,0:T(8,128)(2,1)S(1)} collective-permute-done((bf16[128,1024]{1,0:T(8,128)(2,1)S(1)}, bf16[128,1024]{1,0:T(8,128)(2,1)S(1)}, u32[]{:S(2)}, u32[]{:S(2)}) %collective-permute-start.7) | collective-permute-done | bytes 262176 | tf_op jit(solution)/shard_map/ppermute | solution.py:351
  26.9 1.5 %shard_map.64 = (bf16[1024,128]{1,0:T(8,128)(2,1)S(1)}, f32[32,128]{1,0:T(8,128)S(1)}, bf16[128,1024]{1,0:T(8,128)(2,1)S(1)}, bf16[1024,128]{1,0:T(8,128)(2,1)S(1)}) custom-call(bf16[128,1024]{1,0:T(8,128)(2,1)S(1)} %collective-permute-done.7.block_ref, bf16[1024,3072]{1,0:T(8,128)(2,1)S(1)} %copy-done, f32[1,1024]{1,0:T(1,128)S(1)} %bitcast.8, ...), custom_call_target="tpu_custom_call" | custom-call | flops 671088640 | bytes 9105408 | tf_op jit(solution)/shard_map/pallas_call | solution.py:284
  28.4 0.5 %collective-permute-start.8 = (bf16[1024,128]{1,0:T(8,128)(2,1)S(1)}, bf16[1024,128]{1,0:T(8,128)(2,1)S(1)}, u32[]{:S(2)}, u32[]{:S(2)}) collective-permute-start(bf16[1024,128]{1,0:T(8,128)(2,1)S(1)} %get-tuple-element.110), channel_id=1, source_target_pairs={{0,8},{8,0},{1,9},{9,1},{2,10},{10,2},{3,11},{11,3},{4,12},{12,4},... | collective-permute-start | bytes 786440 | tf_op jit(solution)/shard_map/ppermute | solution.py:371
  28.9 0.1 collective-permute-start.9
  29.0 0.7 %shard_map.65 = (f32[1024,128]{1,0:T(8,128)S(1)}, f32[32,128]{1,0:T(8,128)S(1)}) custom-call(bf16[128,1024]{1,0:T(8,128)(2,1)S(1)} %get-tuple-element.107.keys_ref, bf16[1024,128]{1,0:T(8,128)(2,1)S(1)} %get-tuple-element.108.values_ref, bf16[1024,256]{1,0:T(8,128)(2,1)S(1)} %shard_map.57.refs_5_.refs_6_.q_ref, f32[16,256]{1,0:T(8,128)S(1)} %get-tuple-element.104.max_ref, ...), custom_call_target="tpu_custom_call" | custom-call | flops 167772160 | bytes 2670592 | tf_op jit(solution)/shard_map/pallas_call | solution.py:284
  29.7 0.4 %collective-permute-done.9.their_state_ref = f32[32,128]{1,0:T(8,128)S(1)} collective-permute-done((f32[32,128]{1,0:T(8,128)S(1)}, f32[32,128]{1,0:T(8,128)S(1)}, u32[]{:S(2)}, u32[]{:S(2)}) %collective-permute-start.9) | collective-permute-done | bytes 16416 | tf_op jit(solution)/shard_map/ppermute | solution.py:372
  30.1 1.2 %shard_map.66 = bf16[128,1024]{1,0:T(8,128)(2,1)} custom-call(f32[1024,128]{1,0:T(8,128)S(1)} %get-tuple-element.109.mine_ref, bf16[1024,128]{1,0:T(8,128)(2,1)S(1)} %collective-permute-done.8.theirs_ref, f32[32,128]{1,0:T(8,128)S(1)} %get-tuple-element.111.my_state_ref, f32[32,128]{1,0:T(8,128)S(1)} %collective-permute-done.9.their_state_ref, ...), custom_call_target="tpu_custom_call" | custom-call | flops 268435456 | bytes 3178496 | tf_op jit(solution)/shard_map/pallas_call | solution.py:284
  (18 shorter events, 0.1 us)
Async XLA Ops:
  0.0 3.2 %copy-start.4 = (bf16[128,1024]{1,0:T(8,128)(2,1)S(1)}, bf16[128,1024]{1,0:T(8,128)(2,1)}, u32[]{:S(2)}) copy-start(bf16[128,1024]{1,0:T(8,128)(2,1)} %own_ref.1) | copy-start | bytes 786436
  0.0 3.2 %copy-start.3 = (f32[1024]{0:T(1024)S(1)}, f32[1024]{0:T(1024)}, u32[]{:S(2)}) copy-start(f32[1024]{0:T(1024)} %param.6) | copy-start | bytes 12292
  0.0 3.2 %copy-start = (bf16[1024,3072]{1,0:T(8,128)(2,1)S(1)}, bf16[1024,3072]{1,0:T(8,128)(2,1)}, u32[]{:S(2)}) copy-start(bf16[1024,3072]{1,0:T(8,128)(2,1)} %w_ref.6) | copy-start | bytes 18874372
  0.0 3.2 %collective-permute-start = (bf16[128,1024]{1,0:T(8,128)(2,1)}, bf16[128,1024]{1,0:T(8,128)(2,1)S(1)}, u32[]{:S(2)}, u32[]{:S(2)}) collective-permute-start(bf16[128,1024]{1,0:T(8,128)(2,1)} %own_ref.1), channel_id=1, source_target_pairs={{0,8},{8,0},{1,9},{9,1},{2,10},{10,2},{3,11},{11,3},{4,12},{12,4},... | collective-permute-start | bytes 786440 | tf_op jit(solution)/shard_map/ppermute | solution.py:314
  0.5 6.9 %collective-permute-start.1 = (bf16[128,1024]{1,0:T(8,128)(2,1)}, bf16[128,1024]{1,0:T(8,128)(2,1)S(1)}, u32[]{:S(2)}, u32[]{:S(2)}) collective-permute-start(bf16[128,1024]{1,0:T(8,128)(2,1)} %own_ref.1), channel_id=1, source_target_pairs={{8,2},{0,9},{9,0},{1,11},{10,4},{2,8},{11,1},{3,13},{12,6},{4,10},... | collective-permute-start | bytes 786440 | tf_op jit(solution)/shard_map/ppermute | solution.py:313
  3.2 2.5 %copy-start.2 = (f32[2,1024]{1,0:T(2,128)S(1)}, f32[2,1024]{1,0:T(2,128)}, u32[]{:S(2)}) copy-start(f32[2,1024]{1,0:T(2,128)} %gains_ref.3) | copy-start | bytes 24580
  3.6 7.4 %collective-permute-start.2 = (bf16[128,1024]{1,0:T(8,128)(2,1)S(1)}, bf16[128,1024]{1,0:T(8,128)(2,1)S(1)}, u32[]{:S(2)}, u32[]{:S(2)}) collective-permute-start(bf16[128,1024]{1,0:T(8,128)(2,1)S(1)} %get-tuple-element.62.sibling_ref), channel_id=1, source_target_pairs={{8,2},{0,9},{9,0},{1,11},{10,4},{2,8},{11,1},{3,13},{12,6},{4,10},... | collective-permute-start | bytes 786440 | tf_op jit(solution)/shard_map/ppermute | solution.py:323
  7.4 6.8 %collective-permute-start.3 = (bf16[128,1024]{1,0:T(8,128)(2,1)S(1)}, bf16[128,1024]{1,0:T(8,128)(2,1)S(1)}, u32[]{:S(2)}, u32[]{:S(2)}) collective-permute-start(bf16[128,1024]{1,0:T(8,128)(2,1)S(1)} %collective-permute-done.1.refs_0_), channel_id=1, source_target_pairs={{0,10},{8,1},{1,8},{9,3},{2,12},{10,0},{3,9},{11,5},{4,14},{12,2},... | collective-permute-start | bytes 786440 | tf_op jit(solution)/shard_map/ppermute | solution.py:351
  11.0 6.1 %collective-permute-start.4 = (bf16[128,1024]{1,0:T(8,128)(2,1)S(1)}, bf16[128,1024]{1,0:T(8,128)(2,1)S(1)}, u32[]{:S(2)}, u32[]{:S(2)}) collective-permute-start(bf16[128,1024]{1,0:T(8,128)(2,1)S(1)} %collective-permute-done.2.refs_0_), channel_id=1, source_target_pairs={{0,10},{8,1},{1,8},{9,3},{2,12},{10,0},{3,9},{11,5},{4,14},{12,2},... | collective-permute-start | bytes 786440 | tf_op jit(solution)/shard_map/ppermute | solution.py:354
  14.3 6.8 %collective-permute-start.5 = (bf16[128,1024]{1,0:T(8,128)(2,1)S(1)}, bf16[128,1024]{1,0:T(8,128)(2,1)S(1)}, u32[]{:S(2)}, u32[]{:S(2)}) collective-permute-start(bf16[128,1024]{1,0:T(8,128)(2,1)S(1)} %collective-permute-done.3.refs_0_), channel_id=1, source_target_pairs={{8,2},{0,9},{9,0},{1,11},{10,4},{2,8},{11,1},{3,13},{12,6},{4,10},... | collective-permute-start | bytes 786440 | tf_op jit(solution)/shard_map/ppermute | solution.py:351
  17.1 7.5 %collective-permute-start.6 = (bf16[128,1024]{1,0:T(8,128)(2,1)S(1)}, bf16[128,1024]{1,0:T(8,128)(2,1)S(1)}, u32[]{:S(2)}, u32[]{:S(2)}) collective-permute-start(bf16[128,1024]{1,0:T(8,128)(2,1)S(1)} %collective-permute-done.4.refs_0_), channel_id=1, source_target_pairs={{8,2},{0,9},{9,0},{1,11},{10,4},{2,8},{11,1},{3,13},{12,6},{4,10},... | collective-permute-start | bytes 786440 | tf_op jit(solution)/shard_map/ppermute | solution.py:354
  21.0 5.9 %collective-permute-start.7 = (bf16[128,1024]{1,0:T(8,128)(2,1)S(1)}, bf16[128,1024]{1,0:T(8,128)(2,1)S(1)}, u32[]{:S(2)}, u32[]{:S(2)}) collective-permute-start(bf16[128,1024]{1,0:T(8,128)(2,1)S(1)} %collective-permute-done.5.refs_1_), channel_id=1, source_target_pairs={{0,10},{8,1},{1,8},{9,3},{2,12},{10,0},{3,9},{11,5},{4,14},{12,2},... | collective-permute-start | bytes 786440 | tf_op jit(solution)/shard_map/ppermute | solution.py:351
  26.2 3.9 %copy-start.1 = (bf16[1024,1024]{1,0:T(8,128)(2,1)S(1)}, bf16[1024,1024]{1,0:T(8,128)(2,1)}, u32[]{:S(2)}) copy-start(bf16[1024,1024]{1,0:T(8,128)(2,1)} %w_ref.7) | copy-start | bytes 6291460
  28.4 1.7 %collective-permute-start.8 = (bf16[1024,128]{1,0:T(8,128)(2,1)S(1)}, bf16[1024,128]{1,0:T(8,128)(2,1)S(1)}, u32[]{:S(2)}, u32[]{:S(2)}) collective-permute-start(bf16[1024,128]{1,0:T(8,128)(2,1)S(1)} %get-tuple-element.110), channel_id=1, source_target_pairs={{0,8},{8,0},{1,9},{9,1},{2,10},{10,2},{3,11},{11,3},{4,12},{12,4},... | collective-permute-start | bytes 786440 | tf_op jit(solution)/shard_map/ppermute | solution.py:371
  28.9 1.2 %collective-permute-start.9 = (f32[32,128]{1,0:T(8,128)S(1)}, f32[32,128]{1,0:T(8,128)S(1)}, u32[]{:S(2)}, u32[]{:S(2)}) collective-permute-start(f32[32,128]{1,0:T(8,128)S(1)} %get-tuple-element.112), channel_id=1, source_target_pairs={{0,8},{8,0},{1,9},{9,1},{2,10},{10,2},{3,11},{11,3},{4,12},{12,4},... | collective-permute-start | bytes 49160 | tf_op jit(solution)/shard_map/ppermute | solution.py:372

commit v9 on v8

--- a/solution.py
+++ b/solution.py
@@ -161,6 +161,13 @@
     outs[1][...] = total
 
 
+def parted(values):
+    high = values.astype(BF16)
+    rest = values - high.astype(F32)
+    middle = rest.astype(BF16)
+    return high, middle, (rest - middle.astype(F32)).astype(BF16)
+
+
 def half_stages(held, part, q_ref, max_ref, sum_ref, acc_ref, put):
     old_max, old_sum = max_ref[:, part], sum_ref[:, part]
     half = old_max.shape[1]
@@ -213,7 +220,7 @@
 
 def send_kernel(
     block_ref, w_ref, gain_ref, gains_ref, ones_ref, q_ref, max_ref, sum_ref, acc_ref,
-    sent_ref, sent_state_ref, keys_ref, values_ref,
+    sent_ref, keys_ref, values_ref,
 ):
     width, queries = q_ref.shape
     block = normalised(block_ref[...], gain_ref[...])
@@ -237,8 +244,8 @@
     stages, maxima, sums = half_stages(held, part, q_ref, max_ref, sum_ref, acc_ref, put)
     pipeline((project, norm, *stages), width // SPAN)
     top, total = jnp.concatenate(maxima, axis=0), jnp.concatenate(sums, axis=0)
-    sent_state_ref[:H, :] = top
-    sent_state_ref[H:, :] = total
+    for i, piece in enumerate((*parted(top), *parted(total))):
+        sent_ref[width + i * H : width + (i + 1) * H, :] = piece
 
 
 def keep_kernel(
@@ -260,12 +267,13 @@
     state_ref[H:, :] = jnp.concatenate(sums, axis=0)
 
 
-def finish_kernel(mine_ref, theirs_ref, my_state_ref, their_state_ref, w_ref, out_ref):
+def finish_kernel(mine_ref, my_state_ref, theirs_ref, w_ref, out_ref):
     width = mine_ref.shape[0]
-    top = jnp.maximum(my_state_ref[:H, :], their_state_ref[:H, :])
-    mine = jnp.exp2(my_state_ref[:H, :] - top)
-    theirs = jnp.exp2(their_state_ref[:H, :] - top)
-    total = my_state_ref[H:, :] * mine + their_state_ref[H:, :] * theirs
+    pieces = [theirs_ref[at : at + H, :].astype(F32) for at in range(width, theirs_ref.shape[0], H)]
+    their_top, their_total = sum(pieces[1:3], pieces[0]), sum(pieces[4:6], pieces[3])
+    top = jnp.maximum(my_state_ref[:H, :], their_top)
+    mine, theirs = jnp.exp2(my_state_ref[:H, :] - top), jnp.exp2(their_top - top)
+    total = my_state_ref[H:, :] * mine + their_total * theirs
     mine, theirs = mine / total, theirs / total
     spans = []
     for at in range(0, width, SPAN):
@@ -352,24 +360,18 @@
         if turn < count // 2 - 1:
             state, here_two = tie((take([late], state), here_two))
             two = lax.ppermute(here_two, axes, hops[turn % 2])
-            state, one = tie((take([(here_one, True)], state), one))
-            late = here_two, False
+            state, one = tie((take([(here_two, False)], state), one))
+            late = here_one, True
     state, here_two = tie((take([late, (here_one, True)], state), here_two))
     state, one = tie((take([(here_two, False)], state), one))
-    sent, sent_state, keys, values = call(
+    sent, keys, values = call(
         send_kernel,
-        [
-            shape((width, rows), BF16),
-            shape((2 * H, rows), F32),
-            shape((rows, width), BF16),
-            shape((width, rows), BF16),
-        ],
+        [shape((width + 6 * H, rows), BF16), shape((rows, width), BF16), shape((width, rows), BF16)],
         (one, w_qkv, gain, qk_gains, ones, query, *state),
         flops,
         H * rows * rows,
     )
-    theirs = lax.ppermute(sent, "head", swap)
-    their_state = lax.ppermute(sent_state, "head", swap)
+    came = lax.ppermute(sent, "head", swap)
     mine, my_state = call(
         keep_kernel,
         [shape((width, rows), F32), shape((2 * H, rows), F32)],
@@ -380,7 +382,7 @@
     return call(
         finish_kernel,
         [shape((rows, width), BF16)],
-        (mine, theirs, my_state, their_state, w_out),
+        (mine, my_state, came, w_out),
         2 * rows * width * width,
     )[0]
 

time: 31.5 us -> 31.4 us (level)
    ppermute x3, starting transfers between devices: 4.06 us -> 4.45 us  [per_device(): one = lax.ppermute(here_one, axes, hops[turn % 2])]
    ppermute x3, waiting for transfers between devices: 0.7 us -> 0.37 us  [per_device(): one = lax.ppermute(here_one, axes, hops[turn % 2])]
  transfers between devices with their start and end apart: 10 -> 9, of which waited for: 3 -> 3; matrix products, arithmetic and copies ran while one was open for 0% -> 0% of each run, Pallas kernels for 42% -> 41%
where the time goes in v9:
time: 31.4 us; the launch traced here: 31.3 us
  Pallas kernels  15.8 us (50%)
  starting transfers between devices  13.8 us (44%)
  waiting for transfers between devices  1.51 us (5%)
    pallas_call x12, Pallas kernels, call(): pl.pallas_call(body, out_shape=outs, in_specs=[VMEM] * len(operands), out...  15.8 us
    ppermute x3, starting transfers between devices, per_device(): one = lax.ppermute(here_one, axes, hops[turn % 2])  4.45 us
    ppermute x2, starting transfers between devices, per_device(): two = lax.ppermute(here_two, axes, hops[turn % 2])  3.5 us
    ppermute x1, starting transfers between devices, per_device(): one = lax.ppermute(patches, axes, hops[0])  2.63 us
    ppermute x1, starting transfers between devices, per_device(): two = lax.ppermute(other, axes, hops[0])  2.12 us
  transfers between devices with their start and end apart: 9, of which 3 were waited for; matrix products, arithmetic and copies ran while one was open for 0% of the time, Pallas kernels for 41%

profile of v9, /device:TPU:0, one launch (start us, length us, event | category | flops | bytes accessed | tf_op | source)
XLA Modules:
  0.0 31.3 jit_solution(14639808945047483848)
XLA Ops:
  0.0 0.5 %collective-permute-start = (bf16[128,1024]{1,0:T(8,128)(2,1)}, bf16[128,1024]{1,0:T(8,128)(2,1)S(1)}, u32[]{:S(2)}, u32[]{:S(2)}) collective-permute-start(bf16[128,1024]{1,0:T(8,128)(2,1)} %own_ref.1), channel_id=1, source_target_pairs={{0,8},{8,0},{1,9},{9,1},{2,10},{10,2},{3,11},{11,3},{4,12},{12,4},... | collective-permute-start | bytes 786440 | tf_op jit(solution)/shard_map/ppermute | solution.py:322
  0.5 2.6 %collective-permute-start.1 = (bf16[128,1024]{1,0:T(8,128)(2,1)}, bf16[128,1024]{1,0:T(8,128)(2,1)S(1)}, u32[]{:S(2)}, u32[]{:S(2)}) collective-permute-start(bf16[128,1024]{1,0:T(8,128)(2,1)} %own_ref.1), channel_id=1, source_target_pairs={{8,2},{0,9},{9,0},{1,11},{10,4},{2,8},{11,1},{3,13},{12,6},{4,10},... | collective-permute-start | bytes 786440 | tf_op jit(solution)/shard_map/ppermute | solution.py:321
  3.2 0.0 copy-start.2
  3.2 0.4 %shard_map.56 = (bf16[128,1024]{1,0:T(8,128)(2,1)S(1)}, bf16[128,1024]{1,0:T(8,128)(2,1)S(1)}) custom-call(bf16[128,1024]{1,0:T(8,128)(2,1)S(1)} %copy-done.4, bf16[128,1024]{1,0:T(8,128)(2,1)S(1)} %collective-permute-done.sibling_ref, f32[1,1024]{1,0:T(1,128)S(1)} %bitcast.1, bf16[1024,3072]{1,0:T(8,128)(2,1)S(1)} %copy-done), custom_call_target="tpu_custom_call" | custom-call | bytes 7344128 | tf_op jit(solution)/shard_map/pallas_call | solution.py:292
  3.6 2.1 %collective-permute-start.2 = (bf16[128,1024]{1,0:T(8,128)(2,1)S(1)}, bf16[128,1024]{1,0:T(8,128)(2,1)S(1)}, u32[]{:S(2)}, u32[]{:S(2)}) collective-permute-start(bf16[128,1024]{1,0:T(8,128)(2,1)S(1)} %get-tuple-element.61.sibling_ref), channel_id=1, source_target_pairs={{8,2},{0,9},{9,0},{1,11},{10,4},{2,8},{11,1},{3,13},{12,6},{4,10},... | collective-permute-start | bytes 786440 | tf_op jit(solution)/shard_map/ppermute | solution.py:331
  5.7 1.1 %shard_map.57.refs_5_.refs_6_.q_ref = bf16[1024,256]{1,0:T(8,128)(2,1)S(1)} custom-call(bf16[128,1024]{1,0:T(8,128)(2,1)S(1)} %get-tuple-element.59.own_ref.refs_0_, bf16[128,1024]{1,0:T(8,128)(2,1)S(1)} %get-tuple-element.61.sibling_ref, bf16[1024,3072]{1,0:T(8,128)(2,1)S(1)} %copy-done, f32[2,1024]{1,0:T(2,128)S(1)} %copy-done.2, ...), custom_call_target="tpu_custom_call" | custom-call | flops 536870912 | bytes 7479296 | tf_op jit(solution)/shard_map/pallas_call | solution.py:292
  6.8 0.6 %collective-permute-done.1.refs_0_ = bf16[128,1024]{1,0:T(8,128)(2,1)S(1)} collective-permute-done((bf16[128,1024]{1,0:T(8,128)(2,1)}, bf16[128,1024]{1,0:T(8,128)(2,1)S(1)}, u32[]{:S(2)}, u32[]{:S(2)}) %collective-permute-start.1) | collective-permute-done | bytes 262176 | tf_op jit(solution)/shard_map/ppermute | solution.py:321
  7.4 2.1 %collective-permute-start.3 = (bf16[128,1024]{1,0:T(8,128)(2,1)S(1)}, bf16[128,1024]{1,0:T(8,128)(2,1)S(1)}, u32[]{:S(2)}, u32[]{:S(2)}) collective-permute-start(bf16[128,1024]{1,0:T(8,128)(2,1)S(1)} %collective-permute-done.1.refs_0_), channel_id=1, source_target_pairs={{0,10},{8,1},{1,8},{9,3},{2,12},{10,0},{3,9},{11,5},{4,14},{12,2},... | collective-permute-start | bytes 786440 | tf_op jit(solution)/shard_map/ppermute | solution.py:359
  9.5 1.5 %shard_map.58 = (f32[16,256]{1,0:T(8,128)S(1)}, f32[16,256]{1,0:T(8,128)S(1)}, f32[1024,256]{1,0:T(8,128)S(1)}) custom-call(bf16[128,1024]{1,0:T(8,128)(2,1)S(1)} %get-tuple-element.59.own_ref.refs_0_, bf16[1024,3072]{1,0:T(8,128)(2,1)S(1)} %copy-done, f32[1,1024]{1,0:T(1,128)S(1)} %bitcast.2, f32[2,1024]{1,0:T(2,128)S(1)} %copy-done.2, ...), custom_call_target="tpu_custom_call" | custom-call | flops 671088640 | bytes 8302592 | tf_op jit(solution)/shard_map/pallas_call | solution.py:292
  11.0 1.5 %collective-permute-start.4 = (bf16[128,1024]{1,0:T(8,128)(2,1)S(1)}, bf16[128,1024]{1,0:T(8,128)(2,1)S(1)}, u32[]{:S(2)}, u32[]{:S(2)}) collective-permute-start(bf16[128,1024]{1,0:T(8,128)(2,1)S(1)} %collective-permute-done.2.refs_0_), channel_id=1, source_target_pairs={{0,10},{8,1},{1,8},{9,3},{2,12},{10,0},{3,9},{11,5},{4,14},{12,2},... | collective-permute-start | bytes 786440 | tf_op jit(solution)/shard_map/ppermute | solution.py:362
  12.5 1.5 %shard_map.59 = (f32[16,256]{1,0:T(8,128)S(1)}, f32[16,256]{1,0:T(8,128)S(1)}, f32[1024,256]{1,0:T(8,128)S(1)}) custom-call(bf16[128,1024]{1,0:T(8,128)(2,1)S(1)} %collective-permute-done.2.refs_0_, bf16[1024,3072]{1,0:T(8,128)(2,1)S(1)} %copy-done, f32[1,1024]{1,0:T(1,128)S(1)} %bitcast.3, f32[2,1024]{1,0:T(2,128)S(1)} %copy-done.2, ...), custom_call_target="tpu_custom_call" | custom-call | flops 671088640 | bytes 9383936 | tf_op jit(solution)/shard_map/pallas_call | solution.py:292
  14.1 1.5 %collective-permute-start.5 = (bf16[128,1024]{1,0:T(8,128)(2,1)S(1)}, bf16[128,1024]{1,0:T(8,128)(2,1)S(1)}, u32[]{:S(2)}, u32[]{:S(2)}) collective-permute-start(bf16[128,1024]{1,0:T(8,128)(2,1)S(1)} %collective-permute-done.3.refs_0_), channel_id=1, source_target_pairs={{8,2},{0,9},{9,0},{1,11},{10,4},{2,8},{11,1},{3,13},{12,6},{4,10},... | collective-permute-start | bytes 786440 | tf_op jit(solution)/shard_map/ppermute | solution.py:359
  15.6 1.7 %shard_map.60 = (f32[16,256]{1,0:T(8,128)S(1)}, f32[16,256]{1,0:T(8,128)S(1)}, f32[1024,256]{1,0:T(8,128)S(1)}) custom-call(bf16[128,1024]{1,0:T(8,128)(2,1)S(1)} %collective-permute-done.1.refs_0_, bf16[1024,3072]{1,0:T(8,128)(2,1)S(1)} %copy-done, f32[1,1024]{1,0:T(1,128)S(1)} %bitcast.4, f32[2,1024]{1,0:T(2,128)S(1)} %copy-done.2, ...), custom_call_target="tpu_custom_call" | custom-call | flops 671088640 | bytes 9383936 | tf_op jit(solution)/shard_map/pallas_call | solution.py:292
  17.3 2.0 %collective-permute-start.6 = (bf16[128,1024]{1,0:T(8,128)(2,1)S(1)}, bf16[128,1024]{1,0:T(8,128)(2,1)S(1)}, u32[]{:S(2)}, u32[]{:S(2)}) collective-permute-start(bf16[128,1024]{1,0:T(8,128)(2,1)S(1)} %collective-permute-done.4.refs_0_), channel_id=1, source_target_pairs={{8,2},{0,9},{9,0},{1,11},{10,4},{2,8},{11,1},{3,13},{12,6},{4,10},... | collective-permute-start | bytes 786440 | tf_op jit(solution)/shard_map/ppermute | solution.py:362
  19.3 1.5 %shard_map.61 = (f32[16,256]{1,0:T(8,128)S(1)}, f32[16,256]{1,0:T(8,128)S(1)}, f32[1024,256]{1,0:T(8,128)S(1)}) custom-call(bf16[128,1024]{1,0:T(8,128)(2,1)S(1)} %collective-permute-done.4.refs_0_, bf16[1024,3072]{1,0:T(8,128)(2,1)S(1)} %copy-done, f32[1,1024]{1,0:T(1,128)S(1)} %bitcast.5, f32[2,1024]{1,0:T(2,128)S(1)} %copy-done.2, ...), custom_call_target="tpu_custom_call" | custom-call | flops 671088640 | bytes 9383936 | tf_op jit(solution)/shard_map/pallas_call | solution.py:292
  20.8 0.9 %collective-permute-start.7 = (bf16[128,1024]{1,0:T(8,128)(2,1)S(1)}, bf16[128,1024]{1,0:T(8,128)(2,1)S(1)}, u32[]{:S(2)}, u32[]{:S(2)}) collective-permute-start(bf16[128,1024]{1,0:T(8,128)(2,1)S(1)} %collective-permute-done.5.refs_1_), channel_id=1, source_target_pairs={{0,10},{8,1},{1,8},{9,3},{2,12},{10,0},{3,9},{11,5},{4,14},{12,2},... | collective-permute-start | bytes 786440 | tf_op jit(solution)/shard_map/ppermute | solution.py:359
  21.7 3.0 %shard_map.62 = (f32[16,256]{1,0:T(8,128)S(1)}, f32[16,256]{1,0:T(8,128)S(1)}, f32[1024,256]{1,0:T(8,128)S(1)}) custom-call(bf16[128,1024]{1,0:T(8,128)(2,1)S(1)} %collective-permute-done.3.refs_0_, bf16[128,1024]{1,0:T(8,128)(2,1)S(1)} %collective-permute-done.5.refs_1_, bf16[1024,3072]{1,0:T(8,128)(2,1)S(1)} %copy-done, f32[1,1024]{1,0:T(1,128)S(1)} %bitcast.6, ...), custom_call_target="tpu_custom_call" | custom-call | flops 1342177280 | bytes 9646080 | tf_op jit(solution)/shard_map/pallas_call | solution.py:292
  24.8 1.5 %shard_map.63 = (f32[16,256]{1,0:T(8,128)S(1)}, f32[16,256]{1,0:T(8,128)S(1)}, f32[1024,256]{1,0:T(8,128)S(1)}) custom-call(bf16[128,1024]{1,0:T(8,128)(2,1)S(1)} %collective-permute-done.6.refs_0_, bf16[1024,3072]{1,0:T(8,128)(2,1)S(1)} %copy-done, f32[1,1024]{1,0:T(1,128)S(1)} %bitcast.7, f32[2,1024]{1,0:T(2,128)S(1)} %copy-done.2, ...), custom_call_target="tpu_custom_call" | custom-call | flops 671088640 | bytes 9383936 | tf_op jit(solution)/shard_map/pallas_call | solution.py:292
  26.3 0.4 %collective-permute-done.7.block_ref = bf16[128,1024]{1,0:T(8,128)(2,1)S(1)} collective-permute-done((bf16[128,1024]{1,0:T(8,128)(2,1)S(1)}, bf16[128,1024]{1,0:T(8,128)(2,1)S(1)}, u32[]{:S(2)}, u32[]{:S(2)}) %collective-permute-start.7) | collective-permute-done | bytes 262176 | tf_op jit(solution)/shard_map/ppermute | solution.py:359
  26.7 1.6 %shard_map.64 = (bf16[1120,128]{1,0:T(8,128)(2,1)S(1)}, bf16[128,1024]{1,0:T(8,128)(2,1)S(1)}, bf16[1024,128]{1,0:T(8,128)(2,1)S(1)}) custom-call(bf16[128,1024]{1,0:T(8,128)(2,1)S(1)} %collective-permute-done.7.block_ref, bf16[1024,3072]{1,0:T(8,128)(2,1)S(1)} %copy-done, f32[1,1024]{1,0:T(1,128)S(1)} %bitcast.8, f32[2,1024]{1,0:T(2,128)S(1)} %copy-done.2, ...), custom_call_target="tpu_custom_call" | custom-call | flops 671088640 | bytes 9113600 | tf_op jit(solution)/shard_map/pallas_call | solution.py:292
  28.2 0.6 %collective-permute-start.8 = (bf16[1120,128]{1,0:T(8,128)(2,1)S(1)}, bf16[1120,128]{1,0:T(8,128)(2,1)S(1)}, u32[]{:S(2)}, u32[]{:S(2)}) collective-permute-start(bf16[1120,128]{1,0:T(8,128)(2,1)S(1)} %get-tuple-element.110), channel_id=1, source_target_pairs={{0,8},{8,0},{1,9},{9,1},{2,10},{10,2},{3,11},{11,3},{4,12},{12,4},... | collective-permute-start | bytes 860168 | tf_op jit(solution)/shard_map/ppermute | solution.py:374
  28.9 0.7 %shard_map.65 = (f32[1024,128]{1,0:T(8,128)S(1)}, f32[32,128]{1,0:T(8,128)S(1)}) custom-call(bf16[128,1024]{1,0:T(8,128)(2,1)S(1)} %get-tuple-element.106.keys_ref, bf16[1024,128]{1,0:T(8,128)(2,1)S(1)} %get-tuple-element.107.values_ref, bf16[1024,256]{1,0:T(8,128)(2,1)S(1)} %shard_map.57.refs_5_.refs_6_.q_ref, f32[16,256]{1,0:T(8,128)S(1)} %get-tuple-element.103.max_ref, ...), custom_call_target="tpu_custom_call" | custom-call | flops 167772160 | bytes 2670592 | tf_op jit(solution)/shard_map/pallas_call | solution.py:292
  29.5 0.5 %collective-permute-done.8.theirs_ref = bf16[1120,128]{1,0:T(8,128)(2,1)S(1)} collective-permute-done((bf16[1120,128]{1,0:T(8,128)(2,1)S(1)}, bf16[1120,128]{1,0:T(8,128)(2,1)S(1)}, u32[]{:S(2)}, u32[]{:S(2)}) %collective-permute-start.8) | collective-permute-done | bytes 286752 | tf_op jit(solution)/shard_map/ppermute | solution.py:374
  30.1 1.2 %shard_map.66 = bf16[128,1024]{1,0:T(8,128)(2,1)} custom-call(f32[1024,128]{1,0:T(8,128)S(1)} %get-tuple-element.108.mine_ref, f32[32,128]{1,0:T(8,128)S(1)} %get-tuple-element.109.my_state_ref, bf16[1120,128]{1,0:T(8,128)(2,1)S(1)} %collective-permute-done.8.theirs_ref, bf16[1024,1024]{1,0:T(8,128)(2,1)S(1)} %copy-done.1), custom_call_target="tpu_custom_call" | custom-call | flops 268435456 | bytes 3186688 | tf_op jit(solution)/shard_map/pallas_call | solution.py:292
  (16 shorter events, 0.1 us)
Async XLA Ops:
  0.0 3.2 %copy-start.4 = (bf16[128,1024]{1,0:T(8,128)(2,1)S(1)}, bf16[128,1024]{1,0:T(8,128)(2,1)}, u32[]{:S(2)}) copy-start(bf16[128,1024]{1,0:T(8,128)(2,1)} %own_ref.1) | copy-start | bytes 786436
  0.0 3.2 %copy-start.3 = (f32[1024]{0:T(1024)S(1)}, f32[1024]{0:T(1024)}, u32[]{:S(2)}) copy-start(f32[1024]{0:T(1024)} %param.6) | copy-start | bytes 12292
  0.0 3.2 %copy-start = (bf16[1024,3072]{1,0:T(8,128)(2,1)S(1)}, bf16[1024,3072]{1,0:T(8,128)(2,1)}, u32[]{:S(2)}) copy-start(bf16[1024,3072]{1,0:T(8,128)(2,1)} %w_ref.6) | copy-start | bytes 18874372
  0.0 3.2 %collective-permute-start = (bf16[128,1024]{1,0:T(8,128)(2,1)}, bf16[128,1024]{1,0:T(8,128)(2,1)S(1)}, u32[]{:S(2)}, u32[]{:S(2)}) collective-permute-start(bf16[128,1024]{1,0:T(8,128)(2,1)} %own_ref.1), channel_id=1, source_target_pairs={{0,8},{8,0},{1,9},{9,1},{2,10},{10,2},{3,11},{11,3},{4,12},{12,4},... | collective-permute-start | bytes 786440 | tf_op jit(solution)/shard_map/ppermute | solution.py:322
  0.5 6.9 %collective-permute-start.1 = (bf16[128,1024]{1,0:T(8,128)(2,1)}, bf16[128,1024]{1,0:T(8,128)(2,1)S(1)}, u32[]{:S(2)}, u32[]{:S(2)}) collective-permute-start(bf16[128,1024]{1,0:T(8,128)(2,1)} %own_ref.1), channel_id=1, source_target_pairs={{8,2},{0,9},{9,0},{1,11},{10,4},{2,8},{11,1},{3,13},{12,6},{4,10},... | collective-permute-start | bytes 786440 | tf_op jit(solution)/shard_map/ppermute | solution.py:321
  3.2 2.5 %copy-start.2 = (f32[2,1024]{1,0:T(2,128)S(1)}, f32[2,1024]{1,0:T(2,128)}, u32[]{:S(2)}) copy-start(f32[2,1024]{1,0:T(2,128)} %gains_ref.3) | copy-start | bytes 24580
  3.6 7.4 %collective-permute-start.2 = (bf16[128,1024]{1,0:T(8,128)(2,1)S(1)}, bf16[128,1024]{1,0:T(8,128)(2,1)S(1)}, u32[]{:S(2)}, u32[]{:S(2)}) collective-permute-start(bf16[128,1024]{1,0:T(8,128)(2,1)S(1)} %get-tuple-element.61.sibling_ref), channel_id=1, source_target_pairs={{8,2},{0,9},{9,0},{1,11},{10,4},{2,8},{11,1},{3,13},{12,6},{4,10},... | collective-permute-start | bytes 786440 | tf_op jit(solution)/shard_map/ppermute | solution.py:331
  7.4 6.6 %collective-permute-start.3 = (bf16[128,1024]{1,0:T(8,128)(2,1)S(1)}, bf16[128,1024]{1,0:T(8,128)(2,1)S(1)}, u32[]{:S(2)}, u32[]{:S(2)}) collective-permute-start(bf16[128,1024]{1,0:T(8,128)(2,1)S(1)} %collective-permute-done.1.refs_0_), channel_id=1, source_target_pairs={{0,10},{8,1},{1,8},{9,3},{2,12},{10,0},{3,9},{11,5},{4,14},{12,2},... | collective-permute-start | bytes 786440 | tf_op jit(solution)/shard_map/ppermute | solution.py:359
  11.0 6.3 %collective-permute-start.4 = (bf16[128,1024]{1,0:T(8,128)(2,1)S(1)}, bf16[128,1024]{1,0:T(8,128)(2,1)S(1)}, u32[]{:S(2)}, u32[]{:S(2)}) collective-permute-start(bf16[128,1024]{1,0:T(8,128)(2,1)S(1)} %collective-permute-done.2.refs_0_), channel_id=1, source_target_pairs={{0,10},{8,1},{1,8},{9,3},{2,12},{10,0},{3,9},{11,5},{4,14},{12,2},... | collective-permute-start | bytes 786440 | tf_op jit(solution)/shard_map/ppermute | solution.py:362
  14.1 6.7 %collective-permute-start.5 = (bf16[128,1024]{1,0:T(8,128)(2,1)S(1)}, bf16[128,1024]{1,0:T(8,128)(2,1)S(1)}, u32[]{:S(2)}, u32[]{:S(2)}) collective-permute-start(bf16[128,1024]{1,0:T(8,128)(2,1)S(1)} %collective-permute-done.3.refs_0_), channel_id=1, source_target_pairs={{8,2},{0,9},{9,0},{1,11},{10,4},{2,8},{11,1},{3,13},{12,6},{4,10},... | collective-permute-start | bytes 786440 | tf_op jit(solution)/shard_map/ppermute | solution.py:359
  17.3 7.5 %collective-permute-start.6 = (bf16[128,1024]{1,0:T(8,128)(2,1)S(1)}, bf16[128,1024]{1,0:T(8,128)(2,1)S(1)}, u32[]{:S(2)}, u32[]{:S(2)}) collective-permute-start(bf16[128,1024]{1,0:T(8,128)(2,1)S(1)} %collective-permute-done.4.refs_0_), channel_id=1, source_target_pairs={{8,2},{0,9},{9,0},{1,11},{10,4},{2,8},{11,1},{3,13},{12,6},{4,10},... | collective-permute-start | bytes 786440 | tf_op jit(solution)/shard_map/ppermute | solution.py:362
  20.8 5.9 %collective-permute-start.7 = (bf16[128,1024]{1,0:T(8,128)(2,1)S(1)}, bf16[128,1024]{1,0:T(8,128)(2,1)S(1)}, u32[]{:S(2)}, u32[]{:S(2)}) collective-permute-start(bf16[128,1024]{1,0:T(8,128)(2,1)S(1)} %collective-permute-done.5.refs_1_), channel_id=1, source_target_pairs={{0,10},{8,1},{1,8},{9,3},{2,12},{10,0},{3,9},{11,5},{4,14},{12,2},... | collective-permute-start | bytes 786440 | tf_op jit(solution)/shard_map/ppermute | solution.py:359
  26.3 3.7 %copy-start.1 = (bf16[1024,1024]{1,0:T(8,128)(2,1)S(1)}, bf16[1024,1024]{1,0:T(8,128)(2,1)}, u32[]{:S(2)}) copy-start(bf16[1024,1024]{1,0:T(8,128)(2,1)} %w_ref.7) | copy-start | bytes 6291460
  28.2 1.8 %collective-permute-start.8 = (bf16[1120,128]{1,0:T(8,128)(2,1)S(1)}, bf16[1120,128]{1,0:T(8,128)(2,1)S(1)}, u32[]{:S(2)}, u32[]{:S(2)}) collective-permute-start(bf16[1120,128]{1,0:T(8,128)(2,1)S(1)} %get-tuple-element.110), channel_id=1, source_target_pairs={{0,8},{8,0},{1,9},{9,1},{2,10},{10,2},{3,11},{11,3},{4,12},{12,4},... | collective-permute-start | bytes 860168 | tf_op jit(solution)/shard_map/ppermute | solution.py:374

commit v10 on v9

--- a/solution.py
+++ b/solution.py
@@ -64,7 +64,9 @@
         ref[...] = normalised(block_ref[...], gain_ref[...])
 
 
-def query_kernel(own_ref, sibling_ref, w_ref, gains_ref, ones_ref, query_ref):
+def query_kernel(
+    own_ref, sibling_ref, w_ref, gains_ref, ones_ref, query_ref, keys_ref, values_ref
+):
     rows, width = own_ref.shape
     ones = ones_ref[...]
     spans = [slice(at, at + SPAN) for at in range(0, width, SPAN)]
@@ -76,6 +78,13 @@
     for i, span, columns in projected:
         query = head_norm(columns, gains_ref[0:1, span] * SCALE, ones)
         query_ref[span, i * rows : (i + 1) * rows] = query.astype(F32).T.astype(BF16)
+    for span in spans:
+        columns = [
+            jnp.dot(own_ref[...], w_ref[:, at + span.start : at + span.stop], preferred_element_type=F32)
+            for at in (width, 2 * width)
+        ]
+        keys_ref[:, span] = head_norm(columns[0], gains_ref[1:2, span], ones)
+        values_ref[span, :] = columns[1].T.astype(BF16)
 
 
 def pipeline(stages, count):
@@ -85,8 +94,9 @@
                 stage(turn - behind)
 
 
-def absorb(first, raws, *refs):
+def absorb(first, made, raws, *refs):
     blocks, refs = refs[: len(raws)], refs[len(raws) :]
+    refs_made = [ref[...] for ref in blocks] if made else None
     w_ref, gain_ref, gains_ref, ones_ref, q_ref = refs[:5]
     if first:
         outs = refs[5:]
@@ -98,7 +108,9 @@
     blocks = [
         normalised(ref[...], gain_ref[...]) if raw else ref[...] for ref, raw in zip(blocks, raws)
     ]
-    block = jnp.concatenate(blocks, axis=0) if len(blocks) > 1 else blocks[0]
+    block = jnp.concatenate(blocks, axis=0) if len(blocks) > 1 and not made else blocks[0]
+    if made:
+        block, made_values = refs_made
     ones = ones_ref[...]
     zeros = jnp.zeros((HD, queries), BF16)
     counts = jnp.ones((16, block.shape[0]), BF16)
@@ -106,11 +118,17 @@
     maxima, sums = [], []
 
     def project(i):
+        if made:
+            span = slice(i * SPAN, (i + 1) * SPAN)
+            held["key", i], held["value", i] = block[:, span], made_values[span]
+            return
         for name, at in (("key", width), ("value", 2 * width)):
             span = slice(at + i * SPAN, at + (i + 1) * SPAN)
             held[name, i] = jnp.dot(block, w_ref[:, span], preferred_element_type=F32)
 
     def norm(i):
+        if made:
+            return
         span = slice(i * SPAN, (i + 1) * SPAN)
         held["key", i] = head_norm(held["key", i], gains_ref[1:2, span], ones)
         held["value", i] = held["value", i].T.astype(BF16)
@@ -329,9 +347,9 @@
         0,
     )
     two = lax.ppermute(other, axes, hops[0])
-    (query,) = call(
+    query, keys, values = call(
         query_kernel,
-        [shape((width, 2 * rows), BF16)],
+        [shape((width, 2 * rows), BF16), shape((rows, width), BF16), shape((width, rows), BF16)],
         (normed, other, w_qkv, qk_gains, ones),
         2 * 2 * rows * width * width,
     )
@@ -342,10 +360,10 @@
     ]
     flops = 2 * rows * width * 2 * width + 2 * 2 * rows * 2 * rows * width
 
-    def take(blocks, state):
+    def take(blocks, state, made=False):
         arrays, raws = zip(*blocks)
         return call(
-            functools.partial(absorb, not state, raws),
+            functools.partial(absorb, not state, made, raws),
             state_shapes,
             (*arrays, w_qkv, gain, qk_gains, ones, query, *state),
             len(blocks) * flops,
@@ -353,12 +371,14 @@
         )
 
     one, query = tie((one, query))
-    late, state = (normed, False), ()
+    own = [(keys, False), (values, False)]
+    late, state = None, ()
     for turn in range(1, count // 2):
         here_one, here_two = one, two
         one = lax.ppermute(here_one, axes, hops[turn % 2])
         if turn < count // 2 - 1:
-            state, here_two = tie((take([late], state), here_two))
+            block = [late] if late else own
+            state, here_two = tie((take(block, state, made=not late), here_two))
             two = lax.ppermute(here_two, axes, hops[turn % 2])
             state, one = tie((take([(here_two, False)], state), one))
             late = here_one, True

time: 31.4 us -> 31.1 us (level)
  waiting for transfers between devices: 1.51 us -> 0.7 us
    ppermute x3, starting transfers between devices: 4.45 us -> 5.18 us  [per_device(): one = lax.ppermute(here_one, axes, hops[turn % 2])]
    ppermute x1, waiting for transfers between devices: 0.61 us -> 0.01 us  [per_device(): one = lax.ppermute(patches, axes, hops[0])]
    ppermute x3, waiting for transfers between devices: 0.37 us -> 0.01 us  [per_device(): one = lax.ppermute(here_one, axes, hops[turn % 2])]
    ppermute x1, starting transfers between devices: 0.6 us -> 0.28 us  [per_device(): came = lax.ppermute(sent, 'head', swap)]
  transfers between devices with their start and end apart: 9 -> 9, of which waited for: 3 -> 1; matrix products, arithmetic and copies ran while one was open for 0% -> 0% of each run, Pallas kernels for 41% -> 43%
where the time goes in v10:
time: 31.1 us; the launch traced here: 31 us
  Pallas kernels  16 us (51%)
  starting transfers between devices  14.1 us (45%)
  waiting for transfers between devices  0.7 us (2%)
    pallas_call x12, Pallas kernels, call(): pl.pallas_call(body, out_shape=outs, in_specs=[VMEM] * len(operands), out...  16 us
    ppermute x3, starting transfers between devices, per_device(): one = lax.ppermute(here_one, axes, hops[turn % 2])  5.18 us
    ppermute x2, starting transfers between devices, per_device(): two = lax.ppermute(here_two, axes, hops[turn % 2])  3.32 us
    ppermute x1, starting transfers between devices, per_device(): one = lax.ppermute(patches, axes, hops[0])  2.63 us
    ppermute x1, starting transfers between devices, per_device(): two = lax.ppermute(other, axes, hops[0])  2.12 us
    ppermute x1, waiting for transfers between devices, per_device(): came = lax.ppermute(sent, 'head', swap)  0.68 us
  transfers between devices with their start and end apart: 9, of which 1 were waited for; matrix products, arithmetic and copies ran while one was open for 0% of the time, Pallas kernels for 43%

profile of v10, /device:TPU:0, one launch (start us, length us, event | category | flops | bytes accessed | tf_op | source)
XLA Modules:
  0.0 31.0 jit_solution(16313176884600977469)
XLA Ops:
  0.0 0.5 %collective-permute-start = (bf16[128,1024]{1,0:T(8,128)(2,1)}, bf16[128,1024]{1,0:T(8,128)(2,1)S(1)}, u32[]{:S(2)}, u32[]{:S(2)}) collective-permute-start(bf16[128,1024]{1,0:T(8,128)(2,1)} %own_ref.1), channel_id=1, source_target_pairs={{0,8},{8,0},{1,9},{9,1},{2,10},{10,2},{3,11},{11,3},{4,12},{12,4},... | collective-permute-start | bytes 786440 | tf_op jit(solution)/shard_map/ppermute | solution.py:340
  0.5 2.6 %collective-permute-start.1 = (bf16[128,1024]{1,0:T(8,128)(2,1)}, bf16[128,1024]{1,0:T(8,128)(2,1)S(1)}, u32[]{:S(2)}, u32[]{:S(2)}) collective-permute-start(bf16[128,1024]{1,0:T(8,128)(2,1)} %own_ref.1), channel_id=1, source_target_pairs={{8,2},{0,9},{9,0},{1,11},{10,4},{2,8},{11,1},{3,13},{12,6},{4,10},... | collective-permute-start | bytes 786440 | tf_op jit(solution)/shard_map/ppermute | solution.py:339
  3.2 0.0 copy-start.2
  3.2 0.0 collective-permute-done.sibling_ref
  3.2 0.4 %shard_map.56 = (bf16[128,1024]{1,0:T(8,128)(2,1)S(1)}, bf16[128,1024]{1,0:T(8,128)(2,1)S(1)}) custom-call(bf16[128,1024]{1,0:T(8,128)(2,1)S(1)} %copy-done.4, bf16[128,1024]{1,0:T(8,128)(2,1)S(1)} %collective-permute-done.sibling_ref, f32[1,1024]{1,0:T(1,128)S(1)} %bitcast.1, bf16[1024,3072]{1,0:T(8,128)(2,1)S(1)} %copy-done), custom_call_target="tpu_custom_call" | custom-call | bytes 7344128 | tf_op jit(solution)/shard_map/pallas_call | solution.py:310
  3.6 2.1 %collective-permute-start.2 = (bf16[128,1024]{1,0:T(8,128)(2,1)S(1)}, bf16[128,1024]{1,0:T(8,128)(2,1)S(1)}, u32[]{:S(2)}, u32[]{:S(2)}) collective-permute-start(bf16[128,1024]{1,0:T(8,128)(2,1)S(1)} %get-tuple-element.63.sibling_ref), channel_id=1, source_target_pairs={{8,2},{0,9},{9,0},{1,11},{10,4},{2,8},{11,1},{3,13},{12,6},{4,10},... | collective-permute-start | bytes 786440 | tf_op jit(solution)/shard_map/ppermute | solution.py:349
  5.7 2.0 %shard_map.57 = (bf16[1024,256]{1,0:T(8,128)(2,1)S(1)}, bf16[128,1024]{1,0:T(8,128)(2,1)S(1)}, bf16[1024,128]{1,0:T(8,128)(2,1)S(1)}) custom-call(bf16[128,1024]{1,0:T(8,128)(2,1)S(1)} %get-tuple-element.62.own_ref, bf16[128,1024]{1,0:T(8,128)(2,1)S(1)} %get-tuple-element.63.sibling_ref, bf16[1024,3072]{1,0:T(8,128)(2,1)S(1)} %copy-done, ...), custom_call_target="tpu_custom_call" | custom-call | flops 536870912 | bytes 8003584 | tf_op jit(solution)/shard_map/pallas_call | solution.py:310
  7.7 0.0 collective-permute-done.1.refs_0_
  7.7 2.0 %collective-permute-start.3 = (bf16[128,1024]{1,0:T(8,128)(2,1)S(1)}, bf16[128,1024]{1,0:T(8,128)(2,1)S(1)}, u32[]{:S(2)}, u32[]{:S(2)}) collective-permute-start(bf16[128,1024]{1,0:T(8,128)(2,1)S(1)} %collective-permute-done.1.refs_0_), channel_id=1, source_target_pairs={{0,10},{8,1},{1,8},{9,3},{2,12},{10,0},{3,9},{11,5},{4,14},{12,2},... | collective-permute-start | bytes 786440 | tf_op jit(solution)/shard_map/ppermute | solution.py:378
  9.7 0.8 %shard_map.58 = (f32[16,256]{1,0:T(8,128)S(1)}, f32[16,256]{1,0:T(8,128)S(1)}, f32[1024,256]{1,0:T(8,128)S(1)}) custom-call(bf16[128,1024]{1,0:T(8,128)(2,1)S(1)} %get-tuple-element.65.refs_0_, bf16[1024,128]{1,0:T(8,128)(2,1)S(1)} %get-tuple-element.66.refs_1_, bf16[1024,3072]{1,0:T(8,128)(2,1)S(1)} %copy-done, f32[1,1024]{1,0:T(1,128)S(1)} %bitcast.2, ...), custom_call_target="tpu_custom_call" | custom-call | flops 1342177280 | bytes 8564736 | tf_op jit(solution)/shard_map/pallas_call | solution.py:310
  10.5 1.8 %collective-permute-start.4 = (bf16[128,1024]{1,0:T(8,128)(2,1)S(1)}, bf16[128,1024]{1,0:T(8,128)(2,1)S(1)}, u32[]{:S(2)}, u32[]{:S(2)}) collective-permute-start(bf16[128,1024]{1,0:T(8,128)(2,1)S(1)} %collective-permute-done.2.refs_0_), channel_id=1, source_target_pairs={{0,10},{8,1},{1,8},{9,3},{2,12},{10,0},{3,9},{11,5},{4,14},{12,2},... | collective-permute-start | bytes 786440 | tf_op jit(solution)/shard_map/ppermute | solution.py:382
  12.3 1.5 %shard_map.59 = (f32[16,256]{1,0:T(8,128)S(1)}, f32[16,256]{1,0:T(8,128)S(1)}, f32[1024,256]{1,0:T(8,128)S(1)}) custom-call(bf16[128,1024]{1,0:T(8,128)(2,1)S(1)} %collective-permute-done.2.refs_0_, bf16[1024,3072]{1,0:T(8,128)(2,1)S(1)} %copy-done, f32[1,1024]{1,0:T(1,128)S(1)} %bitcast.3, f32[2,1024]{1,0:T(2,128)S(1)} %copy-done.2, ...), custom_call_target="tpu_custom_call" | custom-call | flops 671088640 | bytes 9383936 | tf_op jit(solution)/shard_map/pallas_call | solution.py:310
  13.9 1.7 %collective-permute-start.5 = (bf16[128,1024]{1,0:T(8,128)(2,1)S(1)}, bf16[128,1024]{1,0:T(8,128)(2,1)S(1)}, u32[]{:S(2)}, u32[]{:S(2)}) collective-permute-start(bf16[128,1024]{1,0:T(8,128)(2,1)S(1)} %collective-permute-done.3.refs_0_), channel_id=1, source_target_pairs={{8,2},{0,9},{9,0},{1,11},{10,4},{2,8},{11,1},{3,13},{12,6},{4,10},... | collective-permute-start | bytes 786440 | tf_op jit(solution)/shard_map/ppermute | solution.py:378
  15.6 1.7 %shard_map.60 = (f32[16,256]{1,0:T(8,128)S(1)}, f32[16,256]{1,0:T(8,128)S(1)}, f32[1024,256]{1,0:T(8,128)S(1)}) custom-call(bf16[128,1024]{1,0:T(8,128)(2,1)S(1)} %collective-permute-done.1.refs_0_, bf16[1024,3072]{1,0:T(8,128)(2,1)S(1)} %copy-done, f32[1,1024]{1,0:T(1,128)S(1)} %bitcast.4, f32[2,1024]{1,0:T(2,128)S(1)} %copy-done.2, ...), custom_call_target="tpu_custom_call" | custom-call | flops 671088640 | bytes 9383936 | tf_op jit(solution)/shard_map/pallas_call | solution.py:310
  17.3 1.5 %collective-permute-start.6 = (bf16[128,1024]{1,0:T(8,128)(2,1)S(1)}, bf16[128,1024]{1,0:T(8,128)(2,1)S(1)}, u32[]{:S(2)}, u32[]{:S(2)}) collective-permute-start(bf16[128,1024]{1,0:T(8,128)(2,1)S(1)} %collective-permute-done.4.refs_0_), channel_id=1, source_target_pairs={{8,2},{0,9},{9,0},{1,11},{10,4},{2,8},{11,1},{3,13},{12,6},{4,10},... | collective-permute-start | bytes 786440 | tf_op jit(solution)/shard_map/ppermute | solution.py:382
  18.8 1.5 %shard_map.61 = (f32[16,256]{1,0:T(8,128)S(1)}, f32[16,256]{1,0:T(8,128)S(1)}, f32[1024,256]{1,0:T(8,128)S(1)}) custom-call(bf16[128,1024]{1,0:T(8,128)(2,1)S(1)} %collective-permute-done.4.refs_0_, bf16[1024,3072]{1,0:T(8,128)(2,1)S(1)} %copy-done, f32[1,1024]{1,0:T(1,128)S(1)} %bitcast.5, f32[2,1024]{1,0:T(2,128)S(1)} %copy-done.2, ...), custom_call_target="tpu_custom_call" | custom-call | flops 671088640 | bytes 9383936 | tf_op jit(solution)/shard_map/pallas_call | solution.py:310
  20.4 1.5 %collective-permute-start.7 = (bf16[128,1024]{1,0:T(8,128)(2,1)S(1)}, bf16[128,1024]{1,0:T(8,128)(2,1)S(1)}, u32[]{:S(2)}, u32[]{:S(2)}) collective-permute-start(bf16[128,1024]{1,0:T(8,128)(2,1)S(1)} %collective-permute-done.5.refs_1_), channel_id=1, source_target_pairs={{0,10},{8,1},{1,8},{9,3},{2,12},{10,0},{3,9},{11,5},{4,14},{12,2},... | collective-permute-start | bytes 786440 | tf_op jit(solution)/shard_map/ppermute | solution.py:378
  21.9 3.0 %shard_map.62 = (f32[16,256]{1,0:T(8,128)S(1)}, f32[16,256]{1,0:T(8,128)S(1)}, f32[1024,256]{1,0:T(8,128)S(1)}) custom-call(bf16[128,1024]{1,0:T(8,128)(2,1)S(1)} %collective-permute-done.3.refs_0_, bf16[128,1024]{1,0:T(8,128)(2,1)S(1)} %collective-permute-done.5.refs_1_, bf16[1024,3072]{1,0:T(8,128)(2,1)S(1)} %copy-done, f32[1,1024]{1,0:T(1,128)S(1)} %bitcast.6, ...), custom_call_target="tpu_custom_call" | custom-call | flops 1342177280 | bytes 9646080 | tf_op jit(solution)/shard_map/pallas_call | solution.py:310
  25.0 1.6 %shard_map.63 = (f32[16,256]{1,0:T(8,128)S(1)}, f32[16,256]{1,0:T(8,128)S(1)}, f32[1024,256]{1,0:T(8,128)S(1)}) custom-call(bf16[128,1024]{1,0:T(8,128)(2,1)S(1)} %collective-permute-done.6.refs_0_, bf16[1024,3072]{1,0:T(8,128)(2,1)S(1)} %copy-done, f32[1,1024]{1,0:T(1,128)S(1)} %bitcast.7, f32[2,1024]{1,0:T(2,128)S(1)} %copy-done.2, ...), custom_call_target="tpu_custom_call" | custom-call | flops 671088640 | bytes 9383936 | tf_op jit(solution)/shard_map/pallas_call | solution.py:310
  26.5 1.6 %shard_map.64 = (bf16[1120,128]{1,0:T(8,128)(2,1)S(1)}, bf16[128,1024]{1,0:T(8,128)(2,1)S(1)}, bf16[1024,128]{1,0:T(8,128)(2,1)S(1)}) custom-call(bf16[128,1024]{1,0:T(8,128)(2,1)S(1)} %collective-permute-done.7.block_ref, bf16[1024,3072]{1,0:T(8,128)(2,1)S(1)} %copy-done, f32[1,1024]{1,0:T(1,128)S(1)} %bitcast.8, f32[2,1024]{1,0:T(2,128)S(1)} %copy-done.2, ...), custom_call_target="tpu_custom_call" | custom-call | flops 671088640 | bytes 9113600 | tf_op jit(solution)/shard_map/pallas_call | solution.py:310
  28.1 0.3 collective-permute-start.8
  28.4 0.7 %shard_map.65 = (f32[1024,128]{1,0:T(8,128)S(1)}, f32[32,128]{1,0:T(8,128)S(1)}) custom-call(bf16[128,1024]{1,0:T(8,128)(2,1)S(1)} %get-tuple-element.112.keys_ref, bf16[1024,128]{1,0:T(8,128)(2,1)S(1)} %get-tuple-element.113.values_ref, bf16[1024,256]{1,0:T(8,128)(2,1)S(1)} %get-tuple-element.68.refs_6_.refs_5_.q_ref, ...), custom_call_target="tpu_custom_call" | custom-call | flops 167772160 | bytes 2670592 | tf_op jit(solution)/shard_map/pallas_call | solution.py:310
  29.1 0.7 %collective-permute-done.8.theirs_ref = bf16[1120,128]{1,0:T(8,128)(2,1)S(1)} collective-permute-done((bf16[1120,128]{1,0:T(8,128)(2,1)S(1)}, bf16[1120,128]{1,0:T(8,128)(2,1)S(1)}, u32[]{:S(2)}, u32[]{:S(2)}) %collective-permute-start.8) | collective-permute-done | bytes 286752 | tf_op jit(solution)/shard_map/ppermute | solution.py:394
  29.7 1.2 %shard_map.66 = bf16[128,1024]{1,0:T(8,128)(2,1)} custom-call(f32[1024,128]{1,0:T(8,128)S(1)} %get-tuple-element.114.mine_ref, f32[32,128]{1,0:T(8,128)S(1)} %get-tuple-element.115.my_state_ref, bf16[1120,128]{1,0:T(8,128)(2,1)S(1)} %collective-permute-done.8.theirs_ref, bf16[1024,1024]{1,0:T(8,128)(2,1)S(1)} %copy-done.1), custom_call_target="tpu_custom_call" | custom-call | flops 268435456 | bytes 3186688 | tf_op jit(solution)/shard_map/pallas_call | solution.py:310
  (16 shorter events, 0.1 us)
Async XLA Ops:
  0.0 3.2 %copy-start.4 = (bf16[128,1024]{1,0:T(8,128)(2,1)S(1)}, bf16[128,1024]{1,0:T(8,128)(2,1)}, u32[]{:S(2)}) copy-start(bf16[128,1024]{1,0:T(8,128)(2,1)} %own_ref.1) | copy-start | bytes 786436
  0.0 3.2 %copy-start.3 = (f32[1024]{0:T(1024)S(1)}, f32[1024]{0:T(1024)}, u32[]{:S(2)}) copy-start(f32[1024]{0:T(1024)} %param.6) | copy-start | bytes 12292
  0.0 3.2 %copy-start = (bf16[1024,3072]{1,0:T(8,128)(2,1)S(1)}, bf16[1024,3072]{1,0:T(8,128)(2,1)}, u32[]{:S(2)}) copy-start(bf16[1024,3072]{1,0:T(8,128)(2,1)} %w_ref.6) | copy-start | bytes 18874372
  0.0 3.2 %collective-permute-start = (bf16[128,1024]{1,0:T(8,128)(2,1)}, bf16[128,1024]{1,0:T(8,128)(2,1)S(1)}, u32[]{:S(2)}, u32[]{:S(2)}) collective-permute-start(bf16[128,1024]{1,0:T(8,128)(2,1)} %own_ref.1), channel_id=1, source_target_pairs={{0,8},{8,0},{1,9},{9,1},{2,10},{10,2},{3,11},{11,3},{4,12},{12,4},... | collective-permute-start | bytes 786440 | tf_op jit(solution)/shard_map/ppermute | solution.py:340
  0.5 7.2 %collective-permute-start.1 = (bf16[128,1024]{1,0:T(8,128)(2,1)}, bf16[128,1024]{1,0:T(8,128)(2,1)S(1)}, u32[]{:S(2)}, u32[]{:S(2)}) collective-permute-start(bf16[128,1024]{1,0:T(8,128)(2,1)} %own_ref.1), channel_id=1, source_target_pairs={{8,2},{0,9},{9,0},{1,11},{10,4},{2,8},{11,1},{3,13},{12,6},{4,10},... | collective-permute-start | bytes 786440 | tf_op jit(solution)/shard_map/ppermute | solution.py:339
  3.2 2.5 %copy-start.2 = (f32[2,1024]{1,0:T(2,128)S(1)}, f32[2,1024]{1,0:T(2,128)}, u32[]{:S(2)}) copy-start(f32[2,1024]{1,0:T(2,128)} %gains_ref.3) | copy-start | bytes 24580
  3.6 6.9 %collective-permute-start.2 = (bf16[128,1024]{1,0:T(8,128)(2,1)S(1)}, bf16[128,1024]{1,0:T(8,128)(2,1)S(1)}, u32[]{:S(2)}, u32[]{:S(2)}) collective-permute-start(bf16[128,1024]{1,0:T(8,128)(2,1)S(1)} %get-tuple-element.63.sibling_ref), channel_id=1, source_target_pairs={{8,2},{0,9},{9,0},{1,11},{10,4},{2,8},{11,1},{3,13},{12,6},{4,10},... | collective-permute-start | bytes 786440 | tf_op jit(solution)/shard_map/ppermute | solution.py:349
  7.7 6.2 %collective-permute-start.3 = (bf16[128,1024]{1,0:T(8,128)(2,1)S(1)}, bf16[128,1024]{1,0:T(8,128)(2,1)S(1)}, u32[]{:S(2)}, u32[]{:S(2)}) collective-permute-start(bf16[128,1024]{1,0:T(8,128)(2,1)S(1)} %collective-permute-done.1.refs_0_), channel_id=1, source_target_pairs={{0,10},{8,1},{1,8},{9,3},{2,12},{10,0},{3,9},{11,5},{4,14},{12,2},... | collective-permute-start | bytes 786440 | tf_op jit(solution)/shard_map/ppermute | solution.py:378
  10.5 6.8 %collective-permute-start.4 = (bf16[128,1024]{1,0:T(8,128)(2,1)S(1)}, bf16[128,1024]{1,0:T(8,128)(2,1)S(1)}, u32[]{:S(2)}, u32[]{:S(2)}) collective-permute-start(bf16[128,1024]{1,0:T(8,128)(2,1)S(1)} %collective-permute-done.2.refs_0_), channel_id=1, source_target_pairs={{0,10},{8,1},{1,8},{9,3},{2,12},{10,0},{3,9},{11,5},{4,14},{12,2},... | collective-permute-start | bytes 786440 | tf_op jit(solution)/shard_map/ppermute | solution.py:382
  13.9 6.4 %collective-permute-start.5 = (bf16[128,1024]{1,0:T(8,128)(2,1)S(1)}, bf16[128,1024]{1,0:T(8,128)(2,1)S(1)}, u32[]{:S(2)}, u32[]{:S(2)}) collective-permute-start(bf16[128,1024]{1,0:T(8,128)(2,1)S(1)} %collective-permute-done.3.refs_0_), channel_id=1, source_target_pairs={{8,2},{0,9},{9,0},{1,11},{10,4},{2,8},{11,1},{3,13},{12,6},{4,10},... | collective-permute-start | bytes 786440 | tf_op jit(solution)/shard_map/ppermute | solution.py:378
  17.3 7.7 %collective-permute-start.6 = (bf16[128,1024]{1,0:T(8,128)(2,1)S(1)}, bf16[128,1024]{1,0:T(8,128)(2,1)S(1)}, u32[]{:S(2)}, u32[]{:S(2)}) collective-permute-start(bf16[128,1024]{1,0:T(8,128)(2,1)S(1)} %collective-permute-done.4.refs_0_), channel_id=1, source_target_pairs={{8,2},{0,9},{9,0},{1,11},{10,4},{2,8},{11,1},{3,13},{12,6},{4,10},... | collective-permute-start | bytes 786440 | tf_op jit(solution)/shard_map/ppermute | solution.py:382
  20.4 6.2 %collective-permute-start.7 = (bf16[128,1024]{1,0:T(8,128)(2,1)S(1)}, bf16[128,1024]{1,0:T(8,128)(2,1)S(1)}, u32[]{:S(2)}, u32[]{:S(2)}) collective-permute-start(bf16[128,1024]{1,0:T(8,128)(2,1)S(1)} %collective-permute-done.5.refs_1_), channel_id=1, source_target_pairs={{0,10},{8,1},{1,8},{9,3},{2,12},{10,0},{3,9},{11,5},{4,14},{12,2},... | collective-permute-start | bytes 786440 | tf_op jit(solution)/shard_map/ppermute | solution.py:378
  26.5 3.2 %copy-start.1 = (bf16[1024,1024]{1,0:T(8,128)(2,1)S(1)}, bf16[1024,1024]{1,0:T(8,128)(2,1)}, u32[]{:S(2)}) copy-start(bf16[1024,1024]{1,0:T(8,128)(2,1)} %w_ref.7) | copy-start | bytes 6291460
  28.1 1.6 %collective-permute-start.8 = (bf16[1120,128]{1,0:T(8,128)(2,1)S(1)}, bf16[1120,128]{1,0:T(8,128)(2,1)S(1)}, u32[]{:S(2)}, u32[]{:S(2)}) collective-permute-start(bf16[1120,128]{1,0:T(8,128)(2,1)S(1)} %get-tuple-element.116), channel_id=1, source_target_pairs={{0,8},{8,0},{1,9},{9,1},{2,10},{10,2},{3,11},{11,3},{4,12},{12,4},... | collective-permute-start | bytes 860168 | tf_op jit(solution)/shard_map/ppermute | solution.py:394

commit v11 on v10

--- a/solution.py
+++ b/solution.py
@@ -380,8 +380,8 @@
             block = [late] if late else own
             state, here_two = tie((take(block, state, made=not late), here_two))
             two = lax.ppermute(here_two, axes, hops[turn % 2])
-            state, one = tie((take([(here_two, False)], state), one))
-            late = here_one, True
+            state, one = tie((take([(here_one, True)], state), one))
+            late = here_two, False
     state, here_two = tie((take([late, (here_one, True)], state), here_two))
     state, one = tie((take([(here_two, False)], state), one))
     sent, keys, values = call(

time: 31.1 us -> 31 us (level)
    ppermute x3, starting transfers between devices: 5.18 us -> 4.79 us  [per_device(): one = lax.ppermute(here_one, axes, hops[turn % 2])]
where the time goes in v11:
time: 31 us; the launch traced here: 30.9 us
  Pallas kernels  16.1 us (52%)
  starting transfers between devices  14.1 us (45%)
  waiting for transfers between devices  0.57 us (2%)
    pallas_call x12, Pallas kernels, call(): pl.pallas_call(body, out_shape=outs, in_specs=[VMEM] * len(operands), out...  16.1 us
    ppermute x3, starting transfers between devices, per_device(): one = lax.ppermute(here_one, axes, hops[turn % 2])  4.79 us
    ppermute x2, starting transfers between devices, per_device(): two = lax.ppermute(here_two, axes, hops[turn % 2])  3.53 us
    ppermute x1, starting transfers between devices, per_device(): one = lax.ppermute(patches, axes, hops[0])  2.63 us
    ppermute x1, starting transfers between devices, per_device(): two = lax.ppermute(other, axes, hops[0])  2.12 us
  transfers between devices with their start and end apart: 9, of which 1 were waited for; matrix products, arithmetic and copies ran while one was open for 0% of the time, Pallas kernels for 43%

profile of v11, /device:TPU:0, one launch (start us, length us, event | category | flops | bytes accessed | tf_op | source)
XLA Modules:
  0.0 30.9 jit_solution(13896703947963325419)
XLA Ops:
  0.0 0.5 %collective-permute-start = (bf16[128,1024]{1,0:T(8,128)(2,1)}, bf16[128,1024]{1,0:T(8,128)(2,1)S(1)}, u32[]{:S(2)}, u32[]{:S(2)}) collective-permute-start(bf16[128,1024]{1,0:T(8,128)(2,1)} %own_ref.1), channel_id=1, source_target_pairs={{0,8},{8,0},{1,9},{9,1},{2,10},{10,2},{3,11},{11,3},{4,12},{12,4},... | collective-permute-start | bytes 786440 | tf_op jit(solution)/shard_map/ppermute | solution.py:340
  0.5 2.6 %collective-permute-start.1 = (bf16[128,1024]{1,0:T(8,128)(2,1)}, bf16[128,1024]{1,0:T(8,128)(2,1)S(1)}, u32[]{:S(2)}, u32[]{:S(2)}) collective-permute-start(bf16[128,1024]{1,0:T(8,128)(2,1)} %own_ref.1), channel_id=1, source_target_pairs={{8,2},{0,9},{9,0},{1,11},{10,4},{2,8},{11,1},{3,13},{12,6},{4,10},... | collective-permute-start | bytes 786440 | tf_op jit(solution)/shard_map/ppermute | solution.py:339
  3.2 0.0 copy-start.2
  3.2 0.0 collective-permute-done.sibling_ref
  3.2 0.4 %shard_map.56 = (bf16[128,1024]{1,0:T(8,128)(2,1)S(1)}, bf16[128,1024]{1,0:T(8,128)(2,1)S(1)}) custom-call(bf16[128,1024]{1,0:T(8,128)(2,1)S(1)} %copy-done.4, bf16[128,1024]{1,0:T(8,128)(2,1)S(1)} %collective-permute-done.sibling_ref, f32[1,1024]{1,0:T(1,128)S(1)} %bitcast.1, bf16[1024,3072]{1,0:T(8,128)(2,1)S(1)} %copy-done), custom_call_target="tpu_custom_call" | custom-call | bytes 7344128 | tf_op jit(solution)/shard_map/pallas_call | solution.py:310
  3.6 2.1 %collective-permute-start.2 = (bf16[128,1024]{1,0:T(8,128)(2,1)S(1)}, bf16[128,1024]{1,0:T(8,128)(2,1)S(1)}, u32[]{:S(2)}, u32[]{:S(2)}) collective-permute-start(bf16[128,1024]{1,0:T(8,128)(2,1)S(1)} %get-tuple-element.63.sibling_ref), channel_id=1, source_target_pairs={{8,2},{0,9},{9,0},{1,11},{10,4},{2,8},{11,1},{3,13},{12,6},{4,10},... | collective-permute-start | bytes 786440 | tf_op jit(solution)/shard_map/ppermute | solution.py:349
  5.7 2.0 %shard_map.57 = (bf16[1024,256]{1,0:T(8,128)(2,1)S(1)}, bf16[128,1024]{1,0:T(8,128)(2,1)S(1)}, bf16[1024,128]{1,0:T(8,128)(2,1)S(1)}) custom-call(bf16[128,1024]{1,0:T(8,128)(2,1)S(1)} %get-tuple-element.62.own_ref, bf16[128,1024]{1,0:T(8,128)(2,1)S(1)} %get-tuple-element.63.sibling_ref, bf16[1024,3072]{1,0:T(8,128)(2,1)S(1)} %copy-done, ...), custom_call_target="tpu_custom_call" | custom-call | flops 536870912 | bytes 8003584 | tf_op jit(solution)/shard_map/pallas_call | solution.py:310
  7.7 2.0 %collective-permute-start.3 = (bf16[128,1024]{1,0:T(8,128)(2,1)S(1)}, bf16[128,1024]{1,0:T(8,128)(2,1)S(1)}, u32[]{:S(2)}, u32[]{:S(2)}) collective-permute-start(bf16[128,1024]{1,0:T(8,128)(2,1)S(1)} %collective-permute-done.1.refs_0_), channel_id=1, source_target_pairs={{0,10},{8,1},{1,8},{9,3},{2,12},{10,0},{3,9},{11,5},{4,14},{12,2},... | collective-permute-start | bytes 786440 | tf_op jit(solution)/shard_map/ppermute | solution.py:378
  9.7 0.8 %shard_map.58 = (f32[16,256]{1,0:T(8,128)S(1)}, f32[16,256]{1,0:T(8,128)S(1)}, f32[1024,256]{1,0:T(8,128)S(1)}) custom-call(bf16[128,1024]{1,0:T(8,128)(2,1)S(1)} %get-tuple-element.65.refs_0_, bf16[1024,128]{1,0:T(8,128)(2,1)S(1)} %get-tuple-element.66.refs_1_, bf16[1024,3072]{1,0:T(8,128)(2,1)S(1)} %copy-done, f32[1,1024]{1,0:T(1,128)S(1)} %bitcast.2, ...), custom_call_target="tpu_custom_call" | custom-call | flops 1342177280 | bytes 8564736 | tf_op jit(solution)/shard_map/pallas_call | solution.py:310
  10.5 1.8 %collective-permute-start.4 = (bf16[128,1024]{1,0:T(8,128)(2,1)S(1)}, bf16[128,1024]{1,0:T(8,128)(2,1)S(1)}, u32[]{:S(2)}, u32[]{:S(2)}) collective-permute-start(bf16[128,1024]{1,0:T(8,128)(2,1)S(1)} %collective-permute-done.2.refs_0_), channel_id=1, source_target_pairs={{0,10},{8,1},{1,8},{9,3},{2,12},{10,0},{3,9},{11,5},{4,14},{12,2},... | collective-permute-start | bytes 786440 | tf_op jit(solution)/shard_map/ppermute | solution.py:382
  12.3 1.7 %shard_map.59 = (f32[16,256]{1,0:T(8,128)S(1)}, f32[16,256]{1,0:T(8,128)S(1)}, f32[1024,256]{1,0:T(8,128)S(1)}) custom-call(bf16[128,1024]{1,0:T(8,128)(2,1)S(1)} %collective-permute-done.1.refs_0_, bf16[1024,3072]{1,0:T(8,128)(2,1)S(1)} %copy-done, f32[1,1024]{1,0:T(1,128)S(1)} %bitcast.3, f32[2,1024]{1,0:T(2,128)S(1)} %copy-done.2, ...), custom_call_target="tpu_custom_call" | custom-call | flops 671088640 | bytes 9383936 | tf_op jit(solution)/shard_map/pallas_call | solution.py:310
  14.1 1.5 %collective-permute-start.5 = (bf16[128,1024]{1,0:T(8,128)(2,1)S(1)}, bf16[128,1024]{1,0:T(8,128)(2,1)S(1)}, u32[]{:S(2)}, u32[]{:S(2)}) collective-permute-start(bf16[128,1024]{1,0:T(8,128)(2,1)S(1)} %collective-permute-done.3.refs_0_), channel_id=1, source_target_pairs={{8,2},{0,9},{9,0},{1,11},{10,4},{2,8},{11,1},{3,13},{12,6},{4,10},... | collective-permute-start | bytes 786440 | tf_op jit(solution)/shard_map/ppermute | solution.py:378
  15.6 1.5 %shard_map.60 = (f32[16,256]{1,0:T(8,128)S(1)}, f32[16,256]{1,0:T(8,128)S(1)}, f32[1024,256]{1,0:T(8,128)S(1)}) custom-call(bf16[128,1024]{1,0:T(8,128)(2,1)S(1)} %collective-permute-done.2.refs_0_, bf16[1024,3072]{1,0:T(8,128)(2,1)S(1)} %copy-done, f32[1,1024]{1,0:T(1,128)S(1)} %bitcast.4, f32[2,1024]{1,0:T(2,128)S(1)} %copy-done.2, ...), custom_call_target="tpu_custom_call" | custom-call | flops 671088640 | bytes 9383936 | tf_op jit(solution)/shard_map/pallas_call | solution.py:310
  17.1 1.7 %collective-permute-start.6 = (bf16[128,1024]{1,0:T(8,128)(2,1)S(1)}, bf16[128,1024]{1,0:T(8,128)(2,1)S(1)}, u32[]{:S(2)}, u32[]{:S(2)}) collective-permute-start(bf16[128,1024]{1,0:T(8,128)(2,1)S(1)} %collective-permute-done.4.refs_0_), channel_id=1, source_target_pairs={{8,2},{0,9},{9,0},{1,11},{10,4},{2,8},{11,1},{3,13},{12,6},{4,10},... | collective-permute-start | bytes 786440 | tf_op jit(solution)/shard_map/ppermute | solution.py:382
  18.8 1.7 %shard_map.61 = (f32[16,256]{1,0:T(8,128)S(1)}, f32[16,256]{1,0:T(8,128)S(1)}, f32[1024,256]{1,0:T(8,128)S(1)}) custom-call(bf16[128,1024]{1,0:T(8,128)(2,1)S(1)} %collective-permute-done.3.refs_0_, bf16[1024,3072]{1,0:T(8,128)(2,1)S(1)} %copy-done, f32[1,1024]{1,0:T(1,128)S(1)} %bitcast.5, f32[2,1024]{1,0:T(2,128)S(1)} %copy-done.2, ...), custom_call_target="tpu_custom_call" | custom-call | flops 671088640 | bytes 9383936 | tf_op jit(solution)/shard_map/pallas_call | solution.py:310
  20.6 1.3 %collective-permute-start.7 = (bf16[128,1024]{1,0:T(8,128)(2,1)S(1)}, bf16[128,1024]{1,0:T(8,128)(2,1)S(1)}, u32[]{:S(2)}, u32[]{:S(2)}) collective-permute-start(bf16[128,1024]{1,0:T(8,128)(2,1)S(1)} %collective-permute-done.5.refs_1_), channel_id=1, source_target_pairs={{0,10},{8,1},{1,8},{9,3},{2,12},{10,0},{3,9},{11,5},{4,14},{12,2},... | collective-permute-start | bytes 786440 | tf_op jit(solution)/shard_map/ppermute | solution.py:378
  21.9 2.9 %shard_map.62 = (f32[16,256]{1,0:T(8,128)S(1)}, f32[16,256]{1,0:T(8,128)S(1)}, f32[1024,256]{1,0:T(8,128)S(1)}) custom-call(bf16[128,1024]{1,0:T(8,128)(2,1)S(1)} %collective-permute-done.4.refs_0_, bf16[128,1024]{1,0:T(8,128)(2,1)S(1)} %collective-permute-done.5.refs_1_, bf16[1024,3072]{1,0:T(8,128)(2,1)S(1)} %copy-done, f32[1,1024]{1,0:T(1,128)S(1)} %bitcast.6, ...), custom_call_target="tpu_custom_call" | custom-call | flops 1342177280 | bytes 9646080 | tf_op jit(solution)/shard_map/pallas_call | solution.py:310
  24.8 1.5 %shard_map.63 = (f32[16,256]{1,0:T(8,128)S(1)}, f32[16,256]{1,0:T(8,128)S(1)}, f32[1024,256]{1,0:T(8,128)S(1)}) custom-call(bf16[128,1024]{1,0:T(8,128)(2,1)S(1)} %collective-permute-done.6.refs_0_, bf16[1024,3072]{1,0:T(8,128)(2,1)S(1)} %copy-done, f32[1,1024]{1,0:T(1,128)S(1)} %bitcast.7, f32[2,1024]{1,0:T(2,128)S(1)} %copy-done.2, ...), custom_call_target="tpu_custom_call" | custom-call | flops 671088640 | bytes 9383936 | tf_op jit(solution)/shard_map/pallas_call | solution.py:310
  26.4 0.0 collective-permute-done.7.block_ref
  26.4 1.6 %shard_map.64 = (bf16[1120,128]{1,0:T(8,128)(2,1)S(1)}, bf16[128,1024]{1,0:T(8,128)(2,1)S(1)}, bf16[1024,128]{1,0:T(8,128)(2,1)S(1)}) custom-call(bf16[128,1024]{1,0:T(8,128)(2,1)S(1)} %collective-permute-done.7.block_ref, bf16[1024,3072]{1,0:T(8,128)(2,1)S(1)} %copy-done, f32[1,1024]{1,0:T(1,128)S(1)} %bitcast.8, f32[2,1024]{1,0:T(2,128)S(1)} %copy-done.2, ...), custom_call_target="tpu_custom_call" | custom-call | flops 671088640 | bytes 9113600 | tf_op jit(solution)/shard_map/pallas_call | solution.py:310
  28.0 0.5 %collective-permute-start.8 = (bf16[1120,128]{1,0:T(8,128)(2,1)S(1)}, bf16[1120,128]{1,0:T(8,128)(2,1)S(1)}, u32[]{:S(2)}, u32[]{:S(2)}) collective-permute-start(bf16[1120,128]{1,0:T(8,128)(2,1)S(1)} %get-tuple-element.116), channel_id=1, source_target_pairs={{0,8},{8,0},{1,9},{9,1},{2,10},{10,2},{3,11},{11,3},{4,12},{12,4},... | collective-permute-start | bytes 860168 | tf_op jit(solution)/shard_map/ppermute | solution.py:394
  28.5 0.7 %shard_map.65 = (f32[1024,128]{1,0:T(8,128)S(1)}, f32[32,128]{1,0:T(8,128)S(1)}) custom-call(bf16[128,1024]{1,0:T(8,128)(2,1)S(1)} %get-tuple-element.112.keys_ref, bf16[1024,128]{1,0:T(8,128)(2,1)S(1)} %get-tuple-element.113.values_ref, bf16[1024,256]{1,0:T(8,128)(2,1)S(1)} %get-tuple-element.68.refs_6_.refs_5_.q_ref, ...), custom_call_target="tpu_custom_call" | custom-call | flops 167772160 | bytes 2670592 | tf_op jit(solution)/shard_map/pallas_call | solution.py:310
  29.1 0.5 %collective-permute-done.8.theirs_ref = bf16[1120,128]{1,0:T(8,128)(2,1)S(1)} collective-permute-done((bf16[1120,128]{1,0:T(8,128)(2,1)S(1)}, bf16[1120,128]{1,0:T(8,128)(2,1)S(1)}, u32[]{:S(2)}, u32[]{:S(2)}) %collective-permute-start.8) | collective-permute-done | bytes 286752 | tf_op jit(solution)/shard_map/ppermute | solution.py:394
  29.7 1.2 %shard_map.66 = bf16[128,1024]{1,0:T(8,128)(2,1)} custom-call(f32[1024,128]{1,0:T(8,128)S(1)} %get-tuple-element.114.mine_ref, f32[32,128]{1,0:T(8,128)S(1)} %get-tuple-element.115.my_state_ref, bf16[1120,128]{1,0:T(8,128)(2,1)S(1)} %collective-permute-done.8.theirs_ref, bf16[1024,1024]{1,0:T(8,128)(2,1)S(1)} %copy-done.1), custom_call_target="tpu_custom_call" | custom-call | flops 268435456 | bytes 3186688 | tf_op jit(solution)/shard_map/pallas_call | solution.py:310
  (16 shorter events, 0.1 us)
Async XLA Ops:
  0.0 3.2 %copy-start.4 = (bf16[128,1024]{1,0:T(8,128)(2,1)S(1)}, bf16[128,1024]{1,0:T(8,128)(2,1)}, u32[]{:S(2)}) copy-start(bf16[128,1024]{1,0:T(8,128)(2,1)} %own_ref.1) | copy-start | bytes 786436
  0.0 3.2 %copy-start.3 = (f32[1024]{0:T(1024)S(1)}, f32[1024]{0:T(1024)}, u32[]{:S(2)}) copy-start(f32[1024]{0:T(1024)} %param.6) | copy-start | bytes 12292
  0.0 3.2 %copy-start = (bf16[1024,3072]{1,0:T(8,128)(2,1)S(1)}, bf16[1024,3072]{1,0:T(8,128)(2,1)}, u32[]{:S(2)}) copy-start(bf16[1024,3072]{1,0:T(8,128)(2,1)} %w_ref.6) | copy-start | bytes 18874372
  0.0 3.2 %collective-permute-start = (bf16[128,1024]{1,0:T(8,128)(2,1)}, bf16[128,1024]{1,0:T(8,128)(2,1)S(1)}, u32[]{:S(2)}, u32[]{:S(2)}) collective-permute-start(bf16[128,1024]{1,0:T(8,128)(2,1)} %own_ref.1), channel_id=1, source_target_pairs={{0,8},{8,0},{1,9},{9,1},{2,10},{10,2},{3,11},{11,3},{4,12},{12,4},... | collective-permute-start | bytes 786440 | tf_op jit(solution)/shard_map/ppermute | solution.py:340
  0.5 7.2 %collective-permute-start.1 = (bf16[128,1024]{1,0:T(8,128)(2,1)}, bf16[128,1024]{1,0:T(8,128)(2,1)S(1)}, u32[]{:S(2)}, u32[]{:S(2)}) collective-permute-start(bf16[128,1024]{1,0:T(8,128)(2,1)} %own_ref.1), channel_id=1, source_target_pairs={{8,2},{0,9},{9,0},{1,11},{10,4},{2,8},{11,1},{3,13},{12,6},{4,10},... | collective-permute-start | bytes 786440 | tf_op jit(solution)/shard_map/ppermute | solution.py:339
  3.2 2.5 %copy-start.2 = (f32[2,1024]{1,0:T(2,128)S(1)}, f32[2,1024]{1,0:T(2,128)}, u32[]{:S(2)}) copy-start(f32[2,1024]{1,0:T(2,128)} %gains_ref.3) | copy-start | bytes 24580
  3.6 6.9 %collective-permute-start.2 = (bf16[128,1024]{1,0:T(8,128)(2,1)S(1)}, bf16[128,1024]{1,0:T(8,128)(2,1)S(1)}, u32[]{:S(2)}, u32[]{:S(2)}) collective-permute-start(bf16[128,1024]{1,0:T(8,128)(2,1)S(1)} %get-tuple-element.63.sibling_ref), channel_id=1, source_target_pairs={{8,2},{0,9},{9,0},{1,11},{10,4},{2,8},{11,1},{3,13},{12,6},{4,10},... | collective-permute-start | bytes 786440 | tf_op jit(solution)/shard_map/ppermute | solution.py:349
  7.7 6.3 %collective-permute-start.3 = (bf16[128,1024]{1,0:T(8,128)(2,1)S(1)}, bf16[128,1024]{1,0:T(8,128)(2,1)S(1)}, u32[]{:S(2)}, u32[]{:S(2)}) collective-permute-start(bf16[128,1024]{1,0:T(8,128)(2,1)S(1)} %collective-permute-done.1.refs_0_), channel_id=1, source_target_pairs={{0,10},{8,1},{1,8},{9,3},{2,12},{10,0},{3,9},{11,5},{4,14},{12,2},... | collective-permute-start | bytes 786440 | tf_op jit(solution)/shard_map/ppermute | solution.py:378
  10.5 6.6 %collective-permute-start.4 = (bf16[128,1024]{1,0:T(8,128)(2,1)S(1)}, bf16[128,1024]{1,0:T(8,128)(2,1)S(1)}, u32[]{:S(2)}, u32[]{:S(2)}) collective-permute-start(bf16[128,1024]{1,0:T(8,128)(2,1)S(1)} %collective-permute-done.2.refs_0_), channel_id=1, source_target_pairs={{0,10},{8,1},{1,8},{9,3},{2,12},{10,0},{3,9},{11,5},{4,14},{12,2},... | collective-permute-start | bytes 786440 | tf_op jit(solution)/shard_map/ppermute | solution.py:382
  14.1 6.5 %collective-permute-start.5 = (bf16[128,1024]{1,0:T(8,128)(2,1)S(1)}, bf16[128,1024]{1,0:T(8,128)(2,1)S(1)}, u32[]{:S(2)}, u32[]{:S(2)}) collective-permute-start(bf16[128,1024]{1,0:T(8,128)(2,1)S(1)} %collective-permute-done.3.refs_0_), channel_id=1, source_target_pairs={{8,2},{0,9},{9,0},{1,11},{10,4},{2,8},{11,1},{3,13},{12,6},{4,10},... | collective-permute-start | bytes 786440 | tf_op jit(solution)/shard_map/ppermute | solution.py:378
  17.1 7.7 %collective-permute-start.6 = (bf16[128,1024]{1,0:T(8,128)(2,1)S(1)}, bf16[128,1024]{1,0:T(8,128)(2,1)S(1)}, u32[]{:S(2)}, u32[]{:S(2)}) collective-permute-start(bf16[128,1024]{1,0:T(8,128)(2,1)S(1)} %collective-permute-done.4.refs_0_), channel_id=1, source_target_pairs={{8,2},{0,9},{9,0},{1,11},{10,4},{2,8},{11,1},{3,13},{12,6},{4,10},... | collective-permute-start | bytes 786440 | tf_op jit(solution)/shard_map/ppermute | solution.py:382
  20.6 5.9 %collective-permute-start.7 = (bf16[128,1024]{1,0:T(8,128)(2,1)S(1)}, bf16[128,1024]{1,0:T(8,128)(2,1)S(1)}, u32[]{:S(2)}, u32[]{:S(2)}) collective-permute-start(bf16[128,1024]{1,0:T(8,128)(2,1)S(1)} %collective-permute-done.5.refs_1_), channel_id=1, source_target_pairs={{0,10},{8,1},{1,8},{9,3},{2,12},{10,0},{3,9},{11,5},{4,14},{12,2},... | collective-permute-start | bytes 786440 | tf_op jit(solution)/shard_map/ppermute | solution.py:378
  26.4 3.3 %copy-start.1 = (bf16[1024,1024]{1,0:T(8,128)(2,1)S(1)}, bf16[1024,1024]{1,0:T(8,128)(2,1)}, u32[]{:S(2)}) copy-start(bf16[1024,1024]{1,0:T(8,128)(2,1)} %w_ref.7) | copy-start | bytes 6291460
  28.0 1.7 %collective-permute-start.8 = (bf16[1120,128]{1,0:T(8,128)(2,1)S(1)}, bf16[1120,128]{1,0:T(8,128)(2,1)S(1)}, u32[]{:S(2)}, u32[]{:S(2)}) collective-permute-start(bf16[1120,128]{1,0:T(8,128)(2,1)S(1)} %get-tuple-element.116), channel_id=1, source_target_pairs={{0,8},{8,0},{1,9},{9,1},{2,10},{10,2},{3,11},{11,3},{4,12},{12,4},... | collective-permute-start | bytes 860168 | tf_op jit(solution)/shard_map/ppermute | solution.py:394
